TPU v7x, 32 devices: a whole 2x2x4 slice. The times are simulated.
32 devices in a mesh: grp: 16 (over z, x, core), rep: 2 (over y).
Axes of the slice: x: 2, y: 2, z: 4, core: 2. Of those that a mesh axis runs over, the one named last changes fastest.
Arguments:
- adjoint: bfloat16 [256, 512], P('grp'), may hold values from -6 to 6
- active: int32 [256, 512], P('grp'), may hold values 0 or 1
- counts: int32 [256, 16384], P('rep', 'grp'), may hold values from 0 to 3, as said below
- src_degree: int32 [256], P('rep'), may hold values from 8 to 256
- dst_degree: int32 [16384], P('grp'), may hold values from 8 to 256
- inputs: bfloat16 [16384, 512], P(('grp', 'rep')), may hold values from -6 to 6
- weight: bfloat16 [512, 512], replicated, may hold values from -0.25 to 0.25
Outputs:
- grad_input: bfloat16 [16384, 512], P(('grp', 'rep'))
- grad_weight: float32 [512, 512], P('rep')
Inputs may be any that keep to these rules, and one draw needn't show every extreme that they name: Edge counts; within an aligned tile of 16 source rows by 1024 destination columns the share of nonzero entries ranges from none to all, differing from tile to tile.
All inputs are finite; a program needn't handle non-finite values. No bound on the sum of `active` on one device may be relied on, other than what follows from the above.
Results may differ from a plain program's by a relative error of at most 0.0057.
Values may be sent and summed in bfloat16 or wider, within the bound.
No kernel may reach another device: no remote copies, remote signals or barrier semaphores. Data moves between devices by JAX's collectives and lax.ppermute only.
A program may use at most 64 MiB of HBM per device.

v0:
```python
import jax
import jax.numpy as jnp
from jax import lax
from jax.sharding import PartitionSpec as P


def spread(shard, axis, root):
    mine = lax.axis_index(axis) == root
    return lax.psum(jnp.where(mine, shard, jnp.zeros_like(shard)), axis)


def weight_term(row_inputs, values):
    high_part = values.astype(jnp.bfloat16)
    low_part = (values - high_part.astype(jnp.float32)).astype(jnp.bfloat16)
    upper = lax.dot_general(
        row_inputs, high_part, (((0,), (0,)), ((), ())), preferred_element_type=jnp.float32
    )
    lower = lax.dot_general(
        row_inputs, low_part, (((0,), (0,)), ((), ())), preferred_element_type=jnp.float32
    )
    return upper + lower


def body(adjoint, active, counts, src_degree, dst_degree, inputs, weight):
    masked = (adjoint.astype(jnp.float32) * active.astype(jnp.float32)).astype(jnp.bfloat16)
    src_scale = lax.rsqrt(src_degree.astype(jnp.float32))
    dst_scale = lax.rsqrt(dst_degree.astype(jnp.float32))
    src_rows = adjoint.shape[0]
    blocks = counts.shape[0] // src_rows
    replica = lax.axis_index("rep")

    def scaled_product(count_tile, row_scale, owner_rows, running):
        scaled_tile = (
            count_tile.astype(jnp.float32) * row_scale[:, None] * dst_scale[None, :]
        ).astype(jnp.bfloat16)
        return running + lax.dot_general(
            scaled_tile, owner_rows, (((0,), (0,)), ((), ())), preferred_element_type=jnp.float32
        )

    def apply_tile(block_index, running):
        owner_index = replica * blocks + block_index
        owner_rows = spread(masked, "grp", owner_index)
        start = block_index * src_rows
        count_tile = lax.dynamic_slice_in_dim(counts, start, src_rows, 0)
        row_scale = lax.dynamic_slice_in_dim(src_scale, start, src_rows, 0)
        return scaled_product(count_tile, row_scale, owner_rows, running)

    partial_value = lax.fori_loop(
        0, blocks, apply_tile, jnp.zeros((counts.shape[1], masked.shape[1]), jnp.float32)
    )
    grad_pre = lax.psum_scatter(partial_value, "rep", scatter_dimension=0, tiled=True)
    grad_input = lax.dot_general(
        grad_pre.astype(jnp.bfloat16),
        weight,
        (((1,), (1,)), ((), ())),
        preferred_element_type=jnp.float32,
    ).astype(jnp.bfloat16)
    vertex_total = inputs.shape[0] * lax.axis_size("grp") * lax.axis_size("rep")
    local_term = weight_term(inputs, grad_pre)
    whole_term = lax.psum(local_term, "grp")
    grad_weight = lax.psum_scatter(whole_term, "rep", scatter_dimension=0, tiled=True)
    return (grad_input, grad_weight / vertex_total)


def solution(mesh):
    in_specs = (
        P("grp", None),
        P("grp", None),
        P("rep", "grp"),
        P("rep"),
        P("grp"),
        P(("grp", "rep"), None),
        P(),
    )
    out_specs = (P(("grp", "rep"), None), P("rep", None))
    return jax.shard_map(body, mesh=mesh, in_specs=in_specs, out_specs=out_specs, check_vma=False)
```

profile of v0, /device:TPU:0, one launch (start us, length us, event | category | flops | bytes accessed | tf_op | source)
XLA Modules:
  0.0 645.6 jit_solution(16749570656859401305)
XLA Ops:
  7.2 0.0 copy-start
  7.2 0.0 reduce-scatter.3.cloned.1.call-start
  7.2 0.7 convert_rsqrt_fusion.1
  7.9 0.7 convert_rsqrt_fusion
  8.6 0.8 multiply_convert_fusion.2
  9.4 479.7 %while.16 = (s32[]{:T(128)}, f32[1024,512]{1,0:T(8,128)S(1)}, s32[128,1024]{1,0:T(8,128)}, f32[128]{0:T(128)S(1)}, f32[1024]{0:T(1024)S(1)}, /*index=5*/s32[]{:T...) while((s32[]{:T(128)}, f32[1024,512]{1,0:T(8,128)S(1)}, ...), condition=%wide.region_2.3_spmd.clone, body=%wide.region_0.2_spmd.clone.sunk | while | flops 17907724 | bytes 4346299 | solution.py:48
  9.4 0.1 dynamic_slice.25
  9.5 62.9 %psum.24 = bf16[16,512]{1,0:T(8,128)(2,1)S(1)} all-reduce(bf16[16,512]{1,0:T(8,128)(2,1)S(1)} %broadcast_select_fusion.2), channel_id=1, replica_groups=mesh['grp'=16,'rep'=2] {'grp'}, use_global_device_ids=true, to_apply=%region_1.1 | all-reduce | flops 8192 | bytes 32768 | tf_op jit(solution)/shard_map/while/body/eval_jaxpr/psum | solution.py:9
  72.5 1.5 select_add_fusion.2
  74.0 0.1 dynamic_slice.25
  74.1 57.6 %psum.24 = bf16[16,512]{1,0:T(8,128)(2,1)S(1)} all-reduce(bf16[16,512]{1,0:T(8,128)(2,1)S(1)} %broadcast_select_fusion.2), channel_id=1, replica_groups=mesh['grp'=16,'rep'=2] {'grp'}, use_global_device_ids=true, to_apply=%region_1.1 | all-reduce | flops 8192 | bytes 32768 | tf_op jit(solution)/shard_map/while/body/eval_jaxpr/psum | solution.py:9
  131.8 1.5 select_add_fusion.2
  133.3 0.1 dynamic_slice.25
  133.4 57.6 %psum.24 = bf16[16,512]{1,0:T(8,128)(2,1)S(1)} all-reduce(bf16[16,512]{1,0:T(8,128)(2,1)S(1)} %broadcast_select_fusion.2), channel_id=1, replica_groups=mesh['grp'=16,'rep'=2] {'grp'}, use_global_device_ids=true, to_apply=%region_1.1 | all-reduce | flops 8192 | bytes 32768 | tf_op jit(solution)/shard_map/while/body/eval_jaxpr/psum | solution.py:9
  191.1 1.5 select_add_fusion.2
  192.7 0.1 dynamic_slice.25
  192.7 57.6 %psum.24 = bf16[16,512]{1,0:T(8,128)(2,1)S(1)} all-reduce(bf16[16,512]{1,0:T(8,128)(2,1)S(1)} %broadcast_select_fusion.2), channel_id=1, replica_groups=mesh['grp'=16,'rep'=2] {'grp'}, use_global_device_ids=true, to_apply=%region_1.1 | all-reduce | flops 8192 | bytes 32768 | tf_op jit(solution)/shard_map/while/body/eval_jaxpr/psum | solution.py:9
  250.4 1.5 select_add_fusion.2
  252.0 0.1 dynamic_slice.25
  252.0 57.6 %psum.24 = bf16[16,512]{1,0:T(8,128)(2,1)S(1)} all-reduce(bf16[16,512]{1,0:T(8,128)(2,1)S(1)} %broadcast_select_fusion.2), channel_id=1, replica_groups=mesh['grp'=16,'rep'=2] {'grp'}, use_global_device_ids=true, to_apply=%region_1.1 | all-reduce | flops 8192 | bytes 32768 | tf_op jit(solution)/shard_map/while/body/eval_jaxpr/psum | solution.py:9
  309.7 1.5 select_add_fusion.2
  311.3 0.1 dynamic_slice.25
  311.3 57.6 %psum.24 = bf16[16,512]{1,0:T(8,128)(2,1)S(1)} all-reduce(bf16[16,512]{1,0:T(8,128)(2,1)S(1)} %broadcast_select_fusion.2), channel_id=1, replica_groups=mesh['grp'=16,'rep'=2] {'grp'}, use_global_device_ids=true, to_apply=%region_1.1 | all-reduce | flops 8192 | bytes 32768 | tf_op jit(solution)/shard_map/while/body/eval_jaxpr/psum | solution.py:9
  369.0 1.5 select_add_fusion.2
  370.6 0.1 dynamic_slice.25
  370.6 57.6 %psum.24 = bf16[16,512]{1,0:T(8,128)(2,1)S(1)} all-reduce(bf16[16,512]{1,0:T(8,128)(2,1)S(1)} %broadcast_select_fusion.2), channel_id=1, replica_groups=mesh['grp'=16,'rep'=2] {'grp'}, use_global_device_ids=true, to_apply=%region_1.1 | all-reduce | flops 8192 | bytes 32768 | tf_op jit(solution)/shard_map/while/body/eval_jaxpr/psum | solution.py:9
  428.3 1.5 select_add_fusion.2
  429.9 0.1 dynamic_slice.25
  429.9 57.6 %psum.24 = bf16[16,512]{1,0:T(8,128)(2,1)S(1)} all-reduce(bf16[16,512]{1,0:T(8,128)(2,1)S(1)} %broadcast_select_fusion.2), channel_id=1, replica_groups=mesh['grp'=16,'rep'=2] {'grp'}, use_global_device_ids=true, to_apply=%region_1.1 | all-reduce | flops 8192 | bytes 32768 | tf_op jit(solution)/shard_map/while/body/eval_jaxpr/psum | solution.py:9
  487.6 1.5 select_add_fusion.2
  489.1 0.0 copy-start.1
  489.1 1.3 copy-done.1
  490.5 0.0 reduce-scatter.3.cloned.1.call-update
  490.5 0.0 reduce-scatter.5.cloned.1.call-start
  490.5 29.2 %reduce-scatter.3.cloned.1.call-done = f32[512,512]{1,0:T(8,128)} async-done(((f32[1024,512]{1,0:T(8,128)}), f32[512,512]{1,0:T(8,128)}) %reduce-scatter.3.cloned.1.call-update) | async-done | bytes 1048592 | tf_op jit(solution)/shard_map/reduce_scatter | solution.py:51
  519.8 0.0 copy-done
  519.8 0.0 copy-start.2
  519.8 1.8 fusion.5
  521.5 0.0 copy-done.2
  521.6 0.0 copy-start.3
  521.6 1.4 fusion.3
  523.0 0.0 reduce-scatter.5.cloned.1.call-update
  523.0 0.0 all-reduce.2.cloned.1.call-start
  523.1 20.4 %reduce-scatter.5.cloned.1.call-done = f32[256,512]{0,1:T(8,128)} async-done(((f32[512,512]{0,1:T(8,128)}), f32[256,512]{0,1:T(8,128)}) %reduce-scatter.5.cloned.1.call-update) | async-done | bytes 524304 | tf_op jit(solution)/shard_map/reduce_scatter | solution.py:61
  543.5 0.0 all-reduce.2.cloned.1.call-update
  543.5 0.0 copy-done.3
  543.5 1.3 convolution_convert_fusion
  544.8 92.2 %all-reduce.2.cloned.1.call-done = f32[256,512]{0,1:T(8,128)} async-done(((f32[256,512]{0,1:T(8,128)}), f32[256,512]{0,1:T(8,128)}) %all-reduce.2.cloned.1.call-update) | async-done | bytes 524304 | tf_op jit(solution)/shard_map/psum | solution.py:60
  637.0 1.1 broadcast_multiply_fusion
  638.1 1.0 copy.9
  (9 shorter events, 0.1 us)
Async XLA Ops:
  7.2 512.6 %copy-start = (bf16[512,512]{1,0:T(8,128)(2,1)S(1)}, bf16[512,512]{1,0:T(8,128)(2,1)}, u32[]{:S(2)}) copy-start(bf16[512,512]{1,0:T(8,128)(2,1)} %param.14) | copy-start | bytes 1572868
  7.2 512.6 %reduce-scatter.3.cloned.1.call-start = ((), (), s32[]{:S(2)}) async-start(), calls=%async_computation.2 | async-start | bytes 3145728 | tf_op jit(solution)/shard_map/reduce_scatter | solution.py:51
  489.1 1.3 copy-start.1
  490.5 53.0 %reduce-scatter.5.cloned.1.call-start = ((), (), s32[]{:S(2)}) async-start(), calls=%async_computation.3 | async-start | bytes 1572864 | tf_op jit(solution)/shard_map/reduce_scatter | solution.py:61
  519.8 1.8 copy-start.2
  521.6 22.0 %copy-start.3 = (bf16[512,512]{1,0:T(8,128)(2,1)S(1)}, bf16[512,512]{1,0:T(8,128)(2,1)}, u32[]{:S(2)}) copy-start(bf16[512,512]{1,0:T(8,128)(2,1)} %param.15) | copy-start | bytes 1572868
  523.0 114.0 %all-reduce.2.cloned.1.call-start = ((), (), s32[]{:S(2)}) async-start(), calls=%async_computation.4 | async-start | bytes 1048576 | tf_op jit(solution)/shard_map/psum | solution.py:60
Sparse Core Ops, SparseCore 0:
  490.6 29.0 reduce-scatter.2
  523.2 20.3 reduce-scatter.4
  546.9 90.0 all-reduce.1
where the time goes:
time: 646 us
  blocking collectives  466 us (72%)
  waiting for transfers between devices  142 us (22%)
  matrix products  16.9 us (3%)
  between operations  13.8 us (2%)
    psum x8, blocking collectives, spread(): return lax.psum(jnp.where(mine, shard, jnp.zeros_like(shard)), axis)  466 us
    psum x1, waiting for transfers between devices, body(): whole_term = lax.psum(local_term, 'grp')  92.2 us
    reduce_scatter x1, waiting for transfers between devices, body(): lax.psum_scatter(partial_value, 'rep', scatter_dimension=0, tiled=True)  29.2 us
    reduce_scatter x1, waiting for transfers between devices, body(): lax.psum_scatter(whole_term, 'rep', scatter_dimension=0, tiled=True)  20.4 us
  transfers between devices with their start and end apart: 3, of which 3 were waited for; matrix products, arithmetic and copies ran while one was open for 0% of the time, Pallas kernels for 0%

commit v1 on v0

v1 whole, which is shorter than its diff:
```python
import jax
import jax.numpy as jnp
from jax import lax
from jax.sharding import PartitionSpec as P


def swap(block, axis, step):
    size = lax.axis_size(axis)
    return lax.ppermute(block, axis, [(at, at ^ step) for at in range(size)])


def bit_of(index, step):
    return (index & step) != 0


def in_order(upper, mine, theirs, axis):
    return jnp.where(
        upper,
        jnp.concatenate([theirs, mine], axis),
        jnp.concatenate([mine, theirs], axis),
    )


def half_of(block, axis, upper):
    size = block.shape[axis] // 2
    low = lax.slice_in_dim(block, 0, size, axis=axis)
    high = lax.slice_in_dim(block, size, 2 * size, axis=axis)
    return jnp.where(upper, high, low)


def matmul(left, right, contract):
    return lax.dot_general(
        left, right, (contract, ((), ())), preferred_element_type=jnp.float32
    )


def body(adjoint, active, counts, src_degree, dst_degree, inputs, weight):
    groups, replicas = lax.axis_size("grp"), lax.axis_size("rep")
    group, replica = lax.axis_index("grp"), lax.axis_index("rep")
    width = inputs.shape[1]
    rows = inputs.shape[0]
    block_rows = adjoint.shape[0]

    src_scale = lax.rsqrt(src_degree.astype(jnp.float32))
    dst_scale = lax.rsqrt(dst_degree.astype(jnp.float32))

    def scaled_part(owner):
        part = lax.dynamic_slice_in_dim(counts, owner * rows, rows, 1)
        col = lax.dynamic_slice_in_dim(dst_scale, owner * rows, rows, 0)
        return (part.astype(jnp.float32) * src_scale[:, None] * col[None, :]).astype(jnp.bfloat16)

    parts = [scaled_part(replica)]
    for step in range(1, replicas):
        parts.append(swap(scaled_part(replica ^ step), "rep", step))
    masked = (adjoint.astype(jnp.float32) * active.astype(jnp.float32)).astype(jnp.bfloat16)

    terms = [matmul(part, inputs, ((1,), (0,))) for part in parts]

    def ordered(pieces):
        step = 1
        while len(pieces) > 1:
            upper = bit_of(replica, step)
            pieces = [in_order(upper, a, b, 0) for a, b in zip(pieces[0::2], pieces[1::2])]
            step *= 2
        return pieces[0]

    scaled = ordered(parts)
    total = ordered(terms)

    odd = bit_of(group, 1)
    pairs = total.reshape(groups // 2, 2, block_rows, width)
    even_half = pairs[:, 0].reshape(-1, width)
    odd_half = pairs[:, 1].reshape(-1, width)
    theirs = swap(jnp.where(odd, even_half, odd_half).astype(jnp.bfloat16), "grp", 1)
    total = jnp.where(odd, odd_half, even_half) + theirs.astype(jnp.float32)

    step = replicas // 2
    while step:
        upper = bit_of(replica, step)
        theirs = swap(half_of(total, 1, ~upper).astype(jnp.bfloat16), "rep", step)
        total = half_of(total, 1, upper) + theirs.astype(jnp.float32)
        step //= 2

    step = groups // 2
    gathered = masked
    kept = total.shape
    while step > 1:
        sent = total.astype(jnp.bfloat16)
        flat = sent.reshape(-1, width) if kept[1] == width else jnp.concatenate(
            jnp.split(sent, width // kept[1], axis=0), axis=1
        )
        answer = swap(jnp.concatenate([flat, gathered], axis=0), "grp", step)
        back = answer[: flat.shape[0]]
        back = jnp.concatenate(jnp.split(back, width // kept[1], axis=1), axis=0)
        total = sent.astype(jnp.float32) + back.astype(jnp.float32)
        gathered = (gathered, answer[flat.shape[0]:])
        upper = bit_of(group, step)
        mine = gathered[0].reshape(-1, 1, block_rows, width)
        other = gathered[1].reshape(-1, 1, block_rows, width)
        gathered = in_order(upper, mine, other, 1).reshape(-1, width)
        step //= 2

    both = jnp.concatenate([total.astype(jnp.bfloat16), gathered], axis=1)
    other = swap(both, "grp", 1)
    cols = both.shape[1]
    both = in_order(
        odd, both.reshape(-1, 1, block_rows, cols), other.reshape(-1, 1, block_rows, cols), 1
    ).reshape(-1, cols)
    total, gathered = both[:, : kept[1]], both[:, kept[1]:]

    grad_pre = matmul(scaled, gathered, ((0,), (0,)))
    grad_input = matmul(grad_pre.astype(jnp.bfloat16), weight, ((1,), (1,))).astype(jnp.bfloat16)
    vertex_total = rows * groups * replicas
    grad_weight = matmul(total, gathered, ((0,), (0,))) / vertex_total
    return (grad_input, grad_weight)


def solution(mesh):
    in_specs = (
        P("grp", None),
        P("grp", None),
        P("rep", "grp"),
        P("rep"),
        P("grp"),
        P(("grp", "rep"), None),
        P(),
    )
    out_specs = (P(("grp", "rep"), None), P("rep", None))
    return jax.shard_map(body, mesh=mesh, in_specs=in_specs, out_specs=out_specs, check_vma=False)
```

time: 646 us -> 35.9 us (0.06)
  blocking collectives: 466 us -> 0 us
  waiting for transfers between devices: 142 us -> 17.5 us
  matrix products: 16.9 us -> 2.89 us
  between operations: 13.8 us -> 0.88 us
  starting transfers between devices: 0.12 us -> 11.2 us
    psum x8 -> x0, blocking collectives: 466 us -> none  [spread(): return lax.psum(jnp.where(mine, shard, jnp.zeros_like(shard)), axis)]
    psum x1 -> x0, waiting for transfers between devices: 92.2 us -> none  [body(): whole_term = lax.psum(local_term, 'grp')]
    reduce_scatter x2 -> x0, waiting for transfers between devices: 49.6 us -> none  [the longest x1 29.2 us: body(): lax.psum_scatter(partial_value, 'rep', scatter_dimension=0, tiled=True)]
    ppermute x0 -> x7, waiting for transfers between devices: none -> 17.5 us  [swap(): return lax.ppermute(block, axis, [(at, at ^ step) for at in range(size)])]
    dot_general x11 -> x4, matrix products: 16.9 us -> 2.89 us  [matmul(): lax.dot_general(left, right, (contract, ((), ())), preferred_element_type...]
    ppermute x0 -> x7, starting transfers between devices: none -> 11.2 us  [swap(): return lax.ppermute(block, axis, [(at, at ^ step) for at in range(size)])]
  transfers between devices with their start and end apart: 3 -> 7, of which waited for: 3 -> 7; matrix products, arithmetic and copies ran while one was open for 0% -> 1% of each run, Pallas kernels for 0% -> 0%
where the time goes in v1:
time: 35.9 us; the launch traced here: 35.7 us
  waiting for transfers between devices  17.5 us (49%)
  starting transfers between devices  11.2 us (31%)
  other arithmetic  3.01 us (8%)
  matrix products  2.89 us (8%)
  between operations  0.88 us (2%)
    ppermute x7, waiting for transfers between devices, swap(): return lax.ppermute(block, axis, [(at, at ^ step) for at in range(size)])  17.5 us
    ppermute x7, starting transfers between devices, swap(): return lax.ppermute(block, axis, [(at, at ^ step) for at in range(size)])  11.2 us
    dot_general x4, matrix products, matmul(): lax.dot_general(left, right, (contract, ((), ())), preferred_element_type...  2.89 us
    convert_element_type x1, other arithmetic, scaled_part(): (part.astype(jnp.float32) * src_scale[:, None] * col[None, :]).astype(jnp...  1.16 us
    rsqrt x1, other arithmetic, body(): src_scale = lax.rsqrt(src_degree.astype(jnp.float32))  0.74 us
  transfers between devices with their start and end apart: 7, of which 7 were waited for; matrix products, arithmetic and copies ran while one was open for 1% of the time, Pallas kernels for 0%

profile of v1, /device:TPU:0, one launch (start us, length us, event | category | flops | bytes accessed | tf_op | source)
XLA Modules:
  0.0 35.7 jit_solution(5589823070084377814)
XLA Ops:
  0.6 0.0 copy-start
  0.6 0.0 copy-start.1
  0.7 0.7 %convert_rsqrt_fusion.1 = f32[128]{0:T(128)S(1)} fusion(s32[128]{0:T(128)} %param.10), kind=kLoop, calls=%fused_computation.36 | loop fusion | flops 128 | bytes 1024 | tf_op jit(solution)/shard_map/rsqrt | solution.py:44
  1.4 0.7 %convert_rsqrt_fusion = f32[1024]{0:T(1024)S(1)} fusion(s32[1024]{0:T(1024)} %param.11), kind=kLoop, calls=%fused_computation.35 | loop fusion | flops 1024 | bytes 8192 | tf_op jit(solution)/shard_map/rsqrt | solution.py:45
  2.1 0.1 fusion.24
  2.2 1.2 %multiply_convert_fusion.1 = (bf16[128,512]{1,0:T(8,128)(2,1)S(1)}, bf16[128,512]{1,0:T(8,128)(2,1)S(1)}) fusion(s32[128,1024]{1,0:T(8,128)} %param.9, s32[]{:T(128)S(6)} %select_n.138, f32[512]{0:T(512)S(1)} %get-tuple-element.16, f32[128]{0:T(128)S(1)} %convert_rsqrt_fusion.1, f32[512]{0:T(512)S(1)} %get-tuple-element.17, s32[]{:T(128)S(6)} %select_n.139), kind=kLoop, calls=%fused_computation.14 | loop fusion | flops 524288 | bytes 791048 | tf_op jit(solution)/shard_map/convert_element_type | solution.py:50
  3.3 3.0 %collective-permute-start = (bf16[128,512]{1,0:T(8,128)(2,1)S(1)}, bf16[128,512]{1,0:T(8,128)(2,1)S(1)}, u32[]{:S(2)}, u32[]{:S(2)}) collective-permute-start(bf16[128,512]{1,0:T(8,128)(2,1)S(1)} %get-tuple-element.2), channel_id=1, source_target_pairs={{0,1},{1,0},{2,3},{3,2},{4,5},{5,4},{6,7},{7,6},{8,9},{9,8},{10,11... | collective-permute-start | bytes 393224 | tf_op jit(solution)/shard_map/ppermute | solution.py:9
  6.4 0.0 copy-done.1
  6.4 0.2 fusion.26
  6.6 3.3 %collective-permute-done = bf16[128,512]{1,0:T(8,128)(2,1)S(1)} collective-permute-done((bf16[128,512]{1,0:T(8,128)(2,1)S(1)}, bf16[128,512]{1,0:T(8,128)(2,1)S(1)}, u32[]{:S(2)}, u32[]{:S(2)}) %collective-permute-start) | collective-permute-done | bytes 131104 | tf_op jit(solution)/shard_map/ppermute | solution.py:9
  9.9 0.2 fusion.25
  10.1 0.1 maximum_select_fusion
  10.2 0.1 collective-permute-start.1
  10.3 1.3 %collective-permute-done.1 = bf16[128,512]{1,0:T(8,128)(2,1)S(1)} collective-permute-done((bf16[128,512]{1,0:T(8,128)(2,1)S(1)}, bf16[128,512]{1,0:T(8,128)(2,1)S(1)}, u32[]{:S(2)}, u32[]{:S(2)}) %collective-permute-start.1) | collective-permute-done | bytes 131104 | tf_op jit(solution)/shard_map/ppermute | solution.py:9
  11.6 0.0 copy-start.2
  11.7 0.0 copy-start.3
  11.7 1.8 %collective-permute-start.2 = (bf16[128,256]{1,0:T(8,128)(2,1)S(1)}, bf16[128,256]{1,0:T(8,128)(2,1)S(1)}, u32[]{:S(2)}, u32[]{:S(2)}) collective-permute-start(bf16[128,256]{1,0:T(8,128)(2,1)S(1)} %select_convert_fusion.1), channel_id=1, source_target_pairs={{0,1},{1,0},{2,3},{3,2},{4,5},{5,4},{6,7},{7,6},{8,9},{9,8},{10,11... | collective-permute-start | bytes 196616 | tf_op jit(solution)/shard_map/ppermute | solution.py:9
  13.5 0.0 copy-done.2
  13.5 0.0 copy-done.3
  13.5 2.5 %collective-permute-done.2 = bf16[128,256]{1,0:T(8,128)(2,1)S(1)} collective-permute-done((bf16[128,256]{1,0:T(8,128)(2,1)S(1)}, bf16[128,256]{1,0:T(8,128)(2,1)S(1)}, u32[]{:S(2)}, u32[]{:S(2)}) %collective-permute-start.2) | collective-permute-done | bytes 65568 | tf_op jit(solution)/shard_map/ppermute | solution.py:9
  16.1 2.9 %collective-permute-start.3 = (bf16[80,512]{1,0:T(8,128)(2,1)S(1)}, bf16[80,512]{1,0:T(8,128)(2,1)S(1)}, u32[]{:S(2)}, u32[]{:S(2)}) collective-permute-start(bf16[80,512]{1,0:T(8,128)(2,1)S(1)} %pad_maximum_fusion.3), channel_id=1, source_target_pairs={{0,16},{2,18},{4,20},{6,22},{8,24},{10,26},{12,28},{14,30},{16,0},... | collective-permute-start | bytes 245768 | tf_op jit(solution)/shard_map/ppermute | solution.py:9
  19.0 2.7 %collective-permute-done.3 = bf16[80,512]{1,0:T(8,128)(2,1)S(1)} collective-permute-done((bf16[80,512]{1,0:T(8,128)(2,1)S(1)}, bf16[80,512]{1,0:T(8,128)(2,1)S(1)}, u32[]{:S(2)}, u32[]{:S(2)}) %collective-permute-start.3) | collective-permute-done | bytes 81952 | tf_op jit(solution)/shard_map/ppermute | solution.py:9
  21.7 1.7 %collective-permute-start.4 = (bf16[96,512]{1,0:T(8,128)(2,1)S(1)}, bf16[96,512]{1,0:T(8,128)(2,1)S(1)}, u32[]{:S(2)}, u32[]{:S(2)}) collective-permute-start(bf16[96,512]{1,0:T(8,128)(2,1)S(1)} %pad_maximum_fusion.2), channel_id=1, source_target_pairs={{0,8},{2,10},{4,12},{6,14},{8,0},{10,2},{12,4},{14,6},{16,24},{18,... | collective-permute-start | bytes 294920 | tf_op jit(solution)/shard_map/ppermute | solution.py:9
  23.5 3.0 %collective-permute-done.4 = bf16[96,512]{1,0:T(8,128)(2,1)S(1)} collective-permute-done((bf16[96,512]{1,0:T(8,128)(2,1)S(1)}, bf16[96,512]{1,0:T(8,128)(2,1)S(1)}, u32[]{:S(2)}, u32[]{:S(2)}) %collective-permute-start.4) | collective-permute-done | bytes 98336 | tf_op jit(solution)/shard_map/ppermute | solution.py:9
  26.5 1.6 %collective-permute-start.5 = (bf16[128,512]{1,0:T(8,128)(2,1)S(1)}, bf16[128,512]{1,0:T(8,128)(2,1)S(1)}, u32[]{:S(2)}, u32[]{:S(2)}) collective-permute-start(bf16[128,512]{1,0:T(8,128)(2,1)S(1)} %pad_maximum_fusion.1), channel_id=1, source_target_pairs={{0,4},{2,6},{4,0},{6,2},{8,12},{10,14},{12,8},{14,10},{16,20},{18,... | collective-permute-start | bytes 393224 | tf_op jit(solution)/shard_map/ppermute | solution.py:9
  28.1 3.4 %collective-permute-done.5 = bf16[128,512]{1,0:T(8,128)(2,1)S(1)} collective-permute-done((bf16[128,512]{1,0:T(8,128)(2,1)S(1)}, bf16[128,512]{1,0:T(8,128)(2,1)S(1)}, u32[]{:S(2)}, u32[]{:S(2)}) %collective-permute-start.5) | collective-permute-done | bytes 131104 | tf_op jit(solution)/shard_map/ppermute | solution.py:9
  31.6 0.1 collective-permute-start.6
  31.7 1.4 %collective-permute-done.6 = bf16[128,768]{1,0:T(8,128)(2,1)S(1)} collective-permute-done((bf16[128,768]{1,0:T(8,128)(2,1)S(1)}, bf16[128,768]{1,0:T(8,128)(2,1)S(1)}, u32[]{:S(2)}, u32[]{:S(2)}) %collective-permute-start.6) | collective-permute-done | bytes 196640 | tf_op jit(solution)/shard_map/ppermute | solution.py:9
  33.1 0.1 maximum_select_fusion.1
  33.2 1.0 %convolution_multiply_fusion = f32[256,512]{1,0:T(8,128)} fusion(bf16[256,768]{1,0:T(8,128)(2,1)S(1)} %bitcast.33), kind=kOutput, calls=%fused_computation.2 | convolution fusion | flops 67239936 | bytes 917504 | tf_op jit(solution)/shard_map/dot_general | solution.py:32
  34.3 0.0 copy-done
  34.3 1.4 %convolution_convert_fusion = bf16[512,512]{1,0:T(8,128)(2,1)} fusion(bf16[512,512]{1,0:T(8,128)(2,1)S(1)} %copy-done, bf16[128,512]{1,0:T(8,128)(2,1)S(1)} %get-tuple-element.3, bf16[128,512]{1,0:T(8,128)(2,1)S(1)} %collective-permute-done, pred[]{:T(512)S(6)} %ne.17, bf16[256,768]{1,0:T(8,128)(2,1)S(1)} %bitcast.34), kind=kOutput, calls=%fused_computation | convolution fusion | flops 404357120 | bytes 1572865 | tf_op jit(solution)/shard_map/dot_general | solution.py:32
  (27 shorter events, 0.4 us)
Async XLA Ops:
  0.6 33.7 %copy-start = (bf16[512,512]{1,0:T(8,128)(2,1)S(1)}, bf16[512,512]{1,0:T(8,128)(2,1)}, u32[]{:S(2)}) copy-start(bf16[512,512]{1,0:T(8,128)(2,1)} %param.13) | copy-start | bytes 1572868
  0.6 5.7 %copy-start.1 = (bf16[512,512]{1,0:T(8,128)(2,1)S(1)}, bf16[512,512]{1,0:T(8,128)(2,1)}, u32[]{:S(2)}) copy-start(bf16[512,512]{1,0:T(8,128)(2,1)} %param.12) | copy-start | bytes 1572868
  3.3 6.5 %collective-permute-start = (bf16[128,512]{1,0:T(8,128)(2,1)S(1)}, bf16[128,512]{1,0:T(8,128)(2,1)S(1)}, u32[]{:S(2)}, u32[]{:S(2)}) collective-permute-start(bf16[128,512]{1,0:T(8,128)(2,1)S(1)} %get-tuple-element.2), channel_id=1, source_target_pairs={{0,1},{1,0},{2,3},{3,2},{4,5},{5,4},{6,7},{7,6},{8,9},{9,8},{10,11... | collective-permute-start | bytes 393224 | tf_op jit(solution)/shard_map/ppermute | solution.py:9
  10.2 1.4 %collective-permute-start.1 = (bf16[128,512]{1,0:T(8,128)(2,1)S(1)}, bf16[128,512]{1,0:T(8,128)(2,1)S(1)}, u32[]{:S(2)}, u32[]{:S(2)}) collective-permute-start(bf16[128,512]{1,0:T(8,128)(2,1)S(1)} %bitcast.44), channel_id=1, source_target_pairs={{0,2},{2,0},{4,6},{6,4},{8,10},{10,8},{12,14},{14,12},{16,18},{18,... | collective-permute-start | bytes 393224 | tf_op jit(solution)/shard_map/ppermute | solution.py:9
  11.6 1.9 %copy-start.2 = (s32[16,512]{1,0:T(8,128)S(1)}, s32[16,512]{1,0:T(8,128)}, u32[]{:S(2)}) copy-start(s32[16,512]{1,0:T(8,128)} %param.8) | copy-start | bytes 98308
  11.7 1.8 %copy-start.3 = (bf16[16,512]{1,0:T(8,128)(2,1)S(1)}, bf16[16,512]{1,0:T(8,128)(2,1)}, u32[]{:S(2)}) copy-start(bf16[16,512]{1,0:T(8,128)(2,1)} %param.7) | copy-start | bytes 49156
  11.7 4.3 %collective-permute-start.2 = (bf16[128,256]{1,0:T(8,128)(2,1)S(1)}, bf16[128,256]{1,0:T(8,128)(2,1)S(1)}, u32[]{:S(2)}, u32[]{:S(2)}) collective-permute-start(bf16[128,256]{1,0:T(8,128)(2,1)S(1)} %select_convert_fusion.1), channel_id=1, source_target_pairs={{0,1},{1,0},{2,3},{3,2},{4,5},{5,4},{6,7},{7,6},{8,9},{9,8},{10,11... | collective-permute-start | bytes 196616 | tf_op jit(solution)/shard_map/ppermute | solution.py:9
  16.1 5.5 %collective-permute-start.3 = (bf16[80,512]{1,0:T(8,128)(2,1)S(1)}, bf16[80,512]{1,0:T(8,128)(2,1)S(1)}, u32[]{:S(2)}, u32[]{:S(2)}) collective-permute-start(bf16[80,512]{1,0:T(8,128)(2,1)S(1)} %pad_maximum_fusion.3), channel_id=1, source_target_pairs={{0,16},{2,18},{4,20},{6,22},{8,24},{10,26},{12,28},{14,30},{16,0},... | collective-permute-start | bytes 245768 | tf_op jit(solution)/shard_map/ppermute | solution.py:9
  21.7 4.7 %collective-permute-start.4 = (bf16[96,512]{1,0:T(8,128)(2,1)S(1)}, bf16[96,512]{1,0:T(8,128)(2,1)S(1)}, u32[]{:S(2)}, u32[]{:S(2)}) collective-permute-start(bf16[96,512]{1,0:T(8,128)(2,1)S(1)} %pad_maximum_fusion.2), channel_id=1, source_target_pairs={{0,8},{2,10},{4,12},{6,14},{8,0},{10,2},{12,4},{14,6},{16,24},{18,... | collective-permute-start | bytes 294920 | tf_op jit(solution)/shard_map/ppermute | solution.py:9
  26.5 5.0 %collective-permute-start.5 = (bf16[128,512]{1,0:T(8,128)(2,1)S(1)}, bf16[128,512]{1,0:T(8,128)(2,1)S(1)}, u32[]{:S(2)}, u32[]{:S(2)}) collective-permute-start(bf16[128,512]{1,0:T(8,128)(2,1)S(1)} %pad_maximum_fusion.1), channel_id=1, source_target_pairs={{0,4},{2,6},{4,0},{6,2},{8,12},{10,14},{12,8},{14,10},{16,20},{18,... | collective-permute-start | bytes 393224 | tf_op jit(solution)/shard_map/ppermute | solution.py:9
  31.6 1.5 %collective-permute-start.6 = (bf16[128,768]{1,0:T(8,128)(2,1)S(1)}, bf16[128,768]{1,0:T(8,128)(2,1)S(1)}, u32[]{:S(2)}, u32[]{:S(2)}) collective-permute-start(bf16[128,768]{1,0:T(8,128)(2,1)S(1)} %pad_maximum_fusion), channel_id=1, source_target_pairs={{0,2},{2,0},{4,6},{6,4},{8,10},{10,8},{12,14},{14,12},{16,18},{18,... | collective-permute-start | bytes 589832 | tf_op jit(solution)/shard_map/ppermute | solution.py:9

commit v2 on v1

v2 whole, which is shorter than its diff:
```python
import functools

import jax
import jax.numpy as jnp
from jax import lax
from jax.experimental import pallas as pl
from jax.experimental.pallas import tpu as pltpu
from jax.sharding import PartitionSpec as P


def swap(block, axis, step):
    size = lax.axis_size(axis)
    return lax.ppermute(block, axis, [(at, at ^ step) for at in range(size)])


def bit_of(index, step):
    return (index & step) != 0


def in_order(upper, mine, theirs, axis):
    return jnp.where(
        upper,
        jnp.concatenate([theirs, mine], axis),
        jnp.concatenate([mine, theirs], axis),
    )


def half_of(block, axis, upper):
    size = block.shape[axis] // 2
    low = lax.slice_in_dim(block, 0, size, axis=axis)
    high = lax.slice_in_dim(block, size, 2 * size, axis=axis)
    return jnp.where(upper, high, low)


def part_of(block, axis, index, parts):
    step = parts // 2
    while step:
        block = half_of(block, axis, bit_of(index, step))
        step //= 2
    return block


def matmul(left, right, contract):
    return lax.dot_general(
        left, right, (contract, ((), ())), preferred_element_type=jnp.float32
    )


CHUNKS = 4


def prepare_kernel(replicas, counts, src_degree, dst_degree, *refs):
    outs, (count_part, src_part, dst_part, sems) = refs[:replicas], refs[replicas:]
    src_rows, rows = outs[0].shape
    piece = src_rows // CHUNKS
    replica = lax.axis_index("rep")
    owners = [replica ^ step for step in range(1, replicas)] + [replica]
    degrees = [
        pltpu.make_async_copy(src_degree, src_part, sems.at[0]),
        pltpu.make_async_copy(dst_degree, dst_part, sems.at[1]),
    ]
    for copy in degrees:
        copy.start()
    copies = []
    for slot, owner in enumerate(owners):
        columns = pl.ds(pl.multiple_of(owner * rows, 128), rows)
        for chunk in range(CHUNKS):
            at = pl.ds(chunk * piece, piece)
            copy = pltpu.make_async_copy(
                counts.at[at, columns], count_part.at[slot, at], sems.at[2 + slot * CHUNKS + chunk]
            )
            copy.start()
            copies.append(copy)
    for copy in degrees:
        copy.wait()
    src_row = lax.rsqrt(src_part[...].astype(jnp.float32)).reshape(1, src_rows)
    square = (src_rows, src_rows)
    diagonal = lax.broadcasted_iota(jnp.int32, square, 0) == lax.broadcasted_iota(jnp.int32, square, 1)
    src_column = jnp.sum(
        jnp.where(diagonal, jnp.broadcast_to(src_row, square), 0.0), axis=1, keepdims=True
    )
    for slot, owner in enumerate(owners):
        pieces = [dst_part[at * rows : (at + 1) * rows] for at in range(replicas)]
        bit = 1
        while len(pieces) > 1:
            upper = bit_of(owner, bit)
            pieces = [jnp.where(upper, b, a) for a, b in zip(pieces[0::2], pieces[1::2])]
            bit *= 2
        dst_row = lax.rsqrt(pieces[0].astype(jnp.float32)).reshape(1, rows)
        for chunk in range(CHUNKS):
            at = slice(chunk * piece, (chunk + 1) * piece)
            copies[slot * CHUNKS + chunk].wait()
            values = count_part[slot, at, :].astype(jnp.float32)
            outs[slot][at, :] = (values * src_column[at] * dst_row).astype(jnp.bfloat16)


def prepare(counts, src_degree, dst_degree, replicas, rows):
    src_rows = counts.shape[0]
    return pl.pallas_call(
        functools.partial(prepare_kernel, replicas),
        out_shape=[pltpu.VMEM((src_rows, rows), jnp.bfloat16)] * replicas,
        in_specs=[pl.BlockSpec(memory_space=pl.ANY)] * 3,
        out_specs=[pl.BlockSpec(memory_space=pltpu.VMEM)] * replicas,
        scratch_shapes=[
            pltpu.VMEM((replicas, src_rows, rows), jnp.int32),
            pltpu.VMEM(src_degree.shape, jnp.int32),
            pltpu.VMEM(dst_degree.shape, jnp.int32),
            pltpu.SemaphoreType.DMA((2 + CHUNKS * replicas,)),
        ],
    )(counts, src_degree, dst_degree)


def own_kernel(own, inputs, term):
    term[...] = jnp.dot(own[...], inputs[...], preferred_element_type=jnp.float32)


def own_product(own, inputs):
    (src_rows, rows), width = own.shape, inputs.shape[1]
    return pl.pallas_call(
        own_kernel,
        out_shape=pltpu.VMEM((src_rows, width), jnp.float32),
        in_specs=[pl.BlockSpec(memory_space=pltpu.VMEM)] * 2,
        out_specs=pl.BlockSpec(memory_space=pltpu.VMEM),
        cost_estimate=pl.CostEstimate(
            flops=2 * src_rows * rows * width,
            bytes_accessed=2 * rows * (src_rows + width),
            transcendentals=0,
        ),
    )(*[pltpu.with_memory_space_constraint(block, pltpu.VMEM) for block in (own, inputs)])


def body(adjoint, active, counts, src_degree, dst_degree, inputs, weight):
    groups, replicas = lax.axis_size("grp"), lax.axis_size("rep")
    group, replica = lax.axis_index("grp"), lax.axis_index("rep")
    rows, width = inputs.shape
    block_rows = adjoint.shape[0]
    odd = bit_of(group, 1)

    *sent, own = prepare(counts, src_degree, dst_degree, replicas, rows)
    answers = [swap(part, "rep", step) for step, part in enumerate(sent, 1)]

    own_term = own_product(own, inputs)
    masked = (adjoint.astype(jnp.float32) * active.astype(jnp.float32)).astype(jnp.bfloat16)

    def gathered(mine, theirs, step):
        return in_order(
            bit_of(group, step),
            mine.reshape(-1, 1, block_rows, width),
            theirs.reshape(-1, 1, block_rows, width),
            1,
        ).reshape(-1, width)

    far = groups // 2
    theirs = swap(masked, "grp", far) if far > 1 else masked
    answers, own_term = lax.optimization_barrier((answers, own_term))
    parts = [own] + answers
    terms = [own_term] + [matmul(part, inputs, ((1,), (0,))) for part in answers]

    def ordered(pieces):
        step = 1
        while len(pieces) > 1:
            upper = bit_of(replica, step)
            pieces = [in_order(upper, a, b, 0) for a, b in zip(pieces[0::2], pieces[1::2])]
            step *= 2
        return pieces[0]

    def halves(block):
        pairs = block.reshape(groups // 2, 2, block_rows, block.shape[1])
        even = pairs[:, 0].reshape(-1, block.shape[1])
        uneven = pairs[:, 1].reshape(-1, block.shape[1])
        return jnp.where(odd, uneven, even), jnp.where(odd, even, uneven)

    kept, sent = halves(ordered(terms))
    total = kept + swap(sent.astype(jnp.bfloat16), "grp", 1).astype(jnp.float32)

    total, theirs = lax.optimization_barrier((total, theirs))
    mine = gathered(masked, theirs, far) if far > 1 else masked

    step = replicas // 2
    while step:
        upper = bit_of(replica, step)
        theirs = swap(half_of(total, 1, ~upper).astype(jnp.bfloat16), "rep", step)
        total = half_of(total, 1, upper) + theirs.astype(jnp.float32)
        step //= 2

    step = far // 2
    while step > 1:
        sent = total.astype(jnp.bfloat16)
        flat = jnp.concatenate(jnp.split(sent, replicas, axis=0), axis=1)
        answer = swap(jnp.concatenate([flat, mine], axis=0), "grp", step)
        count = flat.shape[0]
        theirs = jnp.concatenate(jnp.split(answer[:count], replicas, axis=1), axis=0)
        total = sent.astype(jnp.float32) + theirs.astype(jnp.float32)
        mine = gathered(mine, answer[count:], step)
        step //= 2
    theirs = swap(mine, "grp", 1)
    scaled_mine, scaled_theirs = halves(ordered(parts))
    grad_pre = matmul(scaled_mine, mine, ((0,), (0,)))
    grad_pre += matmul(scaled_theirs, theirs, ((0,), (0,)))
    grad_input = matmul(grad_pre.astype(jnp.bfloat16), weight, ((1,), (1,))).astype(jnp.bfloat16)
    if far > 1:
        sent = total.astype(jnp.bfloat16)
        answer = swap(sent, "grp", far)
        answer, grad_input = lax.optimization_barrier((answer, grad_input))
        total = sent.astype(jnp.float32) + answer.astype(jnp.float32)

    total = total.astype(jnp.bfloat16)
    other = swap(total, "grp", 1)
    vertex_total = rows * groups * replicas
    grad_weight = matmul(total, mine, ((0,), (0,))) + matmul(other, theirs, ((0,), (0,)))
    return (grad_input, grad_weight / vertex_total)


def solution(mesh):
    in_specs = (
        P("grp", None),
        P("grp", None),
        P("rep", "grp"),
        P("rep"),
        P("grp"),
        P(("grp", "rep"), None),
        P(),
    )
    out_specs = (P(("grp", "rep"), None), P("rep", None))
    return jax.shard_map(body, mesh=mesh, in_specs=in_specs, out_specs=out_specs, check_vma=False)
```

time: 35.9 us -> 32.8 us (0.914)
  waiting for transfers between devices: 17.5 us -> 12.3 us
  starting transfers between devices: 11.2 us -> 14.4 us
  other arithmetic: 3.01 us -> 0.4 us
  Pallas kernels: 0 us -> 1.49 us
    ppermute x7 -> x9, waiting for transfers between devices: 17.5 us -> 12.3 us  [swap(): return lax.ppermute(block, axis, [(at, at ^ step) for at in range(size)])]
    ppermute x7 -> x9, starting transfers between devices: 11.2 us -> 14.4 us  [swap(): return lax.ppermute(block, axis, [(at, at ^ step) for at in range(size)])]
    pallas_call x0 -> x2, Pallas kernels: none -> 1.49 us  [the longest x1 1.27 us: prepare(): pl.pallas_call(functools.partial(prepare_kernel, replicas), out_shape=[pl...]
    rsqrt x2 -> x0, other arithmetic: 1.44 us -> none  [the longest x1 0.74 us: body(): src_scale = lax.rsqrt(src_degree.astype(jnp.float32))]
    convert_element_type x3 -> x2, other arithmetic: 1.2 us -> 0.05 us  [the longest x1 0.03 us: body(): total = kept + swap(sent.astype(jnp.bfloat16), 'grp', 1).astype(jnp.float32)]
    dot_general x4 -> x5, matrix products: 2.89 us -> 3.21 us  [matmul(): lax.dot_general(left, right, (contract, ((), ())), preferred_element_type...]
  transfers between devices with their start and end apart: 7 -> 9, of which waited for: 7 -> 7; matrix products, arithmetic and copies ran while one was open for 1% -> 7% of each run, Pallas kernels for 0% -> 1%
where the time goes in v2:
time: 32.8 us; the launch traced here: 32.6 us
  starting transfers between devices  14.4 us (44%)
  waiting for transfers between devices  12.3 us (38%)
  matrix products  3.21 us (10%)
  Pallas kernels  1.49 us (5%)
  between operations  0.84 us (3%)
  other arithmetic  0.4 us (1%)
    ppermute x9, starting transfers between devices, swap(): return lax.ppermute(block, axis, [(at, at ^ step) for at in range(size)])  14.4 us
    ppermute x9, waiting for transfers between devices, swap(): return lax.ppermute(block, axis, [(at, at ^ step) for at in range(size)])  12.3 us
    dot_general x5, matrix products, matmul(): lax.dot_general(left, right, (contract, ((), ())), preferred_element_type...  3.21 us
    pallas_call x1, Pallas kernels, prepare(): pl.pallas_call(functools.partial(prepare_kernel, replicas), out_shape=[pl...  1.27 us
  transfers between devices with their start and end apart: 9, of which 7 were waited for; matrix products, arithmetic and copies ran while one was open for 7% of the time, Pallas kernels for 1%

profile of v2, /device:TPU:0, one launch (start us, length us, event | category | flops | bytes accessed | tf_op | source)
XLA Modules:
  0.0 32.6 jit_solution(4408181309158095047)
XLA Ops:
  0.6 0.0 copy-start
  0.6 0.0 copy-start.2
  0.7 0.0 copy-start.3
  0.7 0.0 copy-start.1
  0.7 1.3 %shard_map.86 = (bf16[128,512]{1,0:T(8,128)(2,1)S(1)}, bf16[128,512]{1,0:T(8,128)(2,1)S(1)}) custom-call(s32[128,1024]{1,0:T(8,128)} %counts.1, s32[128]{0:T(128)} %src_degree.1, s32[1024]{0:T(1024)} %dst_degree.1), custom_call_target="tpu_custom_call" | custom-call | tf_op jit(solution)/shard_map/pallas_call | solution.py:99
  2.0 3.0 %collective-permute-start = (bf16[128,512]{1,0:T(8,128)(2,1)S(1)}, bf16[128,512]{1,0:T(8,128)(2,1)S(1)}, u32[]{:S(2)}, u32[]{:S(2)}) collective-permute-start(bf16[128,512]{1,0:T(8,128)(2,1)S(1)} %get-tuple-element.10), channel_id=1, source_target_pairs={{0,1},{1,0},{2,3},{3,2},{4,5},{5,4},{6,7},{7,6},{8,9},{9,8},{10,11... | collective-permute-start | bytes 393224 | tf_op jit(solution)/shard_map/ppermute | solution.py:13
  5.0 0.0 copy-done.2
  5.0 0.0 copy-done.3
  5.0 2.7 %collective-permute-start.2 = (bf16[16,512]{1,0:T(8,128)(2,1)S(1)}, bf16[16,512]{1,0:T(8,128)(2,1)S(1)}, u32[]{:S(2)}, u32[]{:S(2)}) collective-permute-start(bf16[16,512]{1,0:T(8,128)(2,1)S(1)} %multiply_convert_fusion), channel_id=1, source_target_pairs={{0,16},{2,18},{4,20},{6,22},{8,24},{10,26},{12,28},{14,30},{16,0},... | collective-permute-start | bytes 49160 | tf_op jit(solution)/shard_map/ppermute | solution.py:13
  7.7 0.0 copy-done.1
  7.7 0.2 shard_map.87
  7.9 0.6 %collective-permute-done = bf16[128,512]{1,0:T(8,128)(2,1)S(1)} collective-permute-done((bf16[128,512]{1,0:T(8,128)(2,1)S(1)}, bf16[128,512]{1,0:T(8,128)(2,1)S(1)}, u32[]{:S(2)}, u32[]{:S(2)}) %collective-permute-start) | collective-permute-done | bytes 131104 | tf_op jit(solution)/shard_map/ppermute | solution.py:13
  8.5 0.2 fusion.6
  8.7 0.1 maximum_select_fusion
  8.8 0.1 collective-permute-start.1
  8.9 0.1 maximum_select_fusion.1
  9.0 1.2 %collective-permute-done.1 = bf16[128,512]{1,0:T(8,128)(2,1)S(1)} collective-permute-done((bf16[128,512]{1,0:T(8,128)(2,1)S(1)}, bf16[128,512]{1,0:T(8,128)(2,1)S(1)}, u32[]{:S(2)}, u32[]{:S(2)}) %collective-permute-start.1) | collective-permute-done | bytes 131104 | tf_op jit(solution)/shard_map/ppermute | solution.py:13
  10.3 0.0 collective-permute-done.2
  10.3 1.8 %collective-permute-start.3 = (bf16[128,256]{1,0:T(8,128)(2,1)S(1)}, bf16[128,256]{1,0:T(8,128)(2,1)S(1)}, u32[]{:S(2)}, u32[]{:S(2)}) collective-permute-start(bf16[128,256]{1,0:T(8,128)(2,1)S(1)} %select_convert_fusion.1), channel_id=1, source_target_pairs={{0,1},{1,0},{2,3},{3,2},{4,5},{5,4},{6,7},{7,6},{8,9},{9,8},{10,11... | collective-permute-start | bytes 196616 | tf_op jit(solution)/shard_map/ppermute | solution.py:13
  12.1 2.5 %collective-permute-done.3 = bf16[128,256]{1,0:T(8,128)(2,1)S(1)} collective-permute-done((bf16[128,256]{1,0:T(8,128)(2,1)S(1)}, bf16[128,256]{1,0:T(8,128)(2,1)S(1)}, u32[]{:S(2)}, u32[]{:S(2)}) %collective-permute-start.3) | collective-permute-done | bytes 65568 | tf_op jit(solution)/shard_map/ppermute | solution.py:13
  14.7 1.9 %collective-permute-start.4 = (bf16[96,512]{1,0:T(8,128)(2,1)S(1)}, bf16[96,512]{1,0:T(8,128)(2,1)S(1)}, u32[]{:S(2)}, u32[]{:S(2)}) collective-permute-start(bf16[96,512]{1,0:T(8,128)(2,1)S(1)} %pad_maximum_fusion.1), channel_id=1, source_target_pairs={{0,8},{2,10},{4,12},{6,14},{8,0},{10,2},{12,4},{14,6},{16,24},{18,... | collective-permute-start | bytes 294920 | tf_op jit(solution)/shard_map/ppermute | solution.py:13
  16.6 2.8 %collective-permute-done.4 = bf16[96,512]{1,0:T(8,128)(2,1)S(1)} collective-permute-done((bf16[96,512]{1,0:T(8,128)(2,1)S(1)}, bf16[96,512]{1,0:T(8,128)(2,1)S(1)}, u32[]{:S(2)}, u32[]{:S(2)}) %collective-permute-start.4) | collective-permute-done | bytes 98336 | tf_op jit(solution)/shard_map/ppermute | solution.py:13
  19.5 1.8 %collective-permute-start.5 = (bf16[128,512]{1,0:T(8,128)(2,1)S(1)}, bf16[128,512]{1,0:T(8,128)(2,1)S(1)}, u32[]{:S(2)}, u32[]{:S(2)}) collective-permute-start(bf16[128,512]{1,0:T(8,128)(2,1)S(1)} %pad_maximum_fusion), channel_id=1, source_target_pairs={{0,4},{2,6},{4,0},{6,2},{8,12},{10,14},{12,8},{14,10},{16,20},{18,... | collective-permute-start | bytes 393224 | tf_op jit(solution)/shard_map/ppermute | solution.py:13
  21.3 3.2 %collective-permute-done.5 = bf16[128,512]{1,0:T(8,128)(2,1)S(1)} collective-permute-done((bf16[128,512]{1,0:T(8,128)(2,1)S(1)}, bf16[128,512]{1,0:T(8,128)(2,1)S(1)}, u32[]{:S(2)}, u32[]{:S(2)}) %collective-permute-start.5) | collective-permute-done | bytes 131104 | tf_op jit(solution)/shard_map/ppermute | solution.py:13
  24.5 2.9 %collective-permute-start.6 = (bf16[128,256]{1,0:T(8,128)(2,1)S(1)}, bf16[128,256]{1,0:T(8,128)(2,1)S(1)}, u32[]{:S(2)}, u32[]{:S(2)}) collective-permute-start(bf16[128,256]{1,0:T(8,128)(2,1)S(1)} %add_convert_fusion.1), channel_id=1, source_target_pairs={{0,16},{2,18},{4,20},{6,22},{8,24},{10,26},{12,28},{14,30},{16,0},... | collective-permute-start | bytes 196616 | tf_op jit(solution)/shard_map/ppermute | solution.py:13
  27.4 0.1 collective-permute-start.7
  27.5 0.3 fusion.7
  27.8 1.0 %collective-permute-done.7 = bf16[128,512]{1,0:T(8,128)(2,1)S(1)} collective-permute-done((bf16[128,512]{1,0:T(8,128)(2,1)S(1)}, bf16[128,512]{1,0:T(8,128)(2,1)S(1)}, u32[]{:S(2)}, u32[]{:S(2)}) %collective-permute-start.7) | collective-permute-done | bytes 131104 | tf_op jit(solution)/shard_map/ppermute | solution.py:13
  28.8 0.0 copy-done
  28.8 1.4 %convolution_convert_fusion = bf16[512,512]{1,0:T(8,128)(2,1)} fusion(bf16[512,512]{1,0:T(8,128)(2,1)S(1)} %copy-done, f32[512,512]{1,0:T(8,128)S(1)} %fusion.7, bf16[128,512]{1,0:T(8,128)(2,1)S(1)} %bitcast.34, bf16[128,512]{1,0:T(8,128)(2,1)S(1)} %collective-permute-done.7), kind=kOutput, calls=%fused_computation.2 | convolution fusion | flops 336330752 | bytes 2359296 | tf_op jit(solution)/shard_map/dot_general | solution.py:44
  30.2 0.0 collective-permute-done.6
  30.3 0.2 collective-permute-start.8
  30.5 0.2 fusion.8
  30.7 0.9 %collective-permute-done.8 = bf16[128,256]{1,0:T(8,128)(2,1)S(1)} collective-permute-done((bf16[128,256]{1,0:T(8,128)(2,1)S(1)}, bf16[128,256]{1,0:T(8,128)(2,1)S(1)}, u32[]{:S(2)}, u32[]{:S(2)}) %collective-permute-start.8) | collective-permute-done | bytes 65568 | tf_op jit(solution)/shard_map/ppermute | solution.py:13
  31.6 1.0 %fusion.1 = f32[256,512]{1,0:T(8,128)} fusion(f32[256,512]{1,0:T(8,128)S(1)} %fusion.8, bf16[128,256]{1,0:T(8,128)(2,1)S(1)} %collective-permute-done.8, bf16[128,512]{1,0:T(8,128)(2,1)S(1)} %collective-permute-done.7), kind=kOutput, calls=%fused_computation.4 | convolution fusion | flops 33816576 | bytes 1245184 | tf_op jit(solution)/shard_map/dot_general | solution.py:44
  (22 shorter events, 0.3 us)
Async XLA Ops:
  0.6 28.2 %copy-start = (bf16[512,512]{1,0:T(8,128)(2,1)S(1)}, bf16[512,512]{1,0:T(8,128)(2,1)}, u32[]{:S(2)}) copy-start(bf16[512,512]{1,0:T(8,128)(2,1)} %param.13) | copy-start | bytes 1572868
  0.6 4.3 %copy-start.2 = (s32[16,512]{1,0:T(8,128)S(1)}, s32[16,512]{1,0:T(8,128)}, u32[]{:S(2)}) copy-start(s32[16,512]{1,0:T(8,128)} %param.8) | copy-start | bytes 98308
  0.7 4.3 %copy-start.3 = (bf16[16,512]{1,0:T(8,128)(2,1)S(1)}, bf16[16,512]{1,0:T(8,128)(2,1)}, u32[]{:S(2)}) copy-start(bf16[16,512]{1,0:T(8,128)(2,1)} %param.7) | copy-start | bytes 49156
  0.7 7.0 %copy-start.1 = (bf16[512,512]{1,0:T(8,128)(2,1)S(1)}, bf16[512,512]{1,0:T(8,128)(2,1)}, u32[]{:S(2)}) copy-start(bf16[512,512]{1,0:T(8,128)(2,1)} %inputs.1) | copy-start | bytes 1572868
  2.0 6.5 %collective-permute-start = (bf16[128,512]{1,0:T(8,128)(2,1)S(1)}, bf16[128,512]{1,0:T(8,128)(2,1)S(1)}, u32[]{:S(2)}, u32[]{:S(2)}) collective-permute-start(bf16[128,512]{1,0:T(8,128)(2,1)S(1)} %get-tuple-element.10), channel_id=1, source_target_pairs={{0,1},{1,0},{2,3},{3,2},{4,5},{5,4},{6,7},{7,6},{8,9},{9,8},{10,11... | collective-permute-start | bytes 393224 | tf_op jit(solution)/shard_map/ppermute | solution.py:13
  5.0 5.3 %collective-permute-start.2 = (bf16[16,512]{1,0:T(8,128)(2,1)S(1)}, bf16[16,512]{1,0:T(8,128)(2,1)S(1)}, u32[]{:S(2)}, u32[]{:S(2)}) collective-permute-start(bf16[16,512]{1,0:T(8,128)(2,1)S(1)} %multiply_convert_fusion), channel_id=1, source_target_pairs={{0,16},{2,18},{4,20},{6,22},{8,24},{10,26},{12,28},{14,30},{16,0},... | collective-permute-start | bytes 49160 | tf_op jit(solution)/shard_map/ppermute | solution.py:13
  8.8 1.4 %collective-permute-start.1 = (bf16[128,512]{1,0:T(8,128)(2,1)S(1)}, bf16[128,512]{1,0:T(8,128)(2,1)S(1)}, u32[]{:S(2)}, u32[]{:S(2)}) collective-permute-start(bf16[128,512]{1,0:T(8,128)(2,1)S(1)} %bitcast.39), channel_id=1, source_target_pairs={{0,2},{2,0},{4,6},{6,4},{8,10},{10,8},{12,14},{14,12},{16,18},{18,... | collective-permute-start | bytes 393224 | tf_op jit(solution)/shard_map/ppermute | solution.py:13
  10.3 4.3 %collective-permute-start.3 = (bf16[128,256]{1,0:T(8,128)(2,1)S(1)}, bf16[128,256]{1,0:T(8,128)(2,1)S(1)}, u32[]{:S(2)}, u32[]{:S(2)}) collective-permute-start(bf16[128,256]{1,0:T(8,128)(2,1)S(1)} %select_convert_fusion.1), channel_id=1, source_target_pairs={{0,1},{1,0},{2,3},{3,2},{4,5},{5,4},{6,7},{7,6},{8,9},{9,8},{10,11... | collective-permute-start | bytes 196616 | tf_op jit(solution)/shard_map/ppermute | solution.py:13
  14.7 4.7 %collective-permute-start.4 = (bf16[96,512]{1,0:T(8,128)(2,1)S(1)}, bf16[96,512]{1,0:T(8,128)(2,1)S(1)}, u32[]{:S(2)}, u32[]{:S(2)}) collective-permute-start(bf16[96,512]{1,0:T(8,128)(2,1)S(1)} %pad_maximum_fusion.1), channel_id=1, source_target_pairs={{0,8},{2,10},{4,12},{6,14},{8,0},{10,2},{12,4},{14,6},{16,24},{18,... | collective-permute-start | bytes 294920 | tf_op jit(solution)/shard_map/ppermute | solution.py:13
  19.5 5.0 %collective-permute-start.5 = (bf16[128,512]{1,0:T(8,128)(2,1)S(1)}, bf16[128,512]{1,0:T(8,128)(2,1)S(1)}, u32[]{:S(2)}, u32[]{:S(2)}) collective-permute-start(bf16[128,512]{1,0:T(8,128)(2,1)S(1)} %pad_maximum_fusion), channel_id=1, source_target_pairs={{0,4},{2,6},{4,0},{6,2},{8,12},{10,14},{12,8},{14,10},{16,20},{18,... | collective-permute-start | bytes 393224 | tf_op jit(solution)/shard_map/ppermute | solution.py:13
  24.5 5.7 %collective-permute-start.6 = (bf16[128,256]{1,0:T(8,128)(2,1)S(1)}, bf16[128,256]{1,0:T(8,128)(2,1)S(1)}, u32[]{:S(2)}, u32[]{:S(2)}) collective-permute-start(bf16[128,256]{1,0:T(8,128)(2,1)S(1)} %add_convert_fusion.1), channel_id=1, source_target_pairs={{0,16},{2,18},{4,20},{6,22},{8,24},{10,26},{12,28},{14,30},{16,0},... | collective-permute-start | bytes 196616 | tf_op jit(solution)/shard_map/ppermute | solution.py:13
  27.4 1.4 %collective-permute-start.7 = (bf16[128,512]{1,0:T(8,128)(2,1)S(1)}, bf16[128,512]{1,0:T(8,128)(2,1)S(1)}, u32[]{:S(2)}, u32[]{:S(2)}) collective-permute-start(bf16[128,512]{1,0:T(8,128)(2,1)S(1)} %bitcast.28), channel_id=1, source_target_pairs={{0,2},{2,0},{4,6},{6,4},{8,10},{10,8},{12,14},{14,12},{16,18},{18,... | collective-permute-start | bytes 393224 | tf_op jit(solution)/shard_map/ppermute | solution.py:13
  30.3 1.3 %collective-permute-start.8 = (bf16[128,256]{1,0:T(8,128)(2,1)S(1)}, bf16[128,256]{1,0:T(8,128)(2,1)S(1)}, u32[]{:S(2)}, u32[]{:S(2)}) collective-permute-start(bf16[128,256]{1,0:T(8,128)(2,1)S(1)} %add_convert_fusion), channel_id=1, source_target_pairs={{0,2},{2,0},{4,6},{6,4},{8,10},{10,8},{12,14},{14,12},{16,18},{18,... | collective-permute-start | bytes 196616 | tf_op jit(solution)/shard_map/ppermute | solution.py:13

commit v3 on v2

--- a/solution.py
+++ b/solution.py
@@ -143,10 +143,11 @@
     masked = (adjoint.astype(jnp.float32) * active.astype(jnp.float32)).astype(jnp.bfloat16)
 
     def gathered(mine, theirs, step):
+        run = block_rows * (2 if 2 < step < groups // 2 else 1)
         return in_order(
             bit_of(group, step),
-            mine.reshape(-1, 1, block_rows, width),
-            theirs.reshape(-1, 1, block_rows, width),
+            mine.reshape(-1, 1, run, width),
+            theirs.reshape(-1, 1, run, width),
             1,
         ).reshape(-1, width)
 
@@ -176,32 +177,34 @@
     total, theirs = lax.optimization_barrier((total, theirs))
     mine = gathered(masked, theirs, far) if far > 1 else masked
 
+    near = None
     step = replicas // 2
     while step:
         upper = bit_of(replica, step)
-        theirs = swap(half_of(total, 1, ~upper).astype(jnp.bfloat16), "rep", step)
+        sent = half_of(total, 1, ~upper).astype(jnp.bfloat16)
+        if step == 1 and far > 2:
+            sent, mine = lax.optimization_barrier((sent, mine))
+            near, near_step = swap(mine, "grp", 2), 2
+        theirs = swap(sent, "rep", step)
         total = half_of(total, 1, upper) + theirs.astype(jnp.float32)
         step //= 2
 
-    step = far // 2
-    while step > 1:
+    steps = [far >> at for at in range(1, far.bit_length() - 1)] + [far] * (far > 1)
+    for step in steps:
         sent = total.astype(jnp.bfloat16)
-        flat = jnp.concatenate(jnp.split(sent, replicas, axis=0), axis=1)
-        answer = swap(jnp.concatenate([flat, mine], axis=0), "grp", step)
-        count = flat.shape[0]
-        theirs = jnp.concatenate(jnp.split(answer[:count], replicas, axis=1), axis=0)
-        total = sent.astype(jnp.float32) + theirs.astype(jnp.float32)
-        mine = gathered(mine, answer[count:], step)
-        step //= 2
-    theirs = swap(mine, "grp", 1)
-    scaled_mine, scaled_theirs = halves(ordered(parts))
-    grad_pre = matmul(scaled_mine, mine, ((0,), (0,)))
-    grad_pre += matmul(scaled_theirs, theirs, ((0,), (0,)))
-    grad_input = matmul(grad_pre.astype(jnp.bfloat16), weight, ((1,), (1,))).astype(jnp.bfloat16)
-    if far > 1:
-        sent = total.astype(jnp.bfloat16)
-        answer = swap(sent, "grp", far)
-        answer, grad_input = lax.optimization_barrier((answer, grad_input))
+        answer = swap(sent, "grp", step)
+        if near is not None:
+            sent, near = lax.optimization_barrier((sent, near))
+            mine, near = gathered(mine, near, near_step), None
+        if 2 * step < far:
+            near, near_step = swap(mine, "grp", 2 * step), 2 * step
+        if step == far:
+            theirs = swap(mine, "grp", 1)
+            scaled_mine, scaled_theirs = halves(ordered(parts))
+            grad_pre = matmul(scaled_mine, mine, ((0,), (0,)))
+            grad_pre += matmul(scaled_theirs, theirs, ((0,), (0,)))
+            grad_input = matmul(grad_pre.astype(jnp.bfloat16), weight, ((1,), (1,)))
+            answer, grad_input = lax.optimization_barrier((answer, grad_input.astype(jnp.bfloat16)))
         total = sent.astype(jnp.float32) + answer.astype(jnp.float32)
 
     total = total.astype(jnp.bfloat16)

time: 32.8 us -> 31.6 us (0.963)
  waiting for transfers between devices: 12.3 us -> 8.01 us
  starting transfers between devices: 14.4 us -> 17.6 us
    ppermute x9 -> x11, waiting for transfers between devices: 12.3 us -> 8.01 us  [swap(): return lax.ppermute(block, axis, [(at, at ^ step) for at in range(size)])]
    ppermute x9 -> x11, starting transfers between devices: 14.4 us -> 17.6 us  [swap(): return lax.ppermute(block, axis, [(at, at ^ step) for at in range(size)])]
  transfers between devices with their start and end apart: 9 -> 11, of which waited for: 7 -> 7; matrix products, arithmetic and copies ran while one was open for 7% -> 8% of each run, Pallas kernels for 1% -> 1%
where the time goes in v3:
time: 31.6 us; the launch traced here: 31.5 us
  starting transfers between devices  17.6 us (56%)
  waiting for transfers between devices  8.01 us (25%)
  matrix products  3.21 us (10%)
  Pallas kernels  1.49 us (5%)
  between operations  0.82 us (3%)
  other arithmetic  0.36 us (1%)
    ppermute x11, starting transfers between devices, swap(): return lax.ppermute(block, axis, [(at, at ^ step) for at in range(size)])  17.6 us
    ppermute x11, waiting for transfers between devices, swap(): return lax.ppermute(block, axis, [(at, at ^ step) for at in range(size)])  8.01 us
    dot_general x5, matrix products, matmul(): lax.dot_general(left, right, (contract, ((), ())), preferred_element_type...  3.21 us
    pallas_call x1, Pallas kernels, prepare(): pl.pallas_call(functools.partial(prepare_kernel, replicas), out_shape=[pl...  1.27 us
  transfers between devices with their start and end apart: 11, of which 7 were waited for; matrix products, arithmetic and copies ran while one was open for 8% of the time, Pallas kernels for 1%

profile of v3, /device:TPU:0, one launch (start us, length us, event | category | flops | bytes accessed | tf_op | source)
XLA Modules:
  0.0 31.5 jit_solution(12913734743838944464)
XLA Ops:
  0.6 0.0 copy-start
  0.6 0.0 copy-start.3
  0.7 0.0 copy-start.2
  0.7 0.0 copy-start.1
  0.7 1.3 %shard_map.86 = (bf16[128,512]{1,0:T(8,128)(2,1)S(1)}, bf16[128,512]{1,0:T(8,128)(2,1)S(1)}) custom-call(s32[128,1024]{1,0:T(8,128)} %counts.1, s32[128]{0:T(128)} %src_degree.1, s32[1024]{0:T(1024)} %dst_degree.1), custom_call_target="tpu_custom_call" | custom-call | tf_op jit(solution)/shard_map/pallas_call | solution.py:99
  2.0 3.0 %collective-permute-start = (bf16[128,512]{1,0:T(8,128)(2,1)S(1)}, bf16[128,512]{1,0:T(8,128)(2,1)S(1)}, u32[]{:S(2)}, u32[]{:S(2)}) collective-permute-start(bf16[128,512]{1,0:T(8,128)(2,1)S(1)} %get-tuple-element.16), channel_id=1, source_target_pairs={{0,1},{1,0},{2,3},{3,2},{4,5},{5,4},{6,7},{7,6},{8,9},{9,8},{10,11... | collective-permute-start | bytes 393224 | tf_op jit(solution)/shard_map/ppermute | solution.py:13
  5.0 0.0 copy-done.3
  5.0 0.0 copy-done.2
  5.0 2.7 %collective-permute-start.2 = (bf16[16,512]{1,0:T(8,128)(2,1)S(1)}, bf16[16,512]{1,0:T(8,128)(2,1)S(1)}, u32[]{:S(2)}, u32[]{:S(2)}) collective-permute-start(bf16[16,512]{1,0:T(8,128)(2,1)S(1)} %multiply_convert_fusion), channel_id=1, source_target_pairs={{0,16},{2,18},{4,20},{6,22},{8,24},{10,26},{12,28},{14,30},{16,0},... | collective-permute-start | bytes 49160 | tf_op jit(solution)/shard_map/ppermute | solution.py:13
  7.7 0.0 copy-done.1
  7.7 0.2 shard_map.87
  7.9 0.6 %collective-permute-done = bf16[128,512]{1,0:T(8,128)(2,1)S(1)} collective-permute-done((bf16[128,512]{1,0:T(8,128)(2,1)S(1)}, bf16[128,512]{1,0:T(8,128)(2,1)S(1)}, u32[]{:S(2)}, u32[]{:S(2)}) %collective-permute-start) | collective-permute-done | bytes 131104 | tf_op jit(solution)/shard_map/ppermute | solution.py:13
  8.5 0.2 fusion.2
  8.7 0.1 maximum_select_fusion
  8.8 0.1 collective-permute-start.1
  8.9 1.3 %collective-permute-done.1 = bf16[128,512]{1,0:T(8,128)(2,1)S(1)} collective-permute-done((bf16[128,512]{1,0:T(8,128)(2,1)S(1)}, bf16[128,512]{1,0:T(8,128)(2,1)S(1)}, u32[]{:S(2)}, u32[]{:S(2)}) %collective-permute-start.1) | collective-permute-done | bytes 131104 | tf_op jit(solution)/shard_map/ppermute | solution.py:13
  10.3 0.0 collective-permute-done.2
  10.3 1.8 %collective-permute-start.3 = (bf16[128,256]{1,0:T(8,128)(2,1)S(1)}, bf16[128,256]{1,0:T(8,128)(2,1)S(1)}, u32[]{:S(2)}, u32[]{:S(2)}) collective-permute-start(bf16[128,256]{1,0:T(8,128)(2,1)S(1)} %select_convert_fusion.1), channel_id=1, source_target_pairs={{0,1},{1,0},{2,3},{3,2},{4,5},{5,4},{6,7},{7,6},{8,9},{9,8},{10,11... | collective-permute-start | bytes 196616 | tf_op jit(solution)/shard_map/ppermute | solution.py:13
  12.1 0.1 maximum_select_fusion.1
  12.2 1.6 %collective-permute-start.4 = (bf16[32,512]{1,0:T(8,128)(2,1)S(1)}, bf16[32,512]{1,0:T(8,128)(2,1)S(1)}, u32[]{:S(2)}, u32[]{:S(2)}) collective-permute-start(bf16[32,512]{1,0:T(8,128)(2,1)S(1)} %bitcast.38), channel_id=1, source_target_pairs={{0,4},{2,6},{4,0},{6,2},{8,12},{10,14},{12,8},{14,10},{16,20},{18,... | collective-permute-start | bytes 98312 | tf_op jit(solution)/shard_map/ppermute | solution.py:13
  13.7 0.9 %collective-permute-done.3 = bf16[128,256]{1,0:T(8,128)(2,1)S(1)} collective-permute-done((bf16[128,256]{1,0:T(8,128)(2,1)S(1)}, bf16[128,256]{1,0:T(8,128)(2,1)S(1)}, u32[]{:S(2)}, u32[]{:S(2)}) %collective-permute-start.3) | collective-permute-done | bytes 65568 | tf_op jit(solution)/shard_map/ppermute | solution.py:13
  14.7 1.9 %collective-permute-start.5 = (bf16[128,256]{1,0:T(8,128)(2,1)S(1)}, bf16[128,256]{1,0:T(8,128)(2,1)S(1)}, u32[]{:S(2)}, u32[]{:S(2)}) collective-permute-start(bf16[128,256]{1,0:T(8,128)(2,1)S(1)} %add_convert_fusion.3), channel_id=1, source_target_pairs={{0,8},{2,10},{4,12},{6,14},{8,0},{10,2},{12,4},{14,6},{16,24},{18,... | collective-permute-start | bytes 196616 | tf_op jit(solution)/shard_map/ppermute | solution.py:13
  16.6 0.0 collective-permute-done.4
  16.6 2.4 %collective-permute-done.5 = bf16[128,256]{1,0:T(8,128)(2,1)S(1)} collective-permute-done((bf16[128,256]{1,0:T(8,128)(2,1)S(1)}, bf16[128,256]{1,0:T(8,128)(2,1)S(1)}, u32[]{:S(2)}, u32[]{:S(2)}) %collective-permute-start.5) | collective-permute-done | bytes 65568 | tf_op jit(solution)/shard_map/ppermute | solution.py:13
  19.0 1.8 %collective-permute-start.6 = (bf16[128,256]{1,0:T(8,128)(2,1)S(1)}, bf16[128,256]{1,0:T(8,128)(2,1)S(1)}, u32[]{:S(2)}, u32[]{:S(2)}) collective-permute-start(bf16[128,256]{1,0:T(8,128)(2,1)S(1)} %add_convert_fusion.2), channel_id=1, source_target_pairs={{0,4},{2,6},{4,0},{6,2},{8,12},{10,14},{12,8},{14,10},{16,20},{18,... | collective-permute-start | bytes 196616 | tf_op jit(solution)/shard_map/ppermute | solution.py:13
  20.8 1.6 %collective-permute-start.8 = (bf16[64,512]{1,0:T(8,128)(2,1)S(1)}, bf16[64,512]{1,0:T(8,128)(2,1)S(1)}, u32[]{:S(2)}, u32[]{:S(2)}) collective-permute-start(bf16[64,512]{1,0:T(8,128)(2,1)S(1)} %bitcast.35), channel_id=1, source_target_pairs={{0,8},{2,10},{4,12},{6,14},{8,0},{10,2},{12,4},{14,6},{16,24},{18,... | collective-permute-start | bytes 196616 | tf_op jit(solution)/shard_map/ppermute | solution.py:13
  22.5 0.9 %collective-permute-done.6 = bf16[128,256]{1,0:T(8,128)(2,1)S(1)} collective-permute-done((bf16[128,256]{1,0:T(8,128)(2,1)S(1)}, bf16[128,256]{1,0:T(8,128)(2,1)S(1)}, u32[]{:S(2)}, u32[]{:S(2)}) %collective-permute-start.6) | collective-permute-done | bytes 65568 | tf_op jit(solution)/shard_map/ppermute | solution.py:13
  23.4 2.9 %collective-permute-start.7 = (bf16[128,256]{1,0:T(8,128)(2,1)S(1)}, bf16[128,256]{1,0:T(8,128)(2,1)S(1)}, u32[]{:S(2)}, u32[]{:S(2)}) collective-permute-start(bf16[128,256]{1,0:T(8,128)(2,1)S(1)} %add_convert_fusion.1), channel_id=1, source_target_pairs={{0,16},{2,18},{4,20},{6,22},{8,24},{10,26},{12,28},{14,30},{16,0},... | collective-permute-start | bytes 196616 | tf_op jit(solution)/shard_map/ppermute | solution.py:13
  26.3 0.0 collective-permute-done.8
  26.3 0.1 collective-permute-start.9
  26.4 0.3 fusion.3
  26.7 1.0 %collective-permute-done.9 = bf16[128,512]{1,0:T(8,128)(2,1)S(1)} collective-permute-done((bf16[128,512]{1,0:T(8,128)(2,1)S(1)}, bf16[128,512]{1,0:T(8,128)(2,1)S(1)}, u32[]{:S(2)}, u32[]{:S(2)}) %collective-permute-start.9) | collective-permute-done | bytes 131104 | tf_op jit(solution)/shard_map/ppermute | solution.py:13
  27.7 0.0 copy-done
  27.7 1.4 %convolution_convert_fusion = bf16[512,512]{1,0:T(8,128)(2,1)} fusion(bf16[512,512]{1,0:T(8,128)(2,1)S(1)} %copy-done, f32[512,512]{1,0:T(8,128)S(1)} %fusion.3, bf16[128,512]{1,0:T(8,128)(2,1)S(1)} %bitcast.33, bf16[128,512]{1,0:T(8,128)(2,1)S(1)} %collective-permute-done.9), kind=kOutput, calls=%fused_computation.2 | convolution fusion | flops 336330752 | bytes 2359296 | tf_op jit(solution)/shard_map/dot_general | solution.py:44
  29.1 0.0 collective-permute-done.7
  29.1 0.2 collective-permute-start.10
  29.3 0.2 fusion.4
  29.6 0.9 %collective-permute-done.10 = bf16[128,256]{1,0:T(8,128)(2,1)S(1)} collective-permute-done((bf16[128,256]{1,0:T(8,128)(2,1)S(1)}, bf16[128,256]{1,0:T(8,128)(2,1)S(1)}, u32[]{:S(2)}, u32[]{:S(2)}) %collective-permute-start.10) | collective-permute-done | bytes 65568 | tf_op jit(solution)/shard_map/ppermute | solution.py:13
  30.4 1.0 %fusion.1 = f32[256,512]{1,0:T(8,128)} fusion(f32[256,512]{1,0:T(8,128)S(1)} %fusion.4, bf16[128,256]{1,0:T(8,128)(2,1)S(1)} %collective-permute-done.10, bf16[128,512]{1,0:T(8,128)(2,1)S(1)} %collective-permute-done.9), kind=kOutput, calls=%fused_computation.4 | convolution fusion | flops 33816576 | bytes 1245184 | tf_op jit(solution)/shard_map/dot_general | solution.py:44
  (14 shorter events, 0.3 us)
Async XLA Ops:
  0.6 27.1 %copy-start = (bf16[512,512]{1,0:T(8,128)(2,1)S(1)}, bf16[512,512]{1,0:T(8,128)(2,1)}, u32[]{:S(2)}) copy-start(bf16[512,512]{1,0:T(8,128)(2,1)} %param.13) | copy-start | bytes 1572868
  0.6 4.3 %copy-start.3 = (bf16[16,512]{1,0:T(8,128)(2,1)S(1)}, bf16[16,512]{1,0:T(8,128)(2,1)}, u32[]{:S(2)}) copy-start(bf16[16,512]{1,0:T(8,128)(2,1)} %param.7) | copy-start | bytes 49156
  0.7 4.3 %copy-start.2 = (s32[16,512]{1,0:T(8,128)S(1)}, s32[16,512]{1,0:T(8,128)}, u32[]{:S(2)}) copy-start(s32[16,512]{1,0:T(8,128)} %param.8) | copy-start | bytes 98308
  0.7 7.0 %copy-start.1 = (bf16[512,512]{1,0:T(8,128)(2,1)S(1)}, bf16[512,512]{1,0:T(8,128)(2,1)}, u32[]{:S(2)}) copy-start(bf16[512,512]{1,0:T(8,128)(2,1)} %inputs.1) | copy-start | bytes 1572868
  2.0 6.5 %collective-permute-start = (bf16[128,512]{1,0:T(8,128)(2,1)S(1)}, bf16[128,512]{1,0:T(8,128)(2,1)S(1)}, u32[]{:S(2)}, u32[]{:S(2)}) collective-permute-start(bf16[128,512]{1,0:T(8,128)(2,1)S(1)} %get-tuple-element.16), channel_id=1, source_target_pairs={{0,1},{1,0},{2,3},{3,2},{4,5},{5,4},{6,7},{7,6},{8,9},{9,8},{10,11... | collective-permute-start | bytes 393224 | tf_op jit(solution)/shard_map/ppermute | solution.py:13
  5.0 5.3 %collective-permute-start.2 = (bf16[16,512]{1,0:T(8,128)(2,1)S(1)}, bf16[16,512]{1,0:T(8,128)(2,1)S(1)}, u32[]{:S(2)}, u32[]{:S(2)}) collective-permute-start(bf16[16,512]{1,0:T(8,128)(2,1)S(1)} %multiply_convert_fusion), channel_id=1, source_target_pairs={{0,16},{2,18},{4,20},{6,22},{8,24},{10,26},{12,28},{14,30},{16,0},... | collective-permute-start | bytes 49160 | tf_op jit(solution)/shard_map/ppermute | solution.py:13
  8.8 1.4 %collective-permute-start.1 = (bf16[128,512]{1,0:T(8,128)(2,1)S(1)}, bf16[128,512]{1,0:T(8,128)(2,1)S(1)}, u32[]{:S(2)}, u32[]{:S(2)}) collective-permute-start(bf16[128,512]{1,0:T(8,128)(2,1)S(1)} %bitcast.37), channel_id=1, source_target_pairs={{0,2},{2,0},{4,6},{6,4},{8,10},{10,8},{12,14},{14,12},{16,18},{18,... | collective-permute-start | bytes 393224 | tf_op jit(solution)/shard_map/ppermute | solution.py:13
  10.3 4.3 %collective-permute-start.3 = (bf16[128,256]{1,0:T(8,128)(2,1)S(1)}, bf16[128,256]{1,0:T(8,128)(2,1)S(1)}, u32[]{:S(2)}, u32[]{:S(2)}) collective-permute-start(bf16[128,256]{1,0:T(8,128)(2,1)S(1)} %select_convert_fusion.1), channel_id=1, source_target_pairs={{0,1},{1,0},{2,3},{3,2},{4,5},{5,4},{6,7},{7,6},{8,9},{9,8},{10,11... | collective-permute-start | bytes 196616 | tf_op jit(solution)/shard_map/ppermute | solution.py:13
  12.2 4.4 %collective-permute-start.4 = (bf16[32,512]{1,0:T(8,128)(2,1)S(1)}, bf16[32,512]{1,0:T(8,128)(2,1)S(1)}, u32[]{:S(2)}, u32[]{:S(2)}) collective-permute-start(bf16[32,512]{1,0:T(8,128)(2,1)S(1)} %bitcast.38), channel_id=1, source_target_pairs={{0,4},{2,6},{4,0},{6,2},{8,12},{10,14},{12,8},{14,10},{16,20},{18,... | collective-permute-start | bytes 98312 | tf_op jit(solution)/shard_map/ppermute | solution.py:13
  14.7 4.3 %collective-permute-start.5 = (bf16[128,256]{1,0:T(8,128)(2,1)S(1)}, bf16[128,256]{1,0:T(8,128)(2,1)S(1)}, u32[]{:S(2)}, u32[]{:S(2)}) collective-permute-start(bf16[128,256]{1,0:T(8,128)(2,1)S(1)} %add_convert_fusion.3), channel_id=1, source_target_pairs={{0,8},{2,10},{4,12},{6,14},{8,0},{10,2},{12,4},{14,6},{16,24},{18,... | collective-permute-start | bytes 196616 | tf_op jit(solution)/shard_map/ppermute | solution.py:13
  19.0 4.3 %collective-permute-start.6 = (bf16[128,256]{1,0:T(8,128)(2,1)S(1)}, bf16[128,256]{1,0:T(8,128)(2,1)S(1)}, u32[]{:S(2)}, u32[]{:S(2)}) collective-permute-start(bf16[128,256]{1,0:T(8,128)(2,1)S(1)} %add_convert_fusion.2), channel_id=1, source_target_pairs={{0,4},{2,6},{4,0},{6,2},{8,12},{10,14},{12,8},{14,10},{16,20},{18,... | collective-permute-start | bytes 196616 | tf_op jit(solution)/shard_map/ppermute | solution.py:13
  20.8 5.4 %collective-permute-start.8 = (bf16[64,512]{1,0:T(8,128)(2,1)S(1)}, bf16[64,512]{1,0:T(8,128)(2,1)S(1)}, u32[]{:S(2)}, u32[]{:S(2)}) collective-permute-start(bf16[64,512]{1,0:T(8,128)(2,1)S(1)} %bitcast.35), channel_id=1, source_target_pairs={{0,8},{2,10},{4,12},{6,14},{8,0},{10,2},{12,4},{14,6},{16,24},{18,... | collective-permute-start | bytes 196616 | tf_op jit(solution)/shard_map/ppermute | solution.py:13
  23.4 5.7 %collective-permute-start.7 = (bf16[128,256]{1,0:T(8,128)(2,1)S(1)}, bf16[128,256]{1,0:T(8,128)(2,1)S(1)}, u32[]{:S(2)}, u32[]{:S(2)}) collective-permute-start(bf16[128,256]{1,0:T(8,128)(2,1)S(1)} %add_convert_fusion.1), channel_id=1, source_target_pairs={{0,16},{2,18},{4,20},{6,22},{8,24},{10,26},{12,28},{14,30},{16,0},... | collective-permute-start | bytes 196616 | tf_op jit(solution)/shard_map/ppermute | solution.py:13
  26.3 1.4 %collective-permute-start.9 = (bf16[128,512]{1,0:T(8,128)(2,1)S(1)}, bf16[128,512]{1,0:T(8,128)(2,1)S(1)}, u32[]{:S(2)}, u32[]{:S(2)}) collective-permute-start(bf16[128,512]{1,0:T(8,128)(2,1)S(1)} %bitcast.29), channel_id=1, source_target_pairs={{0,2},{2,0},{4,6},{6,4},{8,10},{10,8},{12,14},{14,12},{16,18},{18,... | collective-permute-start | bytes 393224 | tf_op jit(solution)/shard_map/ppermute | solution.py:13
  29.1 1.3 %collective-permute-start.10 = (bf16[128,256]{1,0:T(8,128)(2,1)S(1)}, bf16[128,256]{1,0:T(8,128)(2,1)S(1)}, u32[]{:S(2)}, u32[]{:S(2)}) collective-permute-start(bf16[128,256]{1,0:T(8,128)(2,1)S(1)} %add_convert_fusion), channel_id=1, source_target_pairs={{0,2},{2,0},{4,6},{6,4},{8,10},{10,8},{12,14},{14,12},{16,18},{18,... | collective-permute-start | bytes 196616 | tf_op jit(solution)/shard_map/ppermute | solution.py:13

commit v4 on v3

--- a/solution.py
+++ b/solution.py
@@ -11,6 +11,24 @@
 def swap(block, axis, step):
     size = lax.axis_size(axis)
     return lax.ppermute(block, axis, [(at, at ^ step) for at in range(size)])
+
+
+def parity(number):
+    count = 0
+    while number:
+        count ^= number & 1
+        number >>= 1
+    return count
+
+
+def crossed(block, group_steps, replica_step):
+    groups, replicas = lax.axis_size("grp"), lax.axis_size("rep")
+    pairs = []
+    for group in range(groups):
+        for replica in range(replicas):
+            step = group_steps[parity(group) ^ parity(replica)] | 1
+            pairs.append((group * replicas + replica, (group ^ step) * replicas + (replica ^ replica_step)))
+    return lax.ppermute(block, ("grp", "rep"), pairs)
 
 
 def bit_of(index, step):
@@ -135,6 +153,12 @@
     rows, width = inputs.shape
     block_rows = adjoint.shape[0]
     odd = bit_of(group, 1)
+    fold = group ^ replica
+    shift = 1 << groups.bit_length().bit_length()
+    while shift:
+        fold ^= fold >> shift
+        shift //= 2
+    upper_half = bit_of(fold, 1)
 
     *sent, own = prepare(counts, src_degree, dst_degree, replicas, rows)
     answers = [swap(part, "rep", step) for step, part in enumerate(sent, 1)]
@@ -142,17 +166,27 @@
     own_term = own_product(own, inputs)
     masked = (adjoint.astype(jnp.float32) * active.astype(jnp.float32)).astype(jnp.bfloat16)
 
+    far = groups // 2
+    others = [far >> at for at in range(1, far.bit_length() - 1)]
+    far_steps = [far] * (far > 1)
+    sum_steps = list(zip(others + far_steps, others[1:] + far_steps + others[:1]))
+    row_steps = far_steps + others[-1:] + others[:-1]
+
     def gathered(mine, theirs, step):
-        run = block_rows * (2 if 2 < step < groups // 2 else 1)
-        return in_order(
-            bit_of(group, step),
-            mine.reshape(-1, 1, run, width),
-            theirs.reshape(-1, 1, run, width),
-            1,
-        ).reshape(-1, width)
-
-    far = groups // 2
-    theirs = swap(masked, "grp", far) if far > 1 else masked
+        upper = bit_of(group, step)
+        return in_order(upper, mine[:, None], theirs[:, None], 1).reshape(-1, block_rows, width)
+
+    def arranged(mine):
+        split = mine.reshape([2] * len(row_steps) + [block_rows, width])
+        order = [row_steps.index(step) for step in far_steps + others]
+        return split.transpose(order + [len(order), len(order) + 1]).reshape(-1, width)
+
+    mine = masked.reshape(1, block_rows, width)
+    left = list(row_steps)
+    moving = None
+    if left:
+        moving = left.pop(0)
+        theirs = swap(mine, "grp", moving)
     answers, own_term = lax.optimization_barrier((answers, own_term))
     parts = [own] + answers
     terms = [own_term] + [matmul(part, inputs, ((1,), (0,))) for part in answers]
@@ -169,40 +203,46 @@
         pairs = block.reshape(groups // 2, 2, block_rows, block.shape[1])
         even = pairs[:, 0].reshape(-1, block.shape[1])
         uneven = pairs[:, 1].reshape(-1, block.shape[1])
-        return jnp.where(odd, uneven, even), jnp.where(odd, even, uneven)
-
-    kept, sent = halves(ordered(terms))
+        return even, uneven
+
+    def chosen(upper, pair):
+        return jnp.where(upper, pair[1], pair[0])
+
+    terms = halves(ordered(terms))
+    kept, sent = chosen(upper_half, terms), chosen(~upper_half, terms)
     total = kept + swap(sent.astype(jnp.bfloat16), "grp", 1).astype(jnp.float32)
 
-    total, theirs = lax.optimization_barrier((total, theirs))
-    mine = gathered(masked, theirs, far) if far > 1 else masked
-
-    near = None
+    if moving:
+        total, theirs = lax.optimization_barrier((total, theirs))
+        mine, moving = gathered(mine, theirs, moving), None
+
     step = replicas // 2
     while step:
         upper = bit_of(replica, step)
         sent = half_of(total, 1, ~upper).astype(jnp.bfloat16)
-        if step == 1 and far > 2:
+        if step == 1 and left:
             sent, mine = lax.optimization_barrier((sent, mine))
-            near, near_step = swap(mine, "grp", 2), 2
-        theirs = swap(sent, "rep", step)
+            moving = left.pop(0)
+            row_theirs = swap(mine, "grp", moving)
+        theirs = crossed(sent, (0, 0), step)
         total = half_of(total, 1, upper) + theirs.astype(jnp.float32)
         step //= 2
 
-    steps = [far >> at for at in range(1, far.bit_length() - 1)] + [far] * (far > 1)
-    for step in steps:
+    for at, steps in enumerate(sum_steps):
         sent = total.astype(jnp.bfloat16)
-        answer = swap(sent, "grp", step)
-        if near is not None:
-            sent, near = lax.optimization_barrier((sent, near))
-            mine, near = gathered(mine, near, near_step), None
-        if 2 * step < far:
-            near, near_step = swap(mine, "grp", 2 * step), 2 * step
-        if step == far:
+        answer = crossed(sent, steps, 0)
+        if moving:
+            sent, row_theirs = lax.optimization_barrier((sent, row_theirs))
+            mine, moving = gathered(mine, row_theirs, moving), None
+        if left and at:
+            moving = left.pop(0)
+            row_theirs = swap(mine, "grp", moving)
+        if at == len(sum_steps) - 1:
+            mine = arranged(mine)
             theirs = swap(mine, "grp", 1)
-            scaled_mine, scaled_theirs = halves(ordered(parts))
-            grad_pre = matmul(scaled_mine, mine, ((0,), (0,)))
-            grad_pre += matmul(scaled_theirs, theirs, ((0,), (0,)))
+            scaled = halves(ordered(parts))
+            grad_pre = matmul(chosen(odd, scaled), mine, ((0,), (0,)))
+            grad_pre += matmul(chosen(~odd, scaled), theirs, ((0,), (0,)))
             grad_input = matmul(grad_pre.astype(jnp.bfloat16), weight, ((1,), (1,)))
             answer, grad_input = lax.optimization_barrier((answer, grad_input.astype(jnp.bfloat16)))
         total = sent.astype(jnp.float32) + answer.astype(jnp.float32)
@@ -210,7 +250,8 @@
     total = total.astype(jnp.bfloat16)
     other = swap(total, "grp", 1)
     vertex_total = rows * groups * replicas
-    grad_weight = matmul(total, mine, ((0,), (0,))) + matmul(other, theirs, ((0,), (0,)))
+    rows_of = jnp.where(odd ^ upper_half, theirs, mine), jnp.where(odd ^ upper_half, mine, theirs)
+    grad_weight = matmul(total, rows_of[0], ((0,), (0,))) + matmul(other, rows_of[1], ((0,), (0,)))
     return (grad_input, grad_weight / vertex_total)
 
 

time: 31.6 us -> 30.6 us (0.968)
  starting transfers between devices: 17.6 us -> 16.7 us
    ppermute x11 -> x7, starting transfers between devices: 17.6 us -> 9.17 us  [swap(): return lax.ppermute(block, axis, [(at, at ^ step) for at in range(size)])]
    ppermute x0 -> x4, starting transfers between devices: none -> 7.54 us  [crossed(): return lax.ppermute(block, ('grp', 'rep'), pairs)]
    ppermute x11 -> x7, waiting for transfers between devices: 8.01 us -> 3.95 us  [swap(): return lax.ppermute(block, axis, [(at, at ^ step) for at in range(size)])]
    ppermute x0 -> x4, waiting for transfers between devices: none -> 3.85 us  [crossed(): return lax.ppermute(block, ('grp', 'rep'), pairs)]
  transfers between devices with their start and end apart: 11 -> 11, of which waited for: 7 -> 7; matrix products, arithmetic and copies ran while one was open for 8% -> 7% of each run, Pallas kernels for 1% -> 1%
where the time goes in v4:
time: 30.6 us; the launch traced here: 30.5 us
  starting transfers between devices  16.7 us (55%)
  waiting for transfers between devices  7.8 us (25%)
  matrix products  3.23 us (11%)
  Pallas kernels  1.49 us (5%)
  between operations  0.82 us (3%)
  other arithmetic  0.38 us (1%)
    ppermute x7, starting transfers between devices, swap(): return lax.ppermute(block, axis, [(at, at ^ step) for at in range(size)])  9.17 us
    ppermute x4, starting transfers between devices, crossed(): return lax.ppermute(block, ('grp', 'rep'), pairs)  7.54 us
    ppermute x7, waiting for transfers between devices, swap(): return lax.ppermute(block, axis, [(at, at ^ step) for at in range(size)])  3.95 us
    ppermute x4, waiting for transfers between devices, crossed(): return lax.ppermute(block, ('grp', 'rep'), pairs)  3.85 us
    dot_general x5, matrix products, matmul(): lax.dot_general(left, right, (contract, ((), ())), preferred_element_type...  3.23 us
    pallas_call x1, Pallas kernels, prepare(): pl.pallas_call(functools.partial(prepare_kernel, replicas), out_shape=[pl...  1.27 us
  transfers between devices with their start and end apart: 11, of which 7 were waited for; matrix products, arithmetic and copies ran while one was open for 7% of the time, Pallas kernels for 1%

profile of v4, /device:TPU:0, one launch (start us, length us, event | category | flops | bytes accessed | tf_op | source)
XLA Modules:
  0.0 30.5 jit_solution(1918591333600928341)
XLA Ops:
  0.6 0.0 copy-start
  0.6 0.0 copy-start.3
  0.7 0.0 copy-start.2
  0.7 0.0 copy-start.1
  0.7 1.3 %shard_map.86 = (bf16[128,512]{1,0:T(8,128)(2,1)S(1)}, bf16[128,512]{1,0:T(8,128)(2,1)S(1)}) custom-call(s32[128,1024]{1,0:T(8,128)} %counts.1, s32[128]{0:T(128)} %src_degree.1, s32[1024]{0:T(1024)} %dst_degree.1), custom_call_target="tpu_custom_call" | custom-call | tf_op jit(solution)/shard_map/pallas_call | solution.py:117
  2.0 3.0 %collective-permute-start = (bf16[128,512]{1,0:T(8,128)(2,1)S(1)}, bf16[128,512]{1,0:T(8,128)(2,1)S(1)}, u32[]{:S(2)}, u32[]{:S(2)}) collective-permute-start(bf16[128,512]{1,0:T(8,128)(2,1)S(1)} %get-tuple-element.16), channel_id=1, source_target_pairs={{0,1},{1,0},{2,3},{3,2},{4,5},{5,4},{6,7},{7,6},{8,9},{9,8},{10,11... | collective-permute-start | bytes 393224 | tf_op jit(solution)/shard_map/ppermute | solution.py:13
  5.0 0.0 copy-done.3
  5.0 0.0 copy-done.2
  5.0 2.7 %collective-permute-start.2 = (bf16[1,16,512]{2,1,0:T(8,128)(2,1)S(1)}, bf16[1,16,512]{2,1,0:T(8,128)(2,1)S(1)}, u32[]{:S(2)}, u32[]{:S(2)}) collective-permute-start(bf16[1,16,512]{2,1,0:T(8,128)(2,1)S(1)} %fusion.8), channel_id=1, source_target_pairs={{0,16},{2,18},{4,20},{6,22},{8,24},{10,26},{12,28},{14,30},{16,0},... | collective-permute-start | bytes 49160 | tf_op jit(solution)/shard_map/ppermute | solution.py:13
  7.7 0.0 copy-done.1
  7.7 0.2 shard_map.87
  7.9 0.6 %collective-permute-done = bf16[128,512]{1,0:T(8,128)(2,1)S(1)} collective-permute-done((bf16[128,512]{1,0:T(8,128)(2,1)S(1)}, bf16[128,512]{1,0:T(8,128)(2,1)S(1)}, u32[]{:S(2)}, u32[]{:S(2)}) %collective-permute-start) | collective-permute-done | bytes 131104 | tf_op jit(solution)/shard_map/ppermute | solution.py:13
  8.5 0.2 fusion.9
  8.7 0.1 maximum_select_fusion
  8.8 0.1 collective-permute-start.1
  8.9 0.1 maximum_select_fusion.1
  9.0 1.2 %collective-permute-done.1 = bf16[128,512]{1,0:T(8,128)(2,1)S(1)} collective-permute-done((bf16[128,512]{1,0:T(8,128)(2,1)S(1)}, bf16[128,512]{1,0:T(8,128)(2,1)S(1)}, u32[]{:S(2)}, u32[]{:S(2)}) %collective-permute-start.1) | collective-permute-done | bytes 131104 | tf_op jit(solution)/shard_map/ppermute | solution.py:13
  10.3 0.0 collective-permute-done.2
  10.3 1.6 %collective-permute-start.3 = (bf16[128,256]{1,0:T(8,128)(2,1)S(1)}, bf16[128,256]{1,0:T(8,128)(2,1)S(1)}, u32[]{:S(2)}, u32[]{:S(2)}) collective-permute-start(bf16[128,256]{1,0:T(8,128)(2,1)S(1)} %select_convert_fusion.1), channel_id=1, source_target_pairs={{0,3},{1,2},{2,1},{3,0},{4,7},{5,6},{6,5},{7,4},{8,11},{9,10},{10,... | collective-permute-start | bytes 196616 | tf_op jit(solution)/shard_map/ppermute | solution.py:31
  11.9 1.6 %collective-permute-start.4 = (bf16[2,16,512]{2,1,0:T(8,128)(2,1)S(1)}, bf16[2,16,512]{2,1,0:T(8,128)(2,1)S(1)}, u32[]{:S(2)}, u32[]{:S(2)}) collective-permute-start(bf16[2,16,512]{2,1,0:T(8,128)(2,1)S(1)} %maximum_select_fusion.5), channel_id=1, source_target_pairs={{0,4},{2,6},{4,0},{6,2},{8,12},{10,14},{12,8},{14,10},{16,20},{18,... | collective-permute-start | bytes 98312 | tf_op jit(solution)/shard_map/ppermute | solution.py:13
  13.5 1.0 %collective-permute-done.3 = bf16[128,256]{1,0:T(8,128)(2,1)S(1)} collective-permute-done((bf16[128,256]{1,0:T(8,128)(2,1)S(1)}, bf16[128,256]{1,0:T(8,128)(2,1)S(1)}, u32[]{:S(2)}, u32[]{:S(2)}) %collective-permute-start.3) | collective-permute-done | bytes 65568 | tf_op jit(solution)/shard_map/ppermute | solution.py:31
  14.5 1.6 %collective-permute-start.5 = (bf16[128,256]{1,0:T(8,128)(2,1)S(1)}, bf16[128,256]{1,0:T(8,128)(2,1)S(1)}, u32[]{:S(2)}, u32[]{:S(2)}) collective-permute-start(bf16[128,256]{1,0:T(8,128)(2,1)S(1)} %add_convert_fusion.3), channel_id=1, source_target_pairs={{0,10},{1,7},{2,4},{3,9},{4,2},{5,15},{6,12},{7,1},{8,14},{9,3},{1... | collective-permute-start | bytes 196616 | tf_op jit(solution)/shard_map/ppermute | solution.py:31
  16.1 0.0 collective-permute-done.4
  16.1 1.6 %collective-permute-start.8 = (bf16[4,16,512]{2,1,0:T(8,128)(2,1)S(1)}, bf16[4,16,512]{2,1,0:T(8,128)(2,1)S(1)}, u32[]{:S(2)}, u32[]{:S(2)}) collective-permute-start(bf16[4,16,512]{2,1,0:T(8,128)(2,1)S(1)} %bitcast.41), channel_id=1, source_target_pairs={{0,8},{2,10},{4,12},{6,14},{8,0},{10,2},{12,4},{14,6},{16,24},{18,... | collective-permute-start | bytes 196616 | tf_op jit(solution)/shard_map/ppermute | solution.py:13
  17.7 0.6 %collective-permute-done.5 = bf16[128,256]{1,0:T(8,128)(2,1)S(1)} collective-permute-done((bf16[128,256]{1,0:T(8,128)(2,1)S(1)}, bf16[128,256]{1,0:T(8,128)(2,1)S(1)}, u32[]{:S(2)}, u32[]{:S(2)}) %collective-permute-start.5) | collective-permute-done | bytes 65568 | tf_op jit(solution)/shard_map/ppermute | solution.py:31
  18.3 1.5 %collective-permute-start.6 = (bf16[128,256]{1,0:T(8,128)(2,1)S(1)}, bf16[128,256]{1,0:T(8,128)(2,1)S(1)}, u32[]{:S(2)}, u32[]{:S(2)}) collective-permute-start(bf16[128,256]{1,0:T(8,128)(2,1)S(1)} %add_convert_fusion.2), channel_id=1, source_target_pairs={{0,6},{1,19},{2,16},{3,5},{4,22},{5,3},{6,0},{7,21},{8,26},{9,15},... | collective-permute-start | bytes 196616 | tf_op jit(solution)/shard_map/ppermute | solution.py:31
  19.8 2.3 %collective-permute-done.6 = bf16[128,256]{1,0:T(8,128)(2,1)S(1)} collective-permute-done((bf16[128,256]{1,0:T(8,128)(2,1)S(1)}, bf16[128,256]{1,0:T(8,128)(2,1)S(1)}, u32[]{:S(2)}, u32[]{:S(2)}) %collective-permute-start.6) | collective-permute-done | bytes 65568 | tf_op jit(solution)/shard_map/ppermute | solution.py:31
  22.1 2.9 %collective-permute-start.7 = (bf16[128,256]{1,0:T(8,128)(2,1)S(1)}, bf16[128,256]{1,0:T(8,128)(2,1)S(1)}, u32[]{:S(2)}, u32[]{:S(2)}) collective-permute-start(bf16[128,256]{1,0:T(8,128)(2,1)S(1)} %add_convert_fusion.1), channel_id=1, source_target_pairs={{0,18},{1,11},{2,8},{3,17},{4,14},{5,23},{6,20},{7,13},{8,2},{9,27... | collective-permute-start | bytes 196616 | tf_op jit(solution)/shard_map/ppermute | solution.py:31
  25.0 0.0 collective-permute-done.8
  25.0 0.1 collective-permute-start.9
  25.1 0.3 %fusion.10 = f32[512,512]{1,0:T(8,128)S(1)} fusion(bf16[128,512]{1,0:T(8,128)(2,1)S(1)} %bitcast.35, bf16[128,512]{1,0:T(8,128)(2,1)S(1)} %bitcast.30), kind=kOutput, calls=%fused_computation.30 | convolution fusion | flops 67108864 | bytes 1310720 | tf_op jit(solution)/shard_map/dot_general | solution.py:62
  25.4 1.0 %collective-permute-done.9 = bf16[128,512]{1,0:T(8,128)(2,1)S(1)} collective-permute-done((bf16[128,512]{1,0:T(8,128)(2,1)S(1)}, bf16[128,512]{1,0:T(8,128)(2,1)S(1)}, u32[]{:S(2)}, u32[]{:S(2)}) %collective-permute-start.9) | collective-permute-done | bytes 131104 | tf_op jit(solution)/shard_map/ppermute | solution.py:13
  26.4 0.0 copy-done
  26.4 1.4 %convolution_convert_fusion = bf16[512,512]{1,0:T(8,128)(2,1)} fusion(bf16[512,512]{1,0:T(8,128)(2,1)S(1)} %copy-done, f32[512,512]{1,0:T(8,128)S(1)} %fusion.10, bf16[128,512]{1,0:T(8,128)(2,1)S(1)} %bitcast.34, bf16[128,512]{1,0:T(8,128)(2,1)S(1)} %collective-permute-done.9), kind=kOutput, calls=%fused_computation.2 | convolution fusion | flops 336330752 | bytes 2359296 | tf_op jit(solution)/shard_map/dot_general | solution.py:62
  27.8 0.0 collective-permute-done.7
  27.8 0.2 collective-permute-start.10
  28.1 1.1 %collective-permute-done.10 = bf16[128,256]{1,0:T(8,128)(2,1)S(1)} collective-permute-done((bf16[128,256]{1,0:T(8,128)(2,1)S(1)}, bf16[128,256]{1,0:T(8,128)(2,1)S(1)}, u32[]{:S(2)}, u32[]{:S(2)}) %collective-permute-start.10) | collective-permute-done | bytes 65568 | tf_op jit(solution)/shard_map/ppermute | solution.py:13
  29.2 0.2 fusion.3
  29.4 1.0 %fusion.1 = f32[256,512]{1,0:T(8,128)} fusion(f32[256,512]{1,0:T(8,128)S(1)} %fusion.3, bf16[128,256]{1,0:T(8,128)(2,1)S(1)} %add_convert_fusion, bf16[128,512]{1,0:T(8,128)(2,1)S(1)} %collective-permute-done.9, bf16[128,512]{1,0:T(8,128)(2,1)S(1)} %bitcast.32, pred[]{:T(512)S(6)} %xor.24), kind=kOutput, calls=%fused_computation.4 | convolution fusion | flops 33882112 | bytes 1376257 | tf_op jit(solution)/shard_map/dot_general | solution.py:62
  (15 shorter events, 0.3 us)
Async XLA Ops:
  0.6 25.8 %copy-start = (bf16[512,512]{1,0:T(8,128)(2,1)S(1)}, bf16[512,512]{1,0:T(8,128)(2,1)}, u32[]{:S(2)}) copy-start(bf16[512,512]{1,0:T(8,128)(2,1)} %param.13) | copy-start | bytes 1572868
  0.6 4.3 %copy-start.3 = (bf16[16,512]{1,0:T(8,128)(2,1)S(1)}, bf16[16,512]{1,0:T(8,128)(2,1)}, u32[]{:S(2)}) copy-start(bf16[16,512]{1,0:T(8,128)(2,1)} %param.7) | copy-start | bytes 49156
  0.7 4.3 %copy-start.2 = (s32[16,512]{1,0:T(8,128)S(1)}, s32[16,512]{1,0:T(8,128)}, u32[]{:S(2)}) copy-start(s32[16,512]{1,0:T(8,128)} %param.8) | copy-start | bytes 98308
  0.7 7.0 %copy-start.1 = (bf16[512,512]{1,0:T(8,128)(2,1)S(1)}, bf16[512,512]{1,0:T(8,128)(2,1)}, u32[]{:S(2)}) copy-start(bf16[512,512]{1,0:T(8,128)(2,1)} %inputs.1) | copy-start | bytes 1572868
  2.0 6.5 %collective-permute-start = (bf16[128,512]{1,0:T(8,128)(2,1)S(1)}, bf16[128,512]{1,0:T(8,128)(2,1)S(1)}, u32[]{:S(2)}, u32[]{:S(2)}) collective-permute-start(bf16[128,512]{1,0:T(8,128)(2,1)S(1)} %get-tuple-element.16), channel_id=1, source_target_pairs={{0,1},{1,0},{2,3},{3,2},{4,5},{5,4},{6,7},{7,6},{8,9},{9,8},{10,11... | collective-permute-start | bytes 393224 | tf_op jit(solution)/shard_map/ppermute | solution.py:13
  5.0 5.3 %collective-permute-start.2 = (bf16[1,16,512]{2,1,0:T(8,128)(2,1)S(1)}, bf16[1,16,512]{2,1,0:T(8,128)(2,1)S(1)}, u32[]{:S(2)}, u32[]{:S(2)}) collective-permute-start(bf16[1,16,512]{2,1,0:T(8,128)(2,1)S(1)} %fusion.8), channel_id=1, source_target_pairs={{0,16},{2,18},{4,20},{6,22},{8,24},{10,26},{12,28},{14,30},{16,0},... | collective-permute-start | bytes 49160 | tf_op jit(solution)/shard_map/ppermute | solution.py:13
  8.8 1.4 %collective-permute-start.1 = (bf16[128,512]{1,0:T(8,128)(2,1)S(1)}, bf16[128,512]{1,0:T(8,128)(2,1)S(1)}, u32[]{:S(2)}, u32[]{:S(2)}) collective-permute-start(bf16[128,512]{1,0:T(8,128)(2,1)S(1)} %bitcast.38), channel_id=1, source_target_pairs={{0,2},{2,0},{4,6},{6,4},{8,10},{10,8},{12,14},{14,12},{16,18},{18,... | collective-permute-start | bytes 393224 | tf_op jit(solution)/shard_map/ppermute | solution.py:13
  10.3 4.1 %collective-permute-start.3 = (bf16[128,256]{1,0:T(8,128)(2,1)S(1)}, bf16[128,256]{1,0:T(8,128)(2,1)S(1)}, u32[]{:S(2)}, u32[]{:S(2)}) collective-permute-start(bf16[128,256]{1,0:T(8,128)(2,1)S(1)} %select_convert_fusion.1), channel_id=1, source_target_pairs={{0,3},{1,2},{2,1},{3,0},{4,7},{5,6},{6,5},{7,4},{8,11},{9,10},{10,... | collective-permute-start | bytes 196616 | tf_op jit(solution)/shard_map/ppermute | solution.py:31
  11.9 4.2 %collective-permute-start.4 = (bf16[2,16,512]{2,1,0:T(8,128)(2,1)S(1)}, bf16[2,16,512]{2,1,0:T(8,128)(2,1)S(1)}, u32[]{:S(2)}, u32[]{:S(2)}) collective-permute-start(bf16[2,16,512]{2,1,0:T(8,128)(2,1)S(1)} %maximum_select_fusion.5), channel_id=1, source_target_pairs={{0,4},{2,6},{4,0},{6,2},{8,12},{10,14},{12,8},{14,10},{16,20},{18,... | collective-permute-start | bytes 98312 | tf_op jit(solution)/shard_map/ppermute | solution.py:13
  14.5 3.8 %collective-permute-start.5 = (bf16[128,256]{1,0:T(8,128)(2,1)S(1)}, bf16[128,256]{1,0:T(8,128)(2,1)S(1)}, u32[]{:S(2)}, u32[]{:S(2)}) collective-permute-start(bf16[128,256]{1,0:T(8,128)(2,1)S(1)} %add_convert_fusion.3), channel_id=1, source_target_pairs={{0,10},{1,7},{2,4},{3,9},{4,2},{5,15},{6,12},{7,1},{8,14},{9,3},{1... | collective-permute-start | bytes 196616 | tf_op jit(solution)/shard_map/ppermute | solution.py:31
  16.1 8.9 %collective-permute-start.8 = (bf16[4,16,512]{2,1,0:T(8,128)(2,1)S(1)}, bf16[4,16,512]{2,1,0:T(8,128)(2,1)S(1)}, u32[]{:S(2)}, u32[]{:S(2)}) collective-permute-start(bf16[4,16,512]{2,1,0:T(8,128)(2,1)S(1)} %bitcast.41), channel_id=1, source_target_pairs={{0,8},{2,10},{4,12},{6,14},{8,0},{10,2},{12,4},{14,6},{16,24},{18,... | collective-permute-start | bytes 196616 | tf_op jit(solution)/shard_map/ppermute | solution.py:13
  18.3 3.8 %collective-permute-start.6 = (bf16[128,256]{1,0:T(8,128)(2,1)S(1)}, bf16[128,256]{1,0:T(8,128)(2,1)S(1)}, u32[]{:S(2)}, u32[]{:S(2)}) collective-permute-start(bf16[128,256]{1,0:T(8,128)(2,1)S(1)} %add_convert_fusion.2), channel_id=1, source_target_pairs={{0,6},{1,19},{2,16},{3,5},{4,22},{5,3},{6,0},{7,21},{8,26},{9,15},... | collective-permute-start | bytes 196616 | tf_op jit(solution)/shard_map/ppermute | solution.py:31
  22.1 5.7 %collective-permute-start.7 = (bf16[128,256]{1,0:T(8,128)(2,1)S(1)}, bf16[128,256]{1,0:T(8,128)(2,1)S(1)}, u32[]{:S(2)}, u32[]{:S(2)}) collective-permute-start(bf16[128,256]{1,0:T(8,128)(2,1)S(1)} %add_convert_fusion.1), channel_id=1, source_target_pairs={{0,18},{1,11},{2,8},{3,17},{4,14},{5,23},{6,20},{7,13},{8,2},{9,27... | collective-permute-start | bytes 196616 | tf_op jit(solution)/shard_map/ppermute | solution.py:31
  25.0 1.4 %collective-permute-start.9 = (bf16[128,512]{1,0:T(8,128)(2,1)S(1)}, bf16[128,512]{1,0:T(8,128)(2,1)S(1)}, u32[]{:S(2)}, u32[]{:S(2)}) collective-permute-start(bf16[128,512]{1,0:T(8,128)(2,1)S(1)} %bitcast.29), channel_id=1, source_target_pairs={{0,2},{2,0},{4,6},{6,4},{8,10},{10,8},{12,14},{14,12},{16,18},{18,... | collective-permute-start | bytes 393224 | tf_op jit(solution)/shard_map/ppermute | solution.py:13
  27.8 1.3 %collective-permute-start.10 = (bf16[128,256]{1,0:T(8,128)(2,1)S(1)}, bf16[128,256]{1,0:T(8,128)(2,1)S(1)}, u32[]{:S(2)}, u32[]{:S(2)}) collective-permute-start(bf16[128,256]{1,0:T(8,128)(2,1)S(1)} %add_convert_fusion), channel_id=1, source_target_pairs={{0,2},{2,0},{4,6},{6,4},{8,10},{10,8},{12,14},{14,12},{16,18},{18,... | collective-permute-start | bytes 196616 | tf_op jit(solution)/shard_map/ppermute | solution.py:13

commit v5 on v4

--- a/solution.py
+++ b/solution.py
@@ -147,6 +147,34 @@
     )(*[pltpu.with_memory_space_constraint(block, pltpu.VMEM) for block in (own, inputs)])
 
 
+def final_kernel(scale, mine, other, rows, out, parts, sems):
+    count, cols, _ = parts.shape
+    copies = []
+    for at in range(count):
+        piece = slice(at * cols, (at + 1) * cols)
+        product = matmul(other[:, piece], rows[...], ((0,), (0,)))
+        parts[at] = (mine[piece, :] + product) * scale
+        copies.append(pltpu.make_async_copy(parts.at[at], out.at[piece, :], sems.at[at]))
+        copies[at].start()
+    for copy in copies:
+        copy.wait()
+
+
+def final_product(mine, other, rows, scale):
+    cols = min(other.shape[1], 128)
+    count = other.shape[1] // cols
+    return pl.pallas_call(
+        functools.partial(final_kernel, scale),
+        out_shape=jax.ShapeDtypeStruct(mine.shape, jnp.float32),
+        in_specs=[pl.BlockSpec(memory_space=pltpu.VMEM)] * 3,
+        out_specs=pl.BlockSpec(memory_space=pl.ANY),
+        scratch_shapes=[
+            pltpu.VMEM((count, cols, mine.shape[1]), jnp.float32),
+            pltpu.SemaphoreType.DMA((count,)),
+        ],
+    )(*[pltpu.with_memory_space_constraint(block, pltpu.VMEM) for block in (mine, other, rows)])
+
+
 def body(adjoint, active, counts, src_degree, dst_degree, inputs, weight):
     groups, replicas = lax.axis_size("grp"), lax.axis_size("rep")
     group, replica = lax.axis_index("grp"), lax.axis_index("rep")
@@ -228,18 +256,22 @@
         total = half_of(total, 1, upper) + theirs.astype(jnp.float32)
         step //= 2
 
+    theirs = None
     for at, steps in enumerate(sum_steps):
         sent = total.astype(jnp.bfloat16)
         answer = crossed(sent, steps, 0)
         if moving:
             sent, row_theirs = lax.optimization_barrier((sent, row_theirs))
             mine, moving = gathered(mine, row_theirs, moving), None
-        if left and at:
+        if left:
             moving = left.pop(0)
             row_theirs = swap(mine, "grp", moving)
-        if at == len(sum_steps) - 1:
+        elif theirs is None:
             mine = arranged(mine)
             theirs = swap(mine, "grp", 1)
+            if at < len(sum_steps) - 1:
+                answer, mine = lax.optimization_barrier((answer, mine))
+        if at == len(sum_steps) - 1:
             scaled = halves(ordered(parts))
             grad_pre = matmul(chosen(odd, scaled), mine, ((0,), (0,)))
             grad_pre += matmul(chosen(~odd, scaled), theirs, ((0,), (0,)))
@@ -250,9 +282,11 @@
     total = total.astype(jnp.bfloat16)
     other = swap(total, "grp", 1)
     vertex_total = rows * groups * replicas
-    rows_of = jnp.where(odd ^ upper_half, theirs, mine), jnp.where(odd ^ upper_half, mine, theirs)
-    grad_weight = matmul(total, rows_of[0], ((0,), (0,))) + matmul(other, rows_of[1], ((0,), (0,)))
-    return (grad_input, grad_weight / vertex_total)
+    swapped = odd ^ upper_half
+    product = matmul(total, jnp.where(swapped, theirs, mine), ((0,), (0,)))
+    rest = jnp.where(swapped, mine, theirs)
+    other, product, rest = lax.optimization_barrier((other, product, rest))
+    return (grad_input, final_product(product, other, rest, 1.0 / vertex_total))
 
 
 def solution(mesh):

time: 30.6 us -> 29.7 us (0.971)
  waiting for transfers between devices: 7.8 us -> 5.67 us
  starting transfers between devices: 16.7 us -> 17.8 us
  matrix products: 3.23 us -> 2.17 us
  Pallas kernels: 1.49 us -> 2.52 us
    ppermute x4, waiting for transfers between devices: 3.85 us -> 2.55 us  [crossed(): return lax.ppermute(block, ('grp', 'rep'), pairs)]
    ppermute x7, starting transfers between devices: 9.17 us -> 10.3 us  [swap(): return lax.ppermute(block, axis, [(at, at ^ step) for at in range(size)])]
    dot_general x5 -> x4, matrix products: 3.23 us -> 2.17 us  [matmul(): lax.dot_general(left, right, (contract, ((), ())), preferred_element_type...]
    pallas_call x0 -> x1, Pallas kernels: none -> 1.02 us  [final_product(): pl.pallas_call(functools.partial(final_kernel, scale), out_shape=jax.Shap...]
    ppermute x7, waiting for transfers between devices: 3.95 us -> 3.12 us  [swap(): return lax.ppermute(block, axis, [(at, at ^ step) for at in range(size)])]
  transfers between devices with their start and end apart: 11 -> 11, of which waited for: 7 -> 8; matrix products, arithmetic and copies ran while one was open for 7% -> 9% of each run, Pallas kernels for 1% -> 1%
where the time goes in v5:
time: 29.7 us; the launch traced here: 29.4 us
  starting transfers between devices  17.8 us (60%)
  waiting for transfers between devices  5.67 us (19%)
  Pallas kernels  2.52 us (8%)
  matrix products  2.17 us (7%)
  between operations  0.82 us (3%)
  other arithmetic  0.41 us (1%)
    ppermute x7, starting transfers between devices, swap(): return lax.ppermute(block, axis, [(at, at ^ step) for at in range(size)])  10.3 us
    ppermute x4, starting transfers between devices, crossed(): return lax.ppermute(block, ('grp', 'rep'), pairs)  7.54 us
    ppermute x7, waiting for transfers between devices, swap(): return lax.ppermute(block, axis, [(at, at ^ step) for at in range(size)])  3.12 us
    ppermute x4, waiting for transfers between devices, crossed(): return lax.ppermute(block, ('grp', 'rep'), pairs)  2.55 us
    dot_general x4, matrix products, matmul(): lax.dot_general(left, right, (contract, ((), ())), preferred_element_type...  2.17 us
    pallas_call x1, Pallas kernels, prepare(): pl.pallas_call(functools.partial(prepare_kernel, replicas), out_shape=[pl...  1.27 us
    pallas_call x1, Pallas kernels, final_product(): pl.pallas_call(functools.partial(final_kernel, scale), out_shape=jax.Shap...  1.02 us
  transfers between devices with their start and end apart: 11, of which 8 were waited for; matrix products, arithmetic and copies ran while one was open for 9% of the time, Pallas kernels for 1%

profile of v5, /device:TPU:0, one launch (start us, length us, event | category | flops | bytes accessed | tf_op | source)
XLA Modules:
  0.0 29.4 jit_solution(13132617137257509296)
XLA Ops:
  0.6 0.0 copy-start
  0.6 0.0 copy-start.2
  0.7 0.0 copy-start.3
  0.7 0.0 copy-start.1
  0.7 1.3 %shard_map.86 = (bf16[128,512]{1,0:T(8,128)(2,1)S(1)}, bf16[128,512]{1,0:T(8,128)(2,1)S(1)}) custom-call(s32[128,1024]{1,0:T(8,128)} %counts.1, s32[128]{0:T(128)} %src_degree.1, s32[1024]{0:T(1024)} %dst_degree.1), custom_call_target="tpu_custom_call" | custom-call | tf_op jit(solution)/shard_map/pallas_call | solution.py:117
  2.0 3.0 %collective-permute-start = (bf16[128,512]{1,0:T(8,128)(2,1)S(1)}, bf16[128,512]{1,0:T(8,128)(2,1)S(1)}, u32[]{:S(2)}, u32[]{:S(2)}) collective-permute-start(bf16[128,512]{1,0:T(8,128)(2,1)S(1)} %get-tuple-element.21), channel_id=1, source_target_pairs={{0,1},{1,0},{2,3},{3,2},{4,5},{5,4},{6,7},{7,6},{8,9},{9,8},{10,11... | collective-permute-start | bytes 393224 | tf_op jit(solution)/shard_map/ppermute | solution.py:13
  5.0 0.0 copy-done.2
  5.0 0.0 copy-done.3
  5.0 2.7 %collective-permute-start.2 = (bf16[1,16,512]{2,1,0:T(8,128)(2,1)S(1)}, bf16[1,16,512]{2,1,0:T(8,128)(2,1)S(1)}, u32[]{:S(2)}, u32[]{:S(2)}) collective-permute-start(bf16[1,16,512]{2,1,0:T(8,128)(2,1)S(1)} %fusion.6), channel_id=1, source_target_pairs={{0,16},{2,18},{4,20},{6,22},{8,24},{10,26},{12,28},{14,30},{16,0},... | collective-permute-start | bytes 49160 | tf_op jit(solution)/shard_map/ppermute | solution.py:13
  7.7 0.0 copy-done.1
  7.7 0.2 shard_map.87
  7.9 0.6 %collective-permute-done = bf16[128,512]{1,0:T(8,128)(2,1)S(1)} collective-permute-done((bf16[128,512]{1,0:T(8,128)(2,1)S(1)}, bf16[128,512]{1,0:T(8,128)(2,1)S(1)}, u32[]{:S(2)}, u32[]{:S(2)}) %collective-permute-start) | collective-permute-done | bytes 131104 | tf_op jit(solution)/shard_map/ppermute | solution.py:13
  8.5 0.2 fusion.7
  8.7 0.1 maximum_select_fusion
  8.8 0.1 collective-permute-start.1
  8.9 0.1 maximum_select_fusion.1
  9.0 1.2 %collective-permute-done.1 = bf16[128,512]{1,0:T(8,128)(2,1)S(1)} collective-permute-done((bf16[128,512]{1,0:T(8,128)(2,1)S(1)}, bf16[128,512]{1,0:T(8,128)(2,1)S(1)}, u32[]{:S(2)}, u32[]{:S(2)}) %collective-permute-start.1) | collective-permute-done | bytes 131104 | tf_op jit(solution)/shard_map/ppermute | solution.py:13
  10.3 0.0 collective-permute-done.2
  10.3 1.6 %collective-permute-start.3 = (bf16[128,256]{1,0:T(8,128)(2,1)S(1)}, bf16[128,256]{1,0:T(8,128)(2,1)S(1)}, u32[]{:S(2)}, u32[]{:S(2)}) collective-permute-start(bf16[128,256]{1,0:T(8,128)(2,1)S(1)} %select_convert_fusion.1), channel_id=1, source_target_pairs={{0,3},{1,2},{2,1},{3,0},{4,7},{5,6},{6,5},{7,4},{8,11},{9,10},{10,... | collective-permute-start | bytes 196616 | tf_op jit(solution)/shard_map/ppermute | solution.py:31
  11.9 1.6 %collective-permute-start.4 = (bf16[2,16,512]{2,1,0:T(8,128)(2,1)S(1)}, bf16[2,16,512]{2,1,0:T(8,128)(2,1)S(1)}, u32[]{:S(2)}, u32[]{:S(2)}) collective-permute-start(bf16[2,16,512]{2,1,0:T(8,128)(2,1)S(1)} %maximum_select_fusion.5), channel_id=1, source_target_pairs={{0,4},{2,6},{4,0},{6,2},{8,12},{10,14},{12,8},{14,10},{16,20},{18,... | collective-permute-start | bytes 98312 | tf_op jit(solution)/shard_map/ppermute | solution.py:13
  13.5 1.0 %collective-permute-done.3 = bf16[128,256]{1,0:T(8,128)(2,1)S(1)} collective-permute-done((bf16[128,256]{1,0:T(8,128)(2,1)S(1)}, bf16[128,256]{1,0:T(8,128)(2,1)S(1)}, u32[]{:S(2)}, u32[]{:S(2)}) %collective-permute-start.3) | collective-permute-done | bytes 65568 | tf_op jit(solution)/shard_map/ppermute | solution.py:31
  14.5 1.6 %collective-permute-start.5 = (bf16[128,256]{1,0:T(8,128)(2,1)S(1)}, bf16[128,256]{1,0:T(8,128)(2,1)S(1)}, u32[]{:S(2)}, u32[]{:S(2)}) collective-permute-start(bf16[128,256]{1,0:T(8,128)(2,1)S(1)} %add_convert_fusion.3), channel_id=1, source_target_pairs={{0,10},{1,7},{2,4},{3,9},{4,2},{5,15},{6,12},{7,1},{8,14},{9,3},{1... | collective-permute-start | bytes 196616 | tf_op jit(solution)/shard_map/ppermute | solution.py:31
  16.1 0.0 collective-permute-done.4
  16.1 1.6 %collective-permute-start.6 = (bf16[4,16,512]{2,1,0:T(8,128)(2,1)S(1)}, bf16[4,16,512]{2,1,0:T(8,128)(2,1)S(1)}, u32[]{:S(2)}, u32[]{:S(2)}) collective-permute-start(bf16[4,16,512]{2,1,0:T(8,128)(2,1)S(1)} %bitcast.52), channel_id=1, source_target_pairs={{0,8},{2,10},{4,12},{6,14},{8,0},{10,2},{12,4},{14,6},{16,24},{18,... | collective-permute-start | bytes 196616 | tf_op jit(solution)/shard_map/ppermute | solution.py:13
  17.7 0.6 %collective-permute-done.5 = bf16[128,256]{1,0:T(8,128)(2,1)S(1)} collective-permute-done((bf16[128,256]{1,0:T(8,128)(2,1)S(1)}, bf16[128,256]{1,0:T(8,128)(2,1)S(1)}, u32[]{:S(2)}, u32[]{:S(2)}) %collective-permute-start.5) | collective-permute-done | bytes 65568 | tf_op jit(solution)/shard_map/ppermute | solution.py:31
  18.3 1.5 %collective-permute-start.7 = (bf16[128,256]{1,0:T(8,128)(2,1)S(1)}, bf16[128,256]{1,0:T(8,128)(2,1)S(1)}, u32[]{:S(2)}, u32[]{:S(2)}) collective-permute-start(bf16[128,256]{1,0:T(8,128)(2,1)S(1)} %add_convert_fusion.2), channel_id=1, source_target_pairs={{0,6},{1,19},{2,16},{3,5},{4,22},{5,3},{6,0},{7,21},{8,26},{9,15},... | collective-permute-start | bytes 196616 | tf_op jit(solution)/shard_map/ppermute | solution.py:31
  19.8 0.7 %collective-permute-done.6 = bf16[4,16,512]{2,1,0:T(8,128)(2,1)S(1)} collective-permute-done((bf16[4,16,512]{2,1,0:T(8,128)(2,1)S(1)}, bf16[4,16,512]{2,1,0:T(8,128)(2,1)S(1)}, u32[]{:S(2)}, u32[]{:S(2)}) %collective-permute-start.6) | collective-permute-done | bytes 65568 | tf_op jit(solution)/shard_map/ppermute | solution.py:13
  20.5 0.9 %collective-permute-start.9 = (bf16[128,512]{1,0:T(8,128)(2,1)S(1)}, bf16[128,512]{1,0:T(8,128)(2,1)S(1)}, u32[]{:S(2)}, u32[]{:S(2)}) collective-permute-start(bf16[128,512]{1,0:T(8,128)(2,1)S(1)} %bitcast.40), channel_id=1, source_target_pairs={{0,2},{2,0},{4,6},{6,4},{8,10},{10,8},{12,14},{14,12},{16,18},{18,... | collective-permute-start | bytes 393224 | tf_op jit(solution)/shard_map/ppermute | solution.py:13
  21.4 0.7 %collective-permute-done.7 = bf16[128,256]{1,0:T(8,128)(2,1)S(1)} collective-permute-done((bf16[128,256]{1,0:T(8,128)(2,1)S(1)}, bf16[128,256]{1,0:T(8,128)(2,1)S(1)}, u32[]{:S(2)}, u32[]{:S(2)}) %collective-permute-start.7) | collective-permute-done | bytes 65568 | tf_op jit(solution)/shard_map/ppermute | solution.py:31
  22.1 2.9 %collective-permute-start.8 = (bf16[128,256]{1,0:T(8,128)(2,1)S(1)}, bf16[128,256]{1,0:T(8,128)(2,1)S(1)}, u32[]{:S(2)}, u32[]{:S(2)}) collective-permute-start(bf16[128,256]{1,0:T(8,128)(2,1)S(1)} %add_convert_fusion.1), channel_id=1, source_target_pairs={{0,18},{1,11},{2,8},{3,17},{4,14},{5,23},{6,20},{7,13},{8,2},{9,27... | collective-permute-start | bytes 196616 | tf_op jit(solution)/shard_map/ppermute | solution.py:31
  25.0 0.0 collective-permute-done.9
  25.0 0.3 %fusion.8 = f32[512,512]{1,0:T(8,128)S(1)} fusion(bf16[128,512]{1,0:T(8,128)(2,1)S(1)} %bitcast.46, bf16[128,512]{1,0:T(8,128)(2,1)S(1)} %collective-permute-done.9), kind=kOutput, calls=%fused_computation.29 | convolution fusion | flops 67108864 | bytes 1310720 | tf_op jit(solution)/shard_map/dot_general | solution.py:62
  25.3 0.0 copy-done
  25.3 1.4 %convolution_convert_fusion = bf16[512,512]{1,0:T(8,128)(2,1)} fusion(bf16[512,512]{1,0:T(8,128)(2,1)S(1)} %copy-done, f32[512,512]{1,0:T(8,128)S(1)} %fusion.8, bf16[128,512]{1,0:T(8,128)(2,1)S(1)} %bitcast.45, bf16[128,512]{1,0:T(8,128)(2,1)S(1)} %bitcast.41), kind=kOutput, calls=%fused_computation.2 | convolution fusion | flops 336330752 | bytes 2359296 | tf_op jit(solution)/shard_map/dot_general | solution.py:62
  26.7 0.3 collective-permute-done.8
  27.0 0.5 %collective-permute-start.10 = (bf16[128,256]{1,0:T(8,128)(2,1)S(1)}, bf16[128,256]{1,0:T(8,128)(2,1)S(1)}, u32[]{:S(2)}, u32[]{:S(2)}) collective-permute-start(bf16[128,256]{1,0:T(8,128)(2,1)S(1)} %add_convert_fusion), channel_id=1, source_target_pairs={{0,2},{2,0},{4,6},{6,4},{8,10},{10,8},{12,14},{14,12},{16,18},{18,... | collective-permute-start | bytes 196616 | tf_op jit(solution)/shard_map/ppermute | solution.py:13
  27.5 0.2 fusion.3.mine
  27.8 0.6 %collective-permute-done.10.other = bf16[128,256]{1,0:T(8,128)(2,1)S(1)} collective-permute-done((bf16[128,256]{1,0:T(8,128)(2,1)S(1)}, bf16[128,256]{1,0:T(8,128)(2,1)S(1)}, u32[]{:S(2)}, u32[]{:S(2)}) %collective-permute-start.10) | collective-permute-done | bytes 65568 | tf_op jit(solution)/shard_map/ppermute | solution.py:13
  28.4 1.0 %shard_map.88 = f32[256,512]{1,0:T(8,128)} custom-call(f32[256,512]{1,0:T(8,128)S(1)} %fusion.3.mine, bf16[128,256]{1,0:T(8,128)(2,1)S(1)} %collective-permute-done.10.other, bf16[128,512]{1,0:T(8,128)(2,1)S(1)} %broadcast_select_fusion.rows), custom_call_target="tpu_custom_call" | custom-call | tf_op jit(solution)/shard_map/pallas_call | solution.py:166
  (16 shorter events, 0.3 us)
Async XLA Ops:
  0.6 24.6 %copy-start = (bf16[512,512]{1,0:T(8,128)(2,1)S(1)}, bf16[512,512]{1,0:T(8,128)(2,1)}, u32[]{:S(2)}) copy-start(bf16[512,512]{1,0:T(8,128)(2,1)} %param.13) | copy-start | bytes 1572868
  0.6 4.3 %copy-start.2 = (s32[16,512]{1,0:T(8,128)S(1)}, s32[16,512]{1,0:T(8,128)}, u32[]{:S(2)}) copy-start(s32[16,512]{1,0:T(8,128)} %param.8) | copy-start | bytes 98308
  0.7 4.3 %copy-start.3 = (bf16[16,512]{1,0:T(8,128)(2,1)S(1)}, bf16[16,512]{1,0:T(8,128)(2,1)}, u32[]{:S(2)}) copy-start(bf16[16,512]{1,0:T(8,128)(2,1)} %param.7) | copy-start | bytes 49156
  0.7 7.0 %copy-start.1 = (bf16[512,512]{1,0:T(8,128)(2,1)S(1)}, bf16[512,512]{1,0:T(8,128)(2,1)}, u32[]{:S(2)}) copy-start(bf16[512,512]{1,0:T(8,128)(2,1)} %inputs.1) | copy-start | bytes 1572868
  2.0 6.5 %collective-permute-start = (bf16[128,512]{1,0:T(8,128)(2,1)S(1)}, bf16[128,512]{1,0:T(8,128)(2,1)S(1)}, u32[]{:S(2)}, u32[]{:S(2)}) collective-permute-start(bf16[128,512]{1,0:T(8,128)(2,1)S(1)} %get-tuple-element.21), channel_id=1, source_target_pairs={{0,1},{1,0},{2,3},{3,2},{4,5},{5,4},{6,7},{7,6},{8,9},{9,8},{10,11... | collective-permute-start | bytes 393224 | tf_op jit(solution)/shard_map/ppermute | solution.py:13
  5.0 5.3 %collective-permute-start.2 = (bf16[1,16,512]{2,1,0:T(8,128)(2,1)S(1)}, bf16[1,16,512]{2,1,0:T(8,128)(2,1)S(1)}, u32[]{:S(2)}, u32[]{:S(2)}) collective-permute-start(bf16[1,16,512]{2,1,0:T(8,128)(2,1)S(1)} %fusion.6), channel_id=1, source_target_pairs={{0,16},{2,18},{4,20},{6,22},{8,24},{10,26},{12,28},{14,30},{16,0},... | collective-permute-start | bytes 49160 | tf_op jit(solution)/shard_map/ppermute | solution.py:13
  8.8 1.4 %collective-permute-start.1 = (bf16[128,512]{1,0:T(8,128)(2,1)S(1)}, bf16[128,512]{1,0:T(8,128)(2,1)S(1)}, u32[]{:S(2)}, u32[]{:S(2)}) collective-permute-start(bf16[128,512]{1,0:T(8,128)(2,1)S(1)} %bitcast.49), channel_id=1, source_target_pairs={{0,2},{2,0},{4,6},{6,4},{8,10},{10,8},{12,14},{14,12},{16,18},{18,... | collective-permute-start | bytes 393224 | tf_op jit(solution)/shard_map/ppermute | solution.py:13
  10.3 4.1 %collective-permute-start.3 = (bf16[128,256]{1,0:T(8,128)(2,1)S(1)}, bf16[128,256]{1,0:T(8,128)(2,1)S(1)}, u32[]{:S(2)}, u32[]{:S(2)}) collective-permute-start(bf16[128,256]{1,0:T(8,128)(2,1)S(1)} %select_convert_fusion.1), channel_id=1, source_target_pairs={{0,3},{1,2},{2,1},{3,0},{4,7},{5,6},{6,5},{7,4},{8,11},{9,10},{10,... | collective-permute-start | bytes 196616 | tf_op jit(solution)/shard_map/ppermute | solution.py:31
  11.9 4.2 %collective-permute-start.4 = (bf16[2,16,512]{2,1,0:T(8,128)(2,1)S(1)}, bf16[2,16,512]{2,1,0:T(8,128)(2,1)S(1)}, u32[]{:S(2)}, u32[]{:S(2)}) collective-permute-start(bf16[2,16,512]{2,1,0:T(8,128)(2,1)S(1)} %maximum_select_fusion.5), channel_id=1, source_target_pairs={{0,4},{2,6},{4,0},{6,2},{8,12},{10,14},{12,8},{14,10},{16,20},{18,... | collective-permute-start | bytes 98312 | tf_op jit(solution)/shard_map/ppermute | solution.py:13
  14.5 3.8 %collective-permute-start.5 = (bf16[128,256]{1,0:T(8,128)(2,1)S(1)}, bf16[128,256]{1,0:T(8,128)(2,1)S(1)}, u32[]{:S(2)}, u32[]{:S(2)}) collective-permute-start(bf16[128,256]{1,0:T(8,128)(2,1)S(1)} %add_convert_fusion.3), channel_id=1, source_target_pairs={{0,10},{1,7},{2,4},{3,9},{4,2},{5,15},{6,12},{7,1},{8,14},{9,3},{1... | collective-permute-start | bytes 196616 | tf_op jit(solution)/shard_map/ppermute | solution.py:31
  16.1 4.3 %collective-permute-start.6 = (bf16[4,16,512]{2,1,0:T(8,128)(2,1)S(1)}, bf16[4,16,512]{2,1,0:T(8,128)(2,1)S(1)}, u32[]{:S(2)}, u32[]{:S(2)}) collective-permute-start(bf16[4,16,512]{2,1,0:T(8,128)(2,1)S(1)} %bitcast.52), channel_id=1, source_target_pairs={{0,8},{2,10},{4,12},{6,14},{8,0},{10,2},{12,4},{14,6},{16,24},{18,... | collective-permute-start | bytes 196616 | tf_op jit(solution)/shard_map/ppermute | solution.py:13
  18.3 3.8 %collective-permute-start.7 = (bf16[128,256]{1,0:T(8,128)(2,1)S(1)}, bf16[128,256]{1,0:T(8,128)(2,1)S(1)}, u32[]{:S(2)}, u32[]{:S(2)}) collective-permute-start(bf16[128,256]{1,0:T(8,128)(2,1)S(1)} %add_convert_fusion.2), channel_id=1, source_target_pairs={{0,6},{1,19},{2,16},{3,5},{4,22},{5,3},{6,0},{7,21},{8,26},{9,15},... | collective-permute-start | bytes 196616 | tf_op jit(solution)/shard_map/ppermute | solution.py:31
  20.5 4.5 %collective-permute-start.9 = (bf16[128,512]{1,0:T(8,128)(2,1)S(1)}, bf16[128,512]{1,0:T(8,128)(2,1)S(1)}, u32[]{:S(2)}, u32[]{:S(2)}) collective-permute-start(bf16[128,512]{1,0:T(8,128)(2,1)S(1)} %bitcast.40), channel_id=1, source_target_pairs={{0,2},{2,0},{4,6},{6,4},{8,10},{10,8},{12,14},{14,12},{16,18},{18,... | collective-permute-start | bytes 393224 | tf_op jit(solution)/shard_map/ppermute | solution.py:13
  22.1 4.9 %collective-permute-start.8 = (bf16[128,256]{1,0:T(8,128)(2,1)S(1)}, bf16[128,256]{1,0:T(8,128)(2,1)S(1)}, u32[]{:S(2)}, u32[]{:S(2)}) collective-permute-start(bf16[128,256]{1,0:T(8,128)(2,1)S(1)} %add_convert_fusion.1), channel_id=1, source_target_pairs={{0,18},{1,11},{2,8},{3,17},{4,14},{5,23},{6,20},{7,13},{8,2},{9,27... | collective-permute-start | bytes 196616 | tf_op jit(solution)/shard_map/ppermute | solution.py:31
  27.0 1.4 %collective-permute-start.10 = (bf16[128,256]{1,0:T(8,128)(2,1)S(1)}, bf16[128,256]{1,0:T(8,128)(2,1)S(1)}, u32[]{:S(2)}, u32[]{:S(2)}) collective-permute-start(bf16[128,256]{1,0:T(8,128)(2,1)S(1)} %add_convert_fusion), channel_id=1, source_target_pairs={{0,2},{2,0},{4,6},{6,4},{8,10},{10,8},{12,14},{14,12},{16,18},{18,... | collective-permute-start | bytes 196616 | tf_op jit(solution)/shard_map/ppermute | solution.py:13

commit v6 on v5

--- a/solution.py
+++ b/solution.py
@@ -58,6 +58,10 @@
     return block
 
 
+def add(first, second):
+    return second if first is None else first if second is None else first + second
+
+
 def matmul(left, right, contract):
     return lax.dot_general(
         left, right, (contract, ((), ())), preferred_element_type=jnp.float32
@@ -67,28 +71,36 @@
 CHUNKS = 4
 
 
-def prepare_kernel(replicas, counts, src_degree, dst_degree, *refs):
-    outs, (count_part, src_part, dst_part, sems) = refs[:replicas], refs[replicas:]
+def prepare_kernel(counts, src_degree, dst_degree, adjoint, active, *refs):
+    outs, masked, scratch = refs[:-7], refs[-7], refs[-6:]
+    count_part, src_part, dst_part, adjoint_part, active_part, sems = scratch
     src_rows, rows = outs[0].shape
     piece = src_rows // CHUNKS
+    replicas = len(outs)
     replica = lax.axis_index("rep")
     owners = [replica ^ step for step in range(1, replicas)] + [replica]
     degrees = [
         pltpu.make_async_copy(src_degree, src_part, sems.at[0]),
         pltpu.make_async_copy(dst_degree, dst_part, sems.at[1]),
     ]
-    for copy in degrees:
-        copy.start()
+    factors = [
+        pltpu.make_async_copy(adjoint, adjoint_part, sems.at[2]),
+        pltpu.make_async_copy(active, active_part, sems.at[3]),
+    ]
     copies = []
     for slot, owner in enumerate(owners):
         columns = pl.ds(pl.multiple_of(owner * rows, 128), rows)
         for chunk in range(CHUNKS):
             at = pl.ds(chunk * piece, piece)
-            copy = pltpu.make_async_copy(
-                counts.at[at, columns], count_part.at[slot, at], sems.at[2 + slot * CHUNKS + chunk]
+            copies.append(
+                pltpu.make_async_copy(
+                    counts.at[at, columns],
+                    count_part.at[slot, at],
+                    sems.at[4 + slot * CHUNKS + chunk],
+                )
             )
-            copy.start()
-            copies.append(copy)
+    for copy in degrees + copies + factors:
+        copy.start()
     for copy in degrees:
         copy.wait()
     src_row = lax.rsqrt(src_part[...].astype(jnp.float32)).reshape(1, src_rows)
@@ -110,22 +122,29 @@
             copies[slot * CHUNKS + chunk].wait()
             values = count_part[slot, at, :].astype(jnp.float32)
             outs[slot][at, :] = (values * src_column[at] * dst_row).astype(jnp.bfloat16)
-
-
-def prepare(counts, src_degree, dst_degree, replicas, rows):
+    for copy in factors:
+        copy.wait()
+    values = adjoint_part[...].astype(jnp.float32) * active_part[...].astype(jnp.float32)
+    masked[...] = values.astype(jnp.bfloat16)
+
+
+def prepare(counts, src_degree, dst_degree, adjoint, active, replicas, rows):
     src_rows = counts.shape[0]
     return pl.pallas_call(
-        functools.partial(prepare_kernel, replicas),
-        out_shape=[pltpu.VMEM((src_rows, rows), jnp.bfloat16)] * replicas,
-        in_specs=[pl.BlockSpec(memory_space=pl.ANY)] * 3,
-        out_specs=[pl.BlockSpec(memory_space=pltpu.VMEM)] * replicas,
+        prepare_kernel,
+        out_shape=[pltpu.VMEM((src_rows, rows), jnp.bfloat16)] * replicas
+        + [pltpu.VMEM(adjoint.shape, jnp.bfloat16)],
+        in_specs=[pl.BlockSpec(memory_space=pl.ANY)] * 5,
+        out_specs=[pl.BlockSpec(memory_space=pltpu.VMEM)] * (replicas + 1),
         scratch_shapes=[
             pltpu.VMEM((replicas, src_rows, rows), jnp.int32),
             pltpu.VMEM(src_degree.shape, jnp.int32),
             pltpu.VMEM(dst_degree.shape, jnp.int32),
-            pltpu.SemaphoreType.DMA((2 + CHUNKS * replicas,)),
+            pltpu.VMEM(adjoint.shape, adjoint.dtype),
+            pltpu.VMEM(active.shape, active.dtype),
+            pltpu.SemaphoreType.DMA((4 + CHUNKS * replicas,)),
         ],
-    )(counts, src_degree, dst_degree)
+    )(counts, src_degree, dst_degree, adjoint, active)
 
 
 def own_kernel(own, inputs, term):
@@ -188,11 +207,12 @@
         shift //= 2
     upper_half = bit_of(fold, 1)
 
-    *sent, own = prepare(counts, src_degree, dst_degree, replicas, rows)
+    *sent, own, masked = prepare(
+        counts, src_degree, dst_degree, adjoint, active, replicas, rows
+    )
     answers = [swap(part, "rep", step) for step, part in enumerate(sent, 1)]
 
     own_term = own_product(own, inputs)
-    masked = (adjoint.astype(jnp.float32) * active.astype(jnp.float32)).astype(jnp.bfloat16)
 
     far = groups // 2
     others = [far >> at for at in range(1, far.bit_length() - 1)]
@@ -215,9 +235,7 @@
     if left:
         moving = left.pop(0)
         theirs = swap(mine, "grp", moving)
-    answers, own_term = lax.optimization_barrier((answers, own_term))
     parts = [own] + answers
-    terms = [own_term] + [matmul(part, inputs, ((1,), (0,))) for part in answers]
 
     def ordered(pieces):
         step = 1
@@ -228,7 +246,7 @@
         return pieces[0]
 
     def halves(block):
-        pairs = block.reshape(groups // 2, 2, block_rows, block.shape[1])
+        pairs = block.reshape(-1, 2, block_rows, block.shape[1])
         even = pairs[:, 0].reshape(-1, block.shape[1])
         uneven = pairs[:, 1].reshape(-1, block.shape[1])
         return even, uneven
@@ -236,25 +254,47 @@
     def chosen(upper, pair):
         return jnp.where(upper, pair[1], pair[0])
 
-    terms = halves(ordered(terms))
-    kept, sent = chosen(upper_half, terms), chosen(~upper_half, terms)
-    total = kept + swap(sent.astype(jnp.bfloat16), "grp", 1).astype(jnp.float32)
-
+    def neighbour_sum(block):
+        pair = halves(block)
+        kept, sent = chosen(upper_half, pair), chosen(~upper_half, pair)
+        return kept + swap(sent.astype(jnp.bfloat16), "grp", 1).astype(jnp.float32)
+
+    own_sum = neighbour_sum(own_term)
+    early = [part_of(own_sum, 1, replica, replicas)]
+    leaving = [
+        part_of(own_sum, 1, replica ^ step, replicas).astype(jnp.bfloat16)
+        for step in range(1, replicas)
+    ]
+    answers, early = lax.optimization_barrier((answers, early))
+    early_theirs = [crossed(block, (0, 0), step) for step, block in enumerate(leaving, 1)]
+
+    terms = neighbour_sum(jnp.concatenate([matmul(part, inputs, ((1,), (0,))) for part in answers], 0))
+    pieces = [None] + jnp.split(terms, replicas - 1, axis=0)
     if moving:
-        total, theirs = lax.optimization_barrier((total, theirs))
+        pieces, theirs = lax.optimization_barrier((pieces, theirs))
         mine, moving = gathered(mine, theirs, moving), None
 
     step = replicas // 2
     while step:
         upper = bit_of(replica, step)
-        sent = half_of(total, 1, ~upper).astype(jnp.bfloat16)
+        there = [at for at, piece in enumerate(pieces) if piece is not None]
+        sent = jnp.concatenate([half_of(pieces[at], 1, ~upper) for at in there], 0).astype(jnp.bfloat16)
         if step == 1 and left:
             sent, mine = lax.optimization_barrier((sent, mine))
             moving = left.pop(0)
             row_theirs = swap(mine, "grp", moving)
-        theirs = crossed(sent, (0, 0), step)
-        total = half_of(total, 1, upper) + theirs.astype(jnp.float32)
+        theirs = jnp.split(crossed(sent, (0, 0), step).astype(jnp.float32), len(there), axis=0)
+        pieces = [piece if piece is None else half_of(piece, 1, upper) for piece in pieces]
+        if step == 1:
+            kept = [pieces[at] for at in there]
+            kept, early_theirs = lax.optimization_barrier((kept, early_theirs))
+            for at, piece in zip(there, kept):
+                pieces[at] = piece
+        for at, block in zip(there, theirs):
+            pieces[at ^ step] = add(pieces[at ^ step], block)
         step //= 2
+    early += [block.astype(jnp.float32) for block in early_theirs]
+    total = ordered([add(*pair) for pair in zip(pieces, early)])
 
     theirs = None
     for at, steps in enumerate(sum_steps):

time: 29.7 us -> 28.8 us (0.970)
  waiting for transfers between devices: 5.67 us -> 4.38 us
  starting transfers between devices: 17.8 us -> 18.2 us
    ppermute x4 -> x5, waiting for transfers between devices: 2.55 us -> 1.4 us  [crossed(): return lax.ppermute(block, ('grp', 'rep'), pairs)]
    ppermute x4 -> x5, starting transfers between devices: 7.54 us -> 7.93 us  [crossed(): return lax.ppermute(block, ('grp', 'rep'), pairs)]
    ppermute x7 -> x8, waiting for transfers between devices: 3.12 us -> 2.99 us  [swap(): return lax.ppermute(block, axis, [(at, at ^ step) for at in range(size)])]
    ppermute x7 -> x8, starting transfers between devices: 10.3 us -> 10.2 us  [swap(): return lax.ppermute(block, axis, [(at, at ^ step) for at in range(size)])]
  transfers between devices with their start and end apart: 11 -> 13, of which waited for: 8 -> 8; matrix products, arithmetic and copies ran while one was open for 9% -> 9% of each run, Pallas kernels for 1% -> 1%
where the time goes in v6:
time: 28.8 us; the launch traced here: 28.6 us
  starting transfers between devices  18.2 us (63%)
  waiting for transfers between devices  4.38 us (15%)
  Pallas kernels  2.55 us (9%)
  matrix products  2.17 us (8%)
  between operations  0.89 us (3%)
  other arithmetic  0.4 us (1%)
    ppermute x8, starting transfers between devices, swap(): return lax.ppermute(block, axis, [(at, at ^ step) for at in range(size)])  10.2 us
    ppermute x5, starting transfers between devices, crossed(): return lax.ppermute(block, ('grp', 'rep'), pairs)  7.93 us
    ppermute x8, waiting for transfers between devices, swap(): return lax.ppermute(block, axis, [(at, at ^ step) for at in range(size)])  2.99 us
    dot_general x4, matrix products, matmul(): lax.dot_general(left, right, (contract, ((), ())), preferred_element_type...  2.17 us
    ppermute x5, waiting for transfers between devices, crossed(): return lax.ppermute(block, ('grp', 'rep'), pairs)  1.4 us
    pallas_call x1, Pallas kernels, prepare(): pl.pallas_call(prepare_kernel, out_shape=[pltpu.VMEM((src_rows, rows), jn...  1.3 us
    pallas_call x1, Pallas kernels, final_product(): pl.pallas_call(functools.partial(final_kernel, scale), out_shape=jax.Shap...  1.02 us
  transfers between devices with their start and end apart: 13, of which 8 were waited for; matrix products, arithmetic and copies ran while one was open for 9% of the time, Pallas kernels for 1%

profile of v6, /device:TPU:0, one launch (start us, length us, event | category | flops | bytes accessed | tf_op | source)
XLA Modules:
  0.0 28.6 jit_solution(7988449929831720155)
XLA Ops:
  0.6 0.0 copy-start
  0.6 0.0 copy-start.1
  0.7 1.3 %shard_map.86 = (bf16[128,512]{1,0:T(8,128)(2,1)S(1)}, bf16[128,512]{1,0:T(8,128)(2,1)S(1)}, bf16[16,512]{1,0:T(8,128)(2,1)S(1)}) custom-call(s32[128,1024]{1,0:T(8,128)} %counts.1, s32[128]{0:T(128)} %src_degree.1, s32[1024]{0:T(1024)} %dst_degree.1, bf16[16,512]{1,0:T(8,128)(2,1)} %adjoint.1, s32[16,512]{1,0:T(8,128)} %active.1), custom_call_target="tpu_custom_call" | custom-call | tf_op jit(solution)/shard_map/pallas_call | solution.py:133
  2.0 3.0 %collective-permute-start = (bf16[128,512]{1,0:T(8,128)(2,1)S(1)}, bf16[128,512]{1,0:T(8,128)(2,1)S(1)}, u32[]{:S(2)}, u32[]{:S(2)}) collective-permute-start(bf16[128,512]{1,0:T(8,128)(2,1)S(1)} %get-tuple-element.24), channel_id=1, source_target_pairs={{0,1},{1,0},{2,3},{3,2},{4,5},{5,4},{6,7},{7,6},{8,9},{9,8},{10,11... | collective-permute-start | bytes 393224 | tf_op jit(solution)/shard_map/ppermute | solution.py:13
  5.0 0.0 copy-done.1
  5.0 0.2 shard_map.87
  5.3 0.1 collective-permute-start.1
  5.3 2.7 %collective-permute-start.3 = (bf16[1,16,512]{2,1,0:T(8,128)(2,1)S(1)}, bf16[1,16,512]{2,1,0:T(8,128)(2,1)S(1)}, u32[]{:S(2)}, u32[]{:S(2)}) collective-permute-start(bf16[1,16,512]{2,1,0:T(8,128)(2,1)S(1)} %bitcast.55), channel_id=1, source_target_pairs={{0,16},{2,18},{4,20},{6,22},{8,24},{10,26},{12,28},{14,30},{16,0},... | collective-permute-start | bytes 49160 | tf_op jit(solution)/shard_map/ppermute | solution.py:13
  8.0 0.0 collective-permute-done.1
  8.1 0.3 %collective-permute-start.4 = (bf16[64,256]{1,0:T(8,128)(2,1)S(1)}, bf16[64,256]{1,0:T(8,128)(2,1)S(1)}, u32[]{:S(2)}, u32[]{:S(2)}) collective-permute-start(bf16[64,256]{1,0:T(8,128)(2,1)S(1)} %select_convert_fusion.3), channel_id=1, source_target_pairs={{0,3},{1,2},{2,1},{3,0},{4,7},{5,6},{6,5},{7,4},{8,11},{9,10},{10,... | collective-permute-start | bytes 98312 | tf_op jit(solution)/shard_map/ppermute | solution.py:31
  8.4 0.0 collective-permute-done
  8.5 0.2 fusion.8
  8.8 0.4 %collective-permute-start.2 = (bf16[64,512]{1,0:T(8,128)(2,1)S(1)}, bf16[64,512]{1,0:T(8,128)(2,1)S(1)}, u32[]{:S(2)}, u32[]{:S(2)}) collective-permute-start(bf16[64,512]{1,0:T(8,128)(2,1)S(1)} %bitcast.71), channel_id=1, source_target_pairs={{0,2},{2,0},{4,6},{6,4},{8,10},{10,8},{12,14},{14,12},{16,18},{18,... | collective-permute-start | bytes 196616 | tf_op jit(solution)/shard_map/ppermute | solution.py:13
  9.1 0.1 maximum_select_fusion
  9.3 0.8 %collective-permute-done.2 = bf16[64,512]{1,0:T(8,128)(2,1)S(1)} collective-permute-done((bf16[64,512]{1,0:T(8,128)(2,1)S(1)}, bf16[64,512]{1,0:T(8,128)(2,1)S(1)}, u32[]{:S(2)}, u32[]{:S(2)}) %collective-permute-start.2) | collective-permute-done | bytes 65568 | tf_op jit(solution)/shard_map/ppermute | solution.py:13
  10.1 0.0 collective-permute-done.3
  10.2 1.6 %collective-permute-start.5 = (bf16[64,256]{1,0:T(8,128)(2,1)S(1)}, bf16[64,256]{1,0:T(8,128)(2,1)S(1)}, u32[]{:S(2)}, u32[]{:S(2)}) collective-permute-start(bf16[64,256]{1,0:T(8,128)(2,1)S(1)} %select_convert_fusion.2), channel_id=1, source_target_pairs={{0,3},{1,2},{2,1},{3,0},{4,7},{5,6},{6,5},{7,4},{8,11},{9,10},{10,... | collective-permute-start | bytes 98312 | tf_op jit(solution)/shard_map/ppermute | solution.py:31
  11.7 0.0 collective-permute-done.4
  11.7 1.5 %collective-permute-start.6 = (bf16[2,16,512]{2,1,0:T(8,128)(2,1)S(1)}, bf16[2,16,512]{2,1,0:T(8,128)(2,1)S(1)}, u32[]{:S(2)}, u32[]{:S(2)}) collective-permute-start(bf16[2,16,512]{2,1,0:T(8,128)(2,1)S(1)} %maximum_select_fusion.5), channel_id=1, source_target_pairs={{0,4},{2,6},{4,0},{6,2},{8,12},{10,14},{12,8},{14,10},{16,20},{18,... | collective-permute-start | bytes 98312 | tf_op jit(solution)/shard_map/ppermute | solution.py:13
  13.2 0.3 %collective-permute-done.5 = bf16[64,256]{1,0:T(8,128)(2,1)S(1)} collective-permute-done((bf16[64,256]{1,0:T(8,128)(2,1)S(1)}, bf16[64,256]{1,0:T(8,128)(2,1)S(1)}, u32[]{:S(2)}, u32[]{:S(2)}) %collective-permute-start.5) | collective-permute-done | bytes 32800 | tf_op jit(solution)/shard_map/ppermute | solution.py:31
  13.6 1.6 %collective-permute-start.7 = (bf16[128,256]{1,0:T(8,128)(2,1)S(1)}, bf16[128,256]{1,0:T(8,128)(2,1)S(1)}, u32[]{:S(2)}, u32[]{:S(2)}) collective-permute-start(bf16[128,256]{1,0:T(8,128)(2,1)S(1)} %fusion.1), channel_id=1, source_target_pairs={{0,10},{1,7},{2,4},{3,9},{4,2},{5,15},{6,12},{7,1},{8,14},{9,3},{1... | collective-permute-start | bytes 196616 | tf_op jit(solution)/shard_map/ppermute | solution.py:31
  15.2 0.4 %collective-permute-done.6 = bf16[2,16,512]{2,1,0:T(8,128)(2,1)S(1)} collective-permute-done((bf16[2,16,512]{2,1,0:T(8,128)(2,1)S(1)}, bf16[2,16,512]{2,1,0:T(8,128)(2,1)S(1)}, u32[]{:S(2)}, u32[]{:S(2)}) %collective-permute-start.6) | collective-permute-done | bytes 32800 | tf_op jit(solution)/shard_map/ppermute | solution.py:13
  15.7 1.6 %collective-permute-start.8 = (bf16[4,16,512]{2,1,0:T(8,128)(2,1)S(1)}, bf16[4,16,512]{2,1,0:T(8,128)(2,1)S(1)}, u32[]{:S(2)}, u32[]{:S(2)}) collective-permute-start(bf16[4,16,512]{2,1,0:T(8,128)(2,1)S(1)} %bitcast.72), channel_id=1, source_target_pairs={{0,8},{2,10},{4,12},{6,14},{8,0},{10,2},{12,4},{14,6},{16,24},{18,... | collective-permute-start | bytes 196616 | tf_op jit(solution)/shard_map/ppermute | solution.py:13
  17.3 0.1 collective-permute-done.7
  17.4 1.5 %collective-permute-start.9 = (bf16[128,256]{1,0:T(8,128)(2,1)S(1)}, bf16[128,256]{1,0:T(8,128)(2,1)S(1)}, u32[]{:S(2)}, u32[]{:S(2)}) collective-permute-start(bf16[128,256]{1,0:T(8,128)(2,1)S(1)} %add_convert_fusion.2), channel_id=1, source_target_pairs={{0,6},{1,19},{2,16},{3,5},{4,22},{5,3},{6,0},{7,21},{8,26},{9,15},... | collective-permute-start | bytes 196616 | tf_op jit(solution)/shard_map/ppermute | solution.py:31
  18.9 1.1 %collective-permute-done.8 = bf16[4,16,512]{2,1,0:T(8,128)(2,1)S(1)} collective-permute-done((bf16[4,16,512]{2,1,0:T(8,128)(2,1)S(1)}, bf16[4,16,512]{2,1,0:T(8,128)(2,1)S(1)}, u32[]{:S(2)}, u32[]{:S(2)}) %collective-permute-start.8) | collective-permute-done | bytes 65568 | tf_op jit(solution)/shard_map/ppermute | solution.py:13
  20.1 0.4 %collective-permute-start.11 = (bf16[128,512]{1,0:T(8,128)(2,1)S(1)}, bf16[128,512]{1,0:T(8,128)(2,1)S(1)}, u32[]{:S(2)}, u32[]{:S(2)}) collective-permute-start(bf16[128,512]{1,0:T(8,128)(2,1)S(1)} %bitcast.57), channel_id=1, source_target_pairs={{0,2},{2,0},{4,6},{6,4},{8,10},{10,8},{12,14},{14,12},{16,18},{18,... | collective-permute-start | bytes 393224 | tf_op jit(solution)/shard_map/ppermute | solution.py:13
  20.5 0.7 %collective-permute-done.9 = bf16[128,256]{1,0:T(8,128)(2,1)S(1)} collective-permute-done((bf16[128,256]{1,0:T(8,128)(2,1)S(1)}, bf16[128,256]{1,0:T(8,128)(2,1)S(1)}, u32[]{:S(2)}, u32[]{:S(2)}) %collective-permute-start.9) | collective-permute-done | bytes 65568 | tf_op jit(solution)/shard_map/ppermute | solution.py:31
  21.2 2.9 %collective-permute-start.10 = (bf16[128,256]{1,0:T(8,128)(2,1)S(1)}, bf16[128,256]{1,0:T(8,128)(2,1)S(1)}, u32[]{:S(2)}, u32[]{:S(2)}) collective-permute-start(bf16[128,256]{1,0:T(8,128)(2,1)S(1)} %add_convert_fusion.1), channel_id=1, source_target_pairs={{0,18},{1,11},{2,8},{3,17},{4,14},{5,23},{6,20},{7,13},{8,2},{9,27... | collective-permute-start | bytes 196616 | tf_op jit(solution)/shard_map/ppermute | solution.py:31
  24.1 0.0 collective-permute-done.11
  24.1 0.3 %fusion.9 = f32[512,512]{1,0:T(8,128)S(1)} fusion(bf16[128,512]{1,0:T(8,128)(2,1)S(1)} %bitcast.65, bf16[128,512]{1,0:T(8,128)(2,1)S(1)} %collective-permute-done.11), kind=kOutput, calls=%fused_computation.37 | convolution fusion | flops 67108864 | bytes 1310720 | tf_op jit(solution)/shard_map/dot_general | solution.py:66
  24.4 0.0 copy-done
  24.4 1.4 %convolution_convert_fusion = bf16[512,512]{1,0:T(8,128)(2,1)} fusion(bf16[512,512]{1,0:T(8,128)(2,1)S(1)} %copy-done, f32[512,512]{1,0:T(8,128)S(1)} %fusion.9, bf16[128,512]{1,0:T(8,128)(2,1)S(1)} %bitcast.64, bf16[128,512]{1,0:T(8,128)(2,1)S(1)} %bitcast.58), kind=kOutput, calls=%fused_computation.2 | convolution fusion | flops 336330752 | bytes 2359296 | tf_op jit(solution)/shard_map/dot_general | solution.py:66
  25.8 0.3 collective-permute-done.10
  26.1 0.5 %collective-permute-start.12 = (bf16[128,256]{1,0:T(8,128)(2,1)S(1)}, bf16[128,256]{1,0:T(8,128)(2,1)S(1)}, u32[]{:S(2)}, u32[]{:S(2)}) collective-permute-start(bf16[128,256]{1,0:T(8,128)(2,1)S(1)} %add_convert_fusion), channel_id=1, source_target_pairs={{0,2},{2,0},{4,6},{6,4},{8,10},{10,8},{12,14},{14,12},{16,18},{18,... | collective-permute-start | bytes 196616 | tf_op jit(solution)/shard_map/ppermute | solution.py:13
  26.7 0.2 fusion.3.mine
  26.9 0.6 %collective-permute-done.12.other = bf16[128,256]{1,0:T(8,128)(2,1)S(1)} collective-permute-done((bf16[128,256]{1,0:T(8,128)(2,1)S(1)}, bf16[128,256]{1,0:T(8,128)(2,1)S(1)}, u32[]{:S(2)}, u32[]{:S(2)}) %collective-permute-start.12) | collective-permute-done | bytes 65568 | tf_op jit(solution)/shard_map/ppermute | solution.py:13
  27.6 1.0 %shard_map.88 = f32[256,512]{1,0:T(8,128)} custom-call(f32[256,512]{1,0:T(8,128)S(1)} %fusion.3.mine, bf16[128,256]{1,0:T(8,128)(2,1)S(1)} %collective-permute-done.12.other, bf16[128,512]{1,0:T(8,128)(2,1)S(1)} %broadcast_select_fusion.rows), custom_call_target="tpu_custom_call" | custom-call | tf_op jit(solution)/shard_map/pallas_call | solution.py:185
  (24 shorter events, 0.4 us)
Async XLA Ops:
  0.6 23.8 %copy-start = (bf16[512,512]{1,0:T(8,128)(2,1)S(1)}, bf16[512,512]{1,0:T(8,128)(2,1)}, u32[]{:S(2)}) copy-start(bf16[512,512]{1,0:T(8,128)(2,1)} %param.13) | copy-start | bytes 1572868
  0.6 4.4 %copy-start.1 = (bf16[512,512]{1,0:T(8,128)(2,1)S(1)}, bf16[512,512]{1,0:T(8,128)(2,1)}, u32[]{:S(2)}) copy-start(bf16[512,512]{1,0:T(8,128)(2,1)} %inputs.1) | copy-start | bytes 1572868
  2.0 6.5 %collective-permute-start = (bf16[128,512]{1,0:T(8,128)(2,1)S(1)}, bf16[128,512]{1,0:T(8,128)(2,1)S(1)}, u32[]{:S(2)}, u32[]{:S(2)}) collective-permute-start(bf16[128,512]{1,0:T(8,128)(2,1)S(1)} %get-tuple-element.24), channel_id=1, source_target_pairs={{0,1},{1,0},{2,3},{3,2},{4,5},{5,4},{6,7},{7,6},{8,9},{9,8},{10,11... | collective-permute-start | bytes 393224 | tf_op jit(solution)/shard_map/ppermute | solution.py:13
  5.3 2.8 %collective-permute-start.1 = (bf16[64,512]{1,0:T(8,128)(2,1)S(1)}, bf16[64,512]{1,0:T(8,128)(2,1)S(1)}, u32[]{:S(2)}, u32[]{:S(2)}) collective-permute-start(bf16[64,512]{1,0:T(8,128)(2,1)S(1)} %bitcast.70), channel_id=1, source_target_pairs={{0,2},{2,0},{4,6},{6,4},{8,10},{10,8},{12,14},{14,12},{16,18},{18,... | collective-permute-start | bytes 196616 | tf_op jit(solution)/shard_map/ppermute | solution.py:13
  5.3 4.8 %collective-permute-start.3 = (bf16[1,16,512]{2,1,0:T(8,128)(2,1)S(1)}, bf16[1,16,512]{2,1,0:T(8,128)(2,1)S(1)}, u32[]{:S(2)}, u32[]{:S(2)}) collective-permute-start(bf16[1,16,512]{2,1,0:T(8,128)(2,1)S(1)} %bitcast.55), channel_id=1, source_target_pairs={{0,16},{2,18},{4,20},{6,22},{8,24},{10,26},{12,28},{14,30},{16,0},... | collective-permute-start | bytes 49160 | tf_op jit(solution)/shard_map/ppermute | solution.py:13
  8.1 3.6 %collective-permute-start.4 = (bf16[64,256]{1,0:T(8,128)(2,1)S(1)}, bf16[64,256]{1,0:T(8,128)(2,1)S(1)}, u32[]{:S(2)}, u32[]{:S(2)}) collective-permute-start(bf16[64,256]{1,0:T(8,128)(2,1)S(1)} %select_convert_fusion.3), channel_id=1, source_target_pairs={{0,3},{1,2},{2,1},{3,0},{4,7},{5,6},{6,5},{7,4},{8,11},{9,10},{10,... | collective-permute-start | bytes 98312 | tf_op jit(solution)/shard_map/ppermute | solution.py:31
  8.8 1.3 %collective-permute-start.2 = (bf16[64,512]{1,0:T(8,128)(2,1)S(1)}, bf16[64,512]{1,0:T(8,128)(2,1)S(1)}, u32[]{:S(2)}, u32[]{:S(2)}) collective-permute-start(bf16[64,512]{1,0:T(8,128)(2,1)S(1)} %bitcast.71), channel_id=1, source_target_pairs={{0,2},{2,0},{4,6},{6,4},{8,10},{10,8},{12,14},{14,12},{16,18},{18,... | collective-permute-start | bytes 196616 | tf_op jit(solution)/shard_map/ppermute | solution.py:13
  10.2 3.4 %collective-permute-start.5 = (bf16[64,256]{1,0:T(8,128)(2,1)S(1)}, bf16[64,256]{1,0:T(8,128)(2,1)S(1)}, u32[]{:S(2)}, u32[]{:S(2)}) collective-permute-start(bf16[64,256]{1,0:T(8,128)(2,1)S(1)} %select_convert_fusion.2), channel_id=1, source_target_pairs={{0,3},{1,2},{2,1},{3,0},{4,7},{5,6},{6,5},{7,4},{8,11},{9,10},{10,... | collective-permute-start | bytes 98312 | tf_op jit(solution)/shard_map/ppermute | solution.py:31
  11.7 3.9 %collective-permute-start.6 = (bf16[2,16,512]{2,1,0:T(8,128)(2,1)S(1)}, bf16[2,16,512]{2,1,0:T(8,128)(2,1)S(1)}, u32[]{:S(2)}, u32[]{:S(2)}) collective-permute-start(bf16[2,16,512]{2,1,0:T(8,128)(2,1)S(1)} %maximum_select_fusion.5), channel_id=1, source_target_pairs={{0,4},{2,6},{4,0},{6,2},{8,12},{10,14},{12,8},{14,10},{16,20},{18,... | collective-permute-start | bytes 98312 | tf_op jit(solution)/shard_map/ppermute | solution.py:13
  13.6 3.8 %collective-permute-start.7 = (bf16[128,256]{1,0:T(8,128)(2,1)S(1)}, bf16[128,256]{1,0:T(8,128)(2,1)S(1)}, u32[]{:S(2)}, u32[]{:S(2)}) collective-permute-start(bf16[128,256]{1,0:T(8,128)(2,1)S(1)} %fusion.1), channel_id=1, source_target_pairs={{0,10},{1,7},{2,4},{3,9},{4,2},{5,15},{6,12},{7,1},{8,14},{9,3},{1... | collective-permute-start | bytes 196616 | tf_op jit(solution)/shard_map/ppermute | solution.py:31
  15.7 4.3 %collective-permute-start.8 = (bf16[4,16,512]{2,1,0:T(8,128)(2,1)S(1)}, bf16[4,16,512]{2,1,0:T(8,128)(2,1)S(1)}, u32[]{:S(2)}, u32[]{:S(2)}) collective-permute-start(bf16[4,16,512]{2,1,0:T(8,128)(2,1)S(1)} %bitcast.72), channel_id=1, source_target_pairs={{0,8},{2,10},{4,12},{6,14},{8,0},{10,2},{12,4},{14,6},{16,24},{18,... | collective-permute-start | bytes 196616 | tf_op jit(solution)/shard_map/ppermute | solution.py:13
  17.4 3.8 %collective-permute-start.9 = (bf16[128,256]{1,0:T(8,128)(2,1)S(1)}, bf16[128,256]{1,0:T(8,128)(2,1)S(1)}, u32[]{:S(2)}, u32[]{:S(2)}) collective-permute-start(bf16[128,256]{1,0:T(8,128)(2,1)S(1)} %add_convert_fusion.2), channel_id=1, source_target_pairs={{0,6},{1,19},{2,16},{3,5},{4,22},{5,3},{6,0},{7,21},{8,26},{9,15},... | collective-permute-start | bytes 196616 | tf_op jit(solution)/shard_map/ppermute | solution.py:31
  20.1 4.1 %collective-permute-start.11 = (bf16[128,512]{1,0:T(8,128)(2,1)S(1)}, bf16[128,512]{1,0:T(8,128)(2,1)S(1)}, u32[]{:S(2)}, u32[]{:S(2)}) collective-permute-start(bf16[128,512]{1,0:T(8,128)(2,1)S(1)} %bitcast.57), channel_id=1, source_target_pairs={{0,2},{2,0},{4,6},{6,4},{8,10},{10,8},{12,14},{14,12},{16,18},{18,... | collective-permute-start | bytes 393224 | tf_op jit(solution)/shard_map/ppermute | solution.py:13
  21.2 4.9 %collective-permute-start.10 = (bf16[128,256]{1,0:T(8,128)(2,1)S(1)}, bf16[128,256]{1,0:T(8,128)(2,1)S(1)}, u32[]{:S(2)}, u32[]{:S(2)}) collective-permute-start(bf16[128,256]{1,0:T(8,128)(2,1)S(1)} %add_convert_fusion.1), channel_id=1, source_target_pairs={{0,18},{1,11},{2,8},{3,17},{4,14},{5,23},{6,20},{7,13},{8,2},{9,27... | collective-permute-start | bytes 196616 | tf_op jit(solution)/shard_map/ppermute | solution.py:31
  26.1 1.4 %collective-permute-start.12 = (bf16[128,256]{1,0:T(8,128)(2,1)S(1)}, bf16[128,256]{1,0:T(8,128)(2,1)S(1)}, u32[]{:S(2)}, u32[]{:S(2)}) collective-permute-start(bf16[128,256]{1,0:T(8,128)(2,1)S(1)} %add_convert_fusion), channel_id=1, source_target_pairs={{0,2},{2,0},{4,6},{6,4},{8,10},{10,8},{12,14},{14,12},{16,18},{18,... | collective-permute-start | bytes 196616 | tf_op jit(solution)/shard_map/ppermute | solution.py:13

commit v7 on v6

--- a/solution.py
+++ b/solution.py
@@ -72,13 +72,13 @@
 
 
 def prepare_kernel(counts, src_degree, dst_degree, adjoint, active, *refs):
-    outs, masked, scratch = refs[:-7], refs[-7], refs[-6:]
+    outs, (src_scale, dst_scale, masked), scratch = refs[:-9], refs[-9:-6], refs[-6:]
     count_part, src_part, dst_part, adjoint_part, active_part, sems = scratch
     src_rows, rows = outs[0].shape
     piece = src_rows // CHUNKS
-    replicas = len(outs)
+    replicas = len(outs) + 1
     replica = lax.axis_index("rep")
-    owners = [replica ^ step for step in range(1, replicas)] + [replica]
+    owners = [replica ^ step for step in range(1, replicas)]
     degrees = [
         pltpu.make_async_copy(src_degree, src_part, sems.at[0]),
         pltpu.make_async_copy(dst_degree, dst_part, sems.at[1]),
@@ -109,7 +109,8 @@
     src_column = jnp.sum(
         jnp.where(diagonal, jnp.broadcast_to(src_row, square), 0.0), axis=1, keepdims=True
     )
-    for slot, owner in enumerate(owners):
+    src_scale[...] = src_row
+    for slot, owner in enumerate(owners + [replica]):
         pieces = [dst_part[at * rows : (at + 1) * rows] for at in range(replicas)]
         bit = 1
         while len(pieces) > 1:
@@ -117,6 +118,9 @@
             pieces = [jnp.where(upper, b, a) for a, b in zip(pieces[0::2], pieces[1::2])]
             bit *= 2
         dst_row = lax.rsqrt(pieces[0].astype(jnp.float32)).reshape(1, rows)
+        if slot == len(outs):
+            dst_scale[...] = dst_row
+            break
         for chunk in range(CHUNKS):
             at = slice(chunk * piece, (chunk + 1) * piece)
             copies[slot * CHUNKS + chunk].wait()
@@ -129,20 +133,24 @@
 
 
 def prepare(counts, src_degree, dst_degree, adjoint, active, replicas, rows):
-    src_rows = counts.shape[0]
+    src_rows, others = counts.shape[0], replicas - 1
     return pl.pallas_call(
         prepare_kernel,
-        out_shape=[pltpu.VMEM((src_rows, rows), jnp.bfloat16)] * replicas
-        + [pltpu.VMEM(adjoint.shape, jnp.bfloat16)],
+        out_shape=[pltpu.VMEM((src_rows, rows), jnp.bfloat16)] * others
+        + [
+            pltpu.VMEM((1, src_rows), jnp.float32),
+            pltpu.VMEM((1, rows), jnp.float32),
+            pltpu.VMEM(adjoint.shape, jnp.bfloat16),
+        ],
         in_specs=[pl.BlockSpec(memory_space=pl.ANY)] * 5,
-        out_specs=[pl.BlockSpec(memory_space=pltpu.VMEM)] * (replicas + 1),
+        out_specs=[pl.BlockSpec(memory_space=pltpu.VMEM)] * (others + 3),
         scratch_shapes=[
-            pltpu.VMEM((replicas, src_rows, rows), jnp.int32),
+            pltpu.VMEM((others, src_rows, rows), jnp.int32),
             pltpu.VMEM(src_degree.shape, jnp.int32),
             pltpu.VMEM(dst_degree.shape, jnp.int32),
             pltpu.VMEM(adjoint.shape, adjoint.dtype),
             pltpu.VMEM(active.shape, active.dtype),
-            pltpu.SemaphoreType.DMA((4 + CHUNKS * replicas,)),
+            pltpu.SemaphoreType.DMA((4 + CHUNKS * others,)),
         ],
     )(counts, src_degree, dst_degree, adjoint, active)
 
@@ -207,18 +215,20 @@
         shift //= 2
     upper_half = bit_of(fold, 1)
 
-    *sent, own, masked = prepare(
+    *sent, src_scale, dst_scale, masked = prepare(
         counts, src_degree, dst_degree, adjoint, active, replicas, rows
     )
     answers = [swap(part, "rep", step) for step, part in enumerate(sent, 1)]
 
+    own = part_of(counts, 1, replica, replicas).astype(jnp.float32)
+    own = (own * src_scale.reshape(-1, 1) * dst_scale).astype(jnp.bfloat16)
     own_term = own_product(own, inputs)
 
     far = groups // 2
     others = [far >> at for at in range(1, far.bit_length() - 1)]
     far_steps = [far] * (far > 1)
     sum_steps = list(zip(others + far_steps, others[1:] + far_steps + others[:1]))
-    row_steps = far_steps + others[-1:] + others[:-1]
+    row_steps = far_steps + others
 
     def gathered(mine, theirs, step):
         upper = bit_of(group, step)

time: 28.8 us -> 28.7 us (level)
  no operation moved by 1% of the time
where the time goes in v7:
time: 28.7 us; the launch traced here: 28.5 us
  starting transfers between devices  18.1 us (63%)
  waiting for transfers between devices  4.35 us (15%)
  Pallas kernels  2.42 us (8%)
  matrix products  2.17 us (8%)
  between operations  0.91 us (3%)
  other arithmetic  0.47 us (2%)
    ppermute x8, starting transfers between devices, swap(): return lax.ppermute(block, axis, [(at, at ^ step) for at in range(size)])  10.3 us
    ppermute x5, starting transfers between devices, crossed(): return lax.ppermute(block, ('grp', 'rep'), pairs)  7.85 us
    ppermute x8, waiting for transfers between devices, swap(): return lax.ppermute(block, axis, [(at, at ^ step) for at in range(size)])  2.93 us
    dot_general x4, matrix products, matmul(): lax.dot_general(left, right, (contract, ((), ())), preferred_element_type...  2.17 us
    ppermute x5, waiting for transfers between devices, crossed(): return lax.ppermute(block, ('grp', 'rep'), pairs)  1.42 us
    pallas_call x1, Pallas kernels, prepare(): pl.pallas_call(prepare_kernel, out_shape=[pltpu.VMEM((src_rows, rows), jn...  1.17 us
    pallas_call x1, Pallas kernels, final_product(): pl.pallas_call(functools.partial(final_kernel, scale), out_shape=jax.Shap...  1.02 us
  transfers between devices with their start and end apart: 13, of which 8 were waited for; matrix products, arithmetic and copies ran while one was open for 9% of the time, Pallas kernels for 1%

profile of v7, /device:TPU:0, one launch (start us, length us, event | category | flops | bytes accessed | tf_op | source)
XLA Modules:
  0.0 28.5 jit_solution(14852031874532735807)
XLA Ops:
  0.6 0.0 copy-start
  0.6 0.0 copy-start.2
  0.7 0.0 copy-start.1
  0.7 1.2 %shard_map.86 = (bf16[128,512]{1,0:T(8,128)(2,1)S(1)}, f32[1,128]{1,0:T(1,128)S(1)}, f32[1,512]{1,0:T(1,128)S(1)}, bf16[16,512]{1,0:T(8,128)(2,1)S(1)}) custom-call(s32[128,1024]{1,0:T(8,128)} %counts.1, s32[128]{0:T(128)} %src_degree.1, s32[1024]{0:T(1024)} %dst_degree.1, bf16[16,512]{1,0:T(8,128)(2,1)} %adjoint.1, s32[16,512]{1,0:T(8,128)} %active.1), custom_call_target="tpu_custom_call" | custom-call | tf_op jit(solution)/shard_map/pallas_call | solution.py:137
  1.8 3.0 %collective-permute-start = (bf16[128,512]{1,0:T(8,128)(2,1)S(1)}, bf16[128,512]{1,0:T(8,128)(2,1)S(1)}, u32[]{:S(2)}, u32[]{:S(2)}) collective-permute-start(bf16[128,512]{1,0:T(8,128)(2,1)S(1)} %get-tuple-element.25), channel_id=1, source_target_pairs={{0,1},{1,0},{2,3},{3,2},{4,5},{5,4},{6,7},{7,6},{8,9},{9,8},{10,11... | collective-permute-start | bytes 393224 | tf_op jit(solution)/shard_map/ppermute | solution.py:13
  4.9 0.0 copy-done.2
  4.9 0.1 multiply_convert_fusion.own
  5.0 0.0 copy-done.1
  5.0 0.2 shard_map.87
  5.2 0.1 collective-permute-start.1
  5.3 2.7 %collective-permute-start.3 = (bf16[1,16,512]{2,1,0:T(8,128)(2,1)S(1)}, bf16[1,16,512]{2,1,0:T(8,128)(2,1)S(1)}, u32[]{:S(2)}, u32[]{:S(2)}) collective-permute-start(bf16[1,16,512]{2,1,0:T(8,128)(2,1)S(1)} %bitcast.54), channel_id=1, source_target_pairs={{0,16},{2,18},{4,20},{6,22},{8,24},{10,26},{12,28},{14,30},{16,0},... | collective-permute-start | bytes 49160 | tf_op jit(solution)/shard_map/ppermute | solution.py:13
  8.0 0.0 collective-permute-done.1
  8.1 0.3 %collective-permute-start.4 = (bf16[64,256]{1,0:T(8,128)(2,1)S(1)}, bf16[64,256]{1,0:T(8,128)(2,1)S(1)}, u32[]{:S(2)}, u32[]{:S(2)}) collective-permute-start(bf16[64,256]{1,0:T(8,128)(2,1)S(1)} %select_convert_fusion.3), channel_id=1, source_target_pairs={{0,3},{1,2},{2,1},{3,0},{4,7},{5,6},{6,5},{7,4},{8,11},{9,10},{10,... | collective-permute-start | bytes 98312 | tf_op jit(solution)/shard_map/ppermute | solution.py:31
  8.4 0.0 collective-permute-done
  8.4 0.2 fusion.7
  8.7 0.4 %collective-permute-start.2 = (bf16[64,512]{1,0:T(8,128)(2,1)S(1)}, bf16[64,512]{1,0:T(8,128)(2,1)S(1)}, u32[]{:S(2)}, u32[]{:S(2)}) collective-permute-start(bf16[64,512]{1,0:T(8,128)(2,1)S(1)} %bitcast.71), channel_id=1, source_target_pairs={{0,2},{2,0},{4,6},{6,4},{8,10},{10,8},{12,14},{14,12},{16,18},{18,... | collective-permute-start | bytes 196616 | tf_op jit(solution)/shard_map/ppermute | solution.py:13
  9.1 0.1 maximum_select_fusion
  9.2 0.8 %collective-permute-done.2 = bf16[64,512]{1,0:T(8,128)(2,1)S(1)} collective-permute-done((bf16[64,512]{1,0:T(8,128)(2,1)S(1)}, bf16[64,512]{1,0:T(8,128)(2,1)S(1)}, u32[]{:S(2)}, u32[]{:S(2)}) %collective-permute-start.2) | collective-permute-done | bytes 65568 | tf_op jit(solution)/shard_map/ppermute | solution.py:13
  10.0 0.0 collective-permute-done.3
  10.1 1.5 %collective-permute-start.5 = (bf16[64,256]{1,0:T(8,128)(2,1)S(1)}, bf16[64,256]{1,0:T(8,128)(2,1)S(1)}, u32[]{:S(2)}, u32[]{:S(2)}) collective-permute-start(bf16[64,256]{1,0:T(8,128)(2,1)S(1)} %select_convert_fusion.2), channel_id=1, source_target_pairs={{0,3},{1,2},{2,1},{3,0},{4,7},{5,6},{6,5},{7,4},{8,11},{9,10},{10,... | collective-permute-start | bytes 98312 | tf_op jit(solution)/shard_map/ppermute | solution.py:31
  11.7 0.0 collective-permute-done.4
  11.7 1.6 %collective-permute-start.6 = (bf16[2,16,512]{2,1,0:T(8,128)(2,1)S(1)}, bf16[2,16,512]{2,1,0:T(8,128)(2,1)S(1)}, u32[]{:S(2)}, u32[]{:S(2)}) collective-permute-start(bf16[2,16,512]{2,1,0:T(8,128)(2,1)S(1)} %maximum_select_fusion.4), channel_id=1, source_target_pairs={{0,8},{2,10},{4,12},{6,14},{8,0},{10,2},{12,4},{14,6},{16,24},{18,... | collective-permute-start | bytes 98312 | tf_op jit(solution)/shard_map/ppermute | solution.py:13
  13.2 0.3 collective-permute-done.5
  13.6 1.6 %collective-permute-start.7 = (bf16[128,256]{1,0:T(8,128)(2,1)S(1)}, bf16[128,256]{1,0:T(8,128)(2,1)S(1)}, u32[]{:S(2)}, u32[]{:S(2)}) collective-permute-start(bf16[128,256]{1,0:T(8,128)(2,1)S(1)} %fusion.1), channel_id=1, source_target_pairs={{0,10},{1,7},{2,4},{3,9},{4,2},{5,15},{6,12},{7,1},{8,14},{9,3},{1... | collective-permute-start | bytes 196616 | tf_op jit(solution)/shard_map/ppermute | solution.py:31
  15.2 0.4 %collective-permute-done.6 = bf16[2,16,512]{2,1,0:T(8,128)(2,1)S(1)} collective-permute-done((bf16[2,16,512]{2,1,0:T(8,128)(2,1)S(1)}, bf16[2,16,512]{2,1,0:T(8,128)(2,1)S(1)}, u32[]{:S(2)}, u32[]{:S(2)}) %collective-permute-start.6) | collective-permute-done | bytes 32800 | tf_op jit(solution)/shard_map/ppermute | solution.py:13
  15.6 1.6 %collective-permute-start.8 = (bf16[4,16,512]{2,1,0:T(8,128)(2,1)S(1)}, bf16[4,16,512]{2,1,0:T(8,128)(2,1)S(1)}, u32[]{:S(2)}, u32[]{:S(2)}) collective-permute-start(bf16[4,16,512]{2,1,0:T(8,128)(2,1)S(1)} %bitcast.67), channel_id=1, source_target_pairs={{0,4},{2,6},{4,0},{6,2},{8,12},{10,14},{12,8},{14,10},{16,20},{18,... | collective-permute-start | bytes 196616 | tf_op jit(solution)/shard_map/ppermute | solution.py:13
  17.2 0.2 collective-permute-done.7
  17.3 1.5 %collective-permute-start.9 = (bf16[128,256]{1,0:T(8,128)(2,1)S(1)}, bf16[128,256]{1,0:T(8,128)(2,1)S(1)}, u32[]{:S(2)}, u32[]{:S(2)}) collective-permute-start(bf16[128,256]{1,0:T(8,128)(2,1)S(1)} %add_convert_fusion.2), channel_id=1, source_target_pairs={{0,6},{1,19},{2,16},{3,5},{4,22},{5,3},{6,0},{7,21},{8,26},{9,15},... | collective-permute-start | bytes 196616 | tf_op jit(solution)/shard_map/ppermute | solution.py:31
  18.8 1.1 %collective-permute-done.8 = bf16[4,16,512]{2,1,0:T(8,128)(2,1)S(1)} collective-permute-done((bf16[4,16,512]{2,1,0:T(8,128)(2,1)S(1)}, bf16[4,16,512]{2,1,0:T(8,128)(2,1)S(1)}, u32[]{:S(2)}, u32[]{:S(2)}) %collective-permute-start.8) | collective-permute-done | bytes 65568 | tf_op jit(solution)/shard_map/ppermute | solution.py:13
  20.0 0.4 %collective-permute-start.11 = (bf16[128,512]{1,0:T(8,128)(2,1)S(1)}, bf16[128,512]{1,0:T(8,128)(2,1)S(1)}, u32[]{:S(2)}, u32[]{:S(2)}) collective-permute-start(bf16[128,512]{1,0:T(8,128)(2,1)S(1)} %bitcast.58), channel_id=1, source_target_pairs={{0,2},{2,0},{4,6},{6,4},{8,10},{10,8},{12,14},{14,12},{16,18},{18,... | collective-permute-start | bytes 393224 | tf_op jit(solution)/shard_map/ppermute | solution.py:13
  20.4 0.7 %collective-permute-done.9 = bf16[128,256]{1,0:T(8,128)(2,1)S(1)} collective-permute-done((bf16[128,256]{1,0:T(8,128)(2,1)S(1)}, bf16[128,256]{1,0:T(8,128)(2,1)S(1)}, u32[]{:S(2)}, u32[]{:S(2)}) %collective-permute-start.9) | collective-permute-done | bytes 65568 | tf_op jit(solution)/shard_map/ppermute | solution.py:31
  21.1 2.9 %collective-permute-start.10 = (bf16[128,256]{1,0:T(8,128)(2,1)S(1)}, bf16[128,256]{1,0:T(8,128)(2,1)S(1)}, u32[]{:S(2)}, u32[]{:S(2)}) collective-permute-start(bf16[128,256]{1,0:T(8,128)(2,1)S(1)} %add_convert_fusion.1), channel_id=1, source_target_pairs={{0,18},{1,11},{2,8},{3,17},{4,14},{5,23},{6,20},{7,13},{8,2},{9,27... | collective-permute-start | bytes 196616 | tf_op jit(solution)/shard_map/ppermute | solution.py:31
  24.0 0.0 collective-permute-done.11
  24.0 0.3 %fusion.8 = f32[512,512]{1,0:T(8,128)S(1)} fusion(bf16[128,512]{1,0:T(8,128)(2,1)S(1)} %bitcast.66, bf16[128,512]{1,0:T(8,128)(2,1)S(1)} %collective-permute-done.11), kind=kOutput, calls=%fused_computation.36 | convolution fusion | flops 67108864 | bytes 1310720 | tf_op jit(solution)/shard_map/dot_general | solution.py:66
  24.3 0.0 copy-done
  24.3 1.4 %convolution_convert_fusion = bf16[512,512]{1,0:T(8,128)(2,1)} fusion(bf16[512,512]{1,0:T(8,128)(2,1)S(1)} %copy-done, f32[512,512]{1,0:T(8,128)S(1)} %fusion.8, bf16[128,512]{1,0:T(8,128)(2,1)S(1)} %bitcast.65, bf16[128,512]{1,0:T(8,128)(2,1)S(1)} %bitcast.59), kind=kOutput, calls=%fused_computation.2 | convolution fusion | flops 336330752 | bytes 2359296 | tf_op jit(solution)/shard_map/dot_general | solution.py:66
  25.7 0.3 collective-permute-done.10
  26.0 0.6 %collective-permute-start.12 = (bf16[128,256]{1,0:T(8,128)(2,1)S(1)}, bf16[128,256]{1,0:T(8,128)(2,1)S(1)}, u32[]{:S(2)}, u32[]{:S(2)}) collective-permute-start(bf16[128,256]{1,0:T(8,128)(2,1)S(1)} %add_convert_fusion), channel_id=1, source_target_pairs={{0,2},{2,0},{4,6},{6,4},{8,10},{10,8},{12,14},{14,12},{16,18},{18,... | collective-permute-start | bytes 196616 | tf_op jit(solution)/shard_map/ppermute | solution.py:13
  26.6 0.2 fusion.2.mine
  26.8 0.6 %collective-permute-done.12.other = bf16[128,256]{1,0:T(8,128)(2,1)S(1)} collective-permute-done((bf16[128,256]{1,0:T(8,128)(2,1)S(1)}, bf16[128,256]{1,0:T(8,128)(2,1)S(1)}, u32[]{:S(2)}, u32[]{:S(2)}) %collective-permute-start.12) | collective-permute-done | bytes 65568 | tf_op jit(solution)/shard_map/ppermute | solution.py:13
  27.5 1.0 %shard_map.88 = f32[256,512]{1,0:T(8,128)} custom-call(f32[256,512]{1,0:T(8,128)S(1)} %fusion.2.mine, bf16[128,256]{1,0:T(8,128)(2,1)S(1)} %collective-permute-done.12.other, bf16[128,512]{1,0:T(8,128)(2,1)S(1)} %broadcast_select_fusion.rows), custom_call_target="tpu_custom_call" | custom-call | tf_op jit(solution)/shard_map/pallas_call | solution.py:193
  (23 shorter events, 0.3 us)
Async XLA Ops:
  0.6 23.7 %copy-start = (bf16[512,512]{1,0:T(8,128)(2,1)S(1)}, bf16[512,512]{1,0:T(8,128)(2,1)}, u32[]{:S(2)}) copy-start(bf16[512,512]{1,0:T(8,128)(2,1)} %param.13) | copy-start | bytes 1572868
  0.6 4.2 %copy-start.2 = (s32[128,1024]{1,0:T(8,128)S(1)}, s32[128,1024]{1,0:T(8,128)}, u32[]{:S(2)}) copy-start(s32[128,1024]{1,0:T(8,128)} %counts.1) | copy-start | bytes 1572868
  0.7 4.3 %copy-start.1 = (bf16[512,512]{1,0:T(8,128)(2,1)S(1)}, bf16[512,512]{1,0:T(8,128)(2,1)}, u32[]{:S(2)}) copy-start(bf16[512,512]{1,0:T(8,128)(2,1)} %inputs.1) | copy-start | bytes 1572868
  1.8 6.6 %collective-permute-start = (bf16[128,512]{1,0:T(8,128)(2,1)S(1)}, bf16[128,512]{1,0:T(8,128)(2,1)S(1)}, u32[]{:S(2)}, u32[]{:S(2)}) collective-permute-start(bf16[128,512]{1,0:T(8,128)(2,1)S(1)} %get-tuple-element.25), channel_id=1, source_target_pairs={{0,1},{1,0},{2,3},{3,2},{4,5},{5,4},{6,7},{7,6},{8,9},{9,8},{10,11... | collective-permute-start | bytes 393224 | tf_op jit(solution)/shard_map/ppermute | solution.py:13
  5.2 2.8 %collective-permute-start.1 = (bf16[64,512]{1,0:T(8,128)(2,1)S(1)}, bf16[64,512]{1,0:T(8,128)(2,1)S(1)}, u32[]{:S(2)}, u32[]{:S(2)}) collective-permute-start(bf16[64,512]{1,0:T(8,128)(2,1)S(1)} %bitcast.70), channel_id=1, source_target_pairs={{0,2},{2,0},{4,6},{6,4},{8,10},{10,8},{12,14},{14,12},{16,18},{18,... | collective-permute-start | bytes 196616 | tf_op jit(solution)/shard_map/ppermute | solution.py:13
  5.3 4.7 %collective-permute-start.3 = (bf16[1,16,512]{2,1,0:T(8,128)(2,1)S(1)}, bf16[1,16,512]{2,1,0:T(8,128)(2,1)S(1)}, u32[]{:S(2)}, u32[]{:S(2)}) collective-permute-start(bf16[1,16,512]{2,1,0:T(8,128)(2,1)S(1)} %bitcast.54), channel_id=1, source_target_pairs={{0,16},{2,18},{4,20},{6,22},{8,24},{10,26},{12,28},{14,30},{16,0},... | collective-permute-start | bytes 49160 | tf_op jit(solution)/shard_map/ppermute | solution.py:13
  8.1 3.6 %collective-permute-start.4 = (bf16[64,256]{1,0:T(8,128)(2,1)S(1)}, bf16[64,256]{1,0:T(8,128)(2,1)S(1)}, u32[]{:S(2)}, u32[]{:S(2)}) collective-permute-start(bf16[64,256]{1,0:T(8,128)(2,1)S(1)} %select_convert_fusion.3), channel_id=1, source_target_pairs={{0,3},{1,2},{2,1},{3,0},{4,7},{5,6},{6,5},{7,4},{8,11},{9,10},{10,... | collective-permute-start | bytes 98312 | tf_op jit(solution)/shard_map/ppermute | solution.py:31
  8.7 1.3 %collective-permute-start.2 = (bf16[64,512]{1,0:T(8,128)(2,1)S(1)}, bf16[64,512]{1,0:T(8,128)(2,1)S(1)}, u32[]{:S(2)}, u32[]{:S(2)}) collective-permute-start(bf16[64,512]{1,0:T(8,128)(2,1)S(1)} %bitcast.71), channel_id=1, source_target_pairs={{0,2},{2,0},{4,6},{6,4},{8,10},{10,8},{12,14},{14,12},{16,18},{18,... | collective-permute-start | bytes 196616 | tf_op jit(solution)/shard_map/ppermute | solution.py:13
  10.1 3.4 %collective-permute-start.5 = (bf16[64,256]{1,0:T(8,128)(2,1)S(1)}, bf16[64,256]{1,0:T(8,128)(2,1)S(1)}, u32[]{:S(2)}, u32[]{:S(2)}) collective-permute-start(bf16[64,256]{1,0:T(8,128)(2,1)S(1)} %select_convert_fusion.2), channel_id=1, source_target_pairs={{0,3},{1,2},{2,1},{3,0},{4,7},{5,6},{6,5},{7,4},{8,11},{9,10},{10,... | collective-permute-start | bytes 98312 | tf_op jit(solution)/shard_map/ppermute | solution.py:31
  11.7 3.9 %collective-permute-start.6 = (bf16[2,16,512]{2,1,0:T(8,128)(2,1)S(1)}, bf16[2,16,512]{2,1,0:T(8,128)(2,1)S(1)}, u32[]{:S(2)}, u32[]{:S(2)}) collective-permute-start(bf16[2,16,512]{2,1,0:T(8,128)(2,1)S(1)} %maximum_select_fusion.4), channel_id=1, source_target_pairs={{0,8},{2,10},{4,12},{6,14},{8,0},{10,2},{12,4},{14,6},{16,24},{18,... | collective-permute-start | bytes 98312 | tf_op jit(solution)/shard_map/ppermute | solution.py:13
  13.6 3.8 %collective-permute-start.7 = (bf16[128,256]{1,0:T(8,128)(2,1)S(1)}, bf16[128,256]{1,0:T(8,128)(2,1)S(1)}, u32[]{:S(2)}, u32[]{:S(2)}) collective-permute-start(bf16[128,256]{1,0:T(8,128)(2,1)S(1)} %fusion.1), channel_id=1, source_target_pairs={{0,10},{1,7},{2,4},{3,9},{4,2},{5,15},{6,12},{7,1},{8,14},{9,3},{1... | collective-permute-start | bytes 196616 | tf_op jit(solution)/shard_map/ppermute | solution.py:31
  15.6 4.3 %collective-permute-start.8 = (bf16[4,16,512]{2,1,0:T(8,128)(2,1)S(1)}, bf16[4,16,512]{2,1,0:T(8,128)(2,1)S(1)}, u32[]{:S(2)}, u32[]{:S(2)}) collective-permute-start(bf16[4,16,512]{2,1,0:T(8,128)(2,1)S(1)} %bitcast.67), channel_id=1, source_target_pairs={{0,4},{2,6},{4,0},{6,2},{8,12},{10,14},{12,8},{14,10},{16,20},{18,... | collective-permute-start | bytes 196616 | tf_op jit(solution)/shard_map/ppermute | solution.py:13
  17.3 3.8 %collective-permute-start.9 = (bf16[128,256]{1,0:T(8,128)(2,1)S(1)}, bf16[128,256]{1,0:T(8,128)(2,1)S(1)}, u32[]{:S(2)}, u32[]{:S(2)}) collective-permute-start(bf16[128,256]{1,0:T(8,128)(2,1)S(1)} %add_convert_fusion.2), channel_id=1, source_target_pairs={{0,6},{1,19},{2,16},{3,5},{4,22},{5,3},{6,0},{7,21},{8,26},{9,15},... | collective-permute-start | bytes 196616 | tf_op jit(solution)/shard_map/ppermute | solution.py:31
  20.0 4.0 %collective-permute-start.11 = (bf16[128,512]{1,0:T(8,128)(2,1)S(1)}, bf16[128,512]{1,0:T(8,128)(2,1)S(1)}, u32[]{:S(2)}, u32[]{:S(2)}) collective-permute-start(bf16[128,512]{1,0:T(8,128)(2,1)S(1)} %bitcast.58), channel_id=1, source_target_pairs={{0,2},{2,0},{4,6},{6,4},{8,10},{10,8},{12,14},{14,12},{16,18},{18,... | collective-permute-start | bytes 393224 | tf_op jit(solution)/shard_map/ppermute | solution.py:13
  21.1 4.9 %collective-permute-start.10 = (bf16[128,256]{1,0:T(8,128)(2,1)S(1)}, bf16[128,256]{1,0:T(8,128)(2,1)S(1)}, u32[]{:S(2)}, u32[]{:S(2)}) collective-permute-start(bf16[128,256]{1,0:T(8,128)(2,1)S(1)} %add_convert_fusion.1), channel_id=1, source_target_pairs={{0,18},{1,11},{2,8},{3,17},{4,14},{5,23},{6,20},{7,13},{8,2},{9,27... | collective-permute-start | bytes 196616 | tf_op jit(solution)/shard_map/ppermute | solution.py:31
  26.0 1.5 %collective-permute-start.12 = (bf16[128,256]{1,0:T(8,128)(2,1)S(1)}, bf16[128,256]{1,0:T(8,128)(2,1)S(1)}, u32[]{:S(2)}, u32[]{:S(2)}) collective-permute-start(bf16[128,256]{1,0:T(8,128)(2,1)S(1)} %add_convert_fusion), channel_id=1, source_target_pairs={{0,2},{2,0},{4,6},{6,4},{8,10},{10,8},{12,14},{14,12},{16,18},{18,... | collective-permute-start | bytes 196616 | tf_op jit(solution)/shard_map/ppermute | solution.py:13

commit v8 on v7

--- a/solution.py
+++ b/solution.py
@@ -26,7 +26,8 @@
     pairs = []
     for group in range(groups):
         for replica in range(replicas):
-            step = group_steps[parity(group) ^ parity(replica)] | 1
+            step = group_steps[parity(group) ^ parity(replica)]
+            step ^= parity(step) ^ parity(replica_step)
             pairs.append((group * replicas + replica, (group ^ step) * replicas + (replica ^ replica_step)))
     return lax.ppermute(block, ("grp", "rep"), pairs)
 

time: 28.7 us -> 28.7 us (level)
  no operation moved by 1% of the time
where the time goes in v8:
time: 28.7 us; the launch traced here: 28.5 us
  starting transfers between devices  18.1 us (63%)
  waiting for transfers between devices  4.35 us (15%)
  Pallas kernels  2.42 us (8%)
  matrix products  2.17 us (8%)
  between operations  0.91 us (3%)
  other arithmetic  0.47 us (2%)
    ppermute x8, starting transfers between devices, swap(): return lax.ppermute(block, axis, [(at, at ^ step) for at in range(size)])  10.3 us
    ppermute x5, starting transfers between devices, crossed(): return lax.ppermute(block, ('grp', 'rep'), pairs)  7.85 us
    ppermute x8, waiting for transfers between devices, swap(): return lax.ppermute(block, axis, [(at, at ^ step) for at in range(size)])  2.93 us
    dot_general x4, matrix products, matmul(): lax.dot_general(left, right, (contract, ((), ())), preferred_element_type...  2.17 us
    ppermute x5, waiting for transfers between devices, crossed(): return lax.ppermute(block, ('grp', 'rep'), pairs)  1.42 us
    pallas_call x1, Pallas kernels, prepare(): pl.pallas_call(prepare_kernel, out_shape=[pltpu.VMEM((src_rows, rows), jn...  1.17 us
    pallas_call x1, Pallas kernels, final_product(): pl.pallas_call(functools.partial(final_kernel, scale), out_shape=jax.Shap...  1.02 us
  transfers between devices with their start and end apart: 13, of which 8 were waited for; matrix products, arithmetic and copies ran while one was open for 9% of the time, Pallas kernels for 1%

profile of v8, /device:TPU:0, one launch (start us, length us, event | category | flops | bytes accessed | tf_op | source)
XLA Modules:
  0.0 28.5 jit_solution(14852031874532735807)
XLA Ops:
  0.6 0.0 copy-start
  0.6 0.0 copy-start.2
  0.7 0.0 copy-start.1
  0.7 1.2 %shard_map.86 = (bf16[128,512]{1,0:T(8,128)(2,1)S(1)}, f32[1,128]{1,0:T(1,128)S(1)}, f32[1,512]{1,0:T(1,128)S(1)}, bf16[16,512]{1,0:T(8,128)(2,1)S(1)}) custom-call(s32[128,1024]{1,0:T(8,128)} %counts.1, s32[128]{0:T(128)} %src_degree.1, s32[1024]{0:T(1024)} %dst_degree.1, bf16[16,512]{1,0:T(8,128)(2,1)} %adjoint.1, s32[16,512]{1,0:T(8,128)} %active.1), custom_call_target="tpu_custom_call" | custom-call | tf_op jit(solution)/shard_map/pallas_call | solution.py:138
  1.8 3.0 %collective-permute-start = (bf16[128,512]{1,0:T(8,128)(2,1)S(1)}, bf16[128,512]{1,0:T(8,128)(2,1)S(1)}, u32[]{:S(2)}, u32[]{:S(2)}) collective-permute-start(bf16[128,512]{1,0:T(8,128)(2,1)S(1)} %get-tuple-element.25), channel_id=1, source_target_pairs={{0,1},{1,0},{2,3},{3,2},{4,5},{5,4},{6,7},{7,6},{8,9},{9,8},{10,11... | collective-permute-start | bytes 393224 | tf_op jit(solution)/shard_map/ppermute | solution.py:13
  4.9 0.0 copy-done.2
  4.9 0.1 multiply_convert_fusion.own
  5.0 0.0 copy-done.1
  5.0 0.2 shard_map.87
  5.2 0.1 collective-permute-start.1
  5.3 2.7 %collective-permute-start.3 = (bf16[1,16,512]{2,1,0:T(8,128)(2,1)S(1)}, bf16[1,16,512]{2,1,0:T(8,128)(2,1)S(1)}, u32[]{:S(2)}, u32[]{:S(2)}) collective-permute-start(bf16[1,16,512]{2,1,0:T(8,128)(2,1)S(1)} %bitcast.54), channel_id=1, source_target_pairs={{0,16},{2,18},{4,20},{6,22},{8,24},{10,26},{12,28},{14,30},{16,0},... | collective-permute-start | bytes 49160 | tf_op jit(solution)/shard_map/ppermute | solution.py:13
  8.0 0.0 collective-permute-done.1
  8.1 0.3 %collective-permute-start.4 = (bf16[64,256]{1,0:T(8,128)(2,1)S(1)}, bf16[64,256]{1,0:T(8,128)(2,1)S(1)}, u32[]{:S(2)}, u32[]{:S(2)}) collective-permute-start(bf16[64,256]{1,0:T(8,128)(2,1)S(1)} %select_convert_fusion.3), channel_id=1, source_target_pairs={{0,3},{1,2},{2,1},{3,0},{4,7},{5,6},{6,5},{7,4},{8,11},{9,10},{10,... | collective-permute-start | bytes 98312 | tf_op jit(solution)/shard_map/ppermute | solution.py:32
  8.4 0.0 collective-permute-done
  8.4 0.2 fusion.7
  8.7 0.4 %collective-permute-start.2 = (bf16[64,512]{1,0:T(8,128)(2,1)S(1)}, bf16[64,512]{1,0:T(8,128)(2,1)S(1)}, u32[]{:S(2)}, u32[]{:S(2)}) collective-permute-start(bf16[64,512]{1,0:T(8,128)(2,1)S(1)} %bitcast.71), channel_id=1, source_target_pairs={{0,2},{2,0},{4,6},{6,4},{8,10},{10,8},{12,14},{14,12},{16,18},{18,... | collective-permute-start | bytes 196616 | tf_op jit(solution)/shard_map/ppermute | solution.py:13
  9.1 0.1 maximum_select_fusion
  9.2 0.8 %collective-permute-done.2 = bf16[64,512]{1,0:T(8,128)(2,1)S(1)} collective-permute-done((bf16[64,512]{1,0:T(8,128)(2,1)S(1)}, bf16[64,512]{1,0:T(8,128)(2,1)S(1)}, u32[]{:S(2)}, u32[]{:S(2)}) %collective-permute-start.2) | collective-permute-done | bytes 65568 | tf_op jit(solution)/shard_map/ppermute | solution.py:13
  10.0 0.0 collective-permute-done.3
  10.1 1.5 %collective-permute-start.5 = (bf16[64,256]{1,0:T(8,128)(2,1)S(1)}, bf16[64,256]{1,0:T(8,128)(2,1)S(1)}, u32[]{:S(2)}, u32[]{:S(2)}) collective-permute-start(bf16[64,256]{1,0:T(8,128)(2,1)S(1)} %select_convert_fusion.2), channel_id=1, source_target_pairs={{0,3},{1,2},{2,1},{3,0},{4,7},{5,6},{6,5},{7,4},{8,11},{9,10},{10,... | collective-permute-start | bytes 98312 | tf_op jit(solution)/shard_map/ppermute | solution.py:32
  11.7 0.0 collective-permute-done.4
  11.7 1.6 %collective-permute-start.6 = (bf16[2,16,512]{2,1,0:T(8,128)(2,1)S(1)}, bf16[2,16,512]{2,1,0:T(8,128)(2,1)S(1)}, u32[]{:S(2)}, u32[]{:S(2)}) collective-permute-start(bf16[2,16,512]{2,1,0:T(8,128)(2,1)S(1)} %maximum_select_fusion.4), channel_id=1, source_target_pairs={{0,8},{2,10},{4,12},{6,14},{8,0},{10,2},{12,4},{14,6},{16,24},{18,... | collective-permute-start | bytes 98312 | tf_op jit(solution)/shard_map/ppermute | solution.py:13
  13.2 0.3 collective-permute-done.5
  13.6 1.6 %collective-permute-start.7 = (bf16[128,256]{1,0:T(8,128)(2,1)S(1)}, bf16[128,256]{1,0:T(8,128)(2,1)S(1)}, u32[]{:S(2)}, u32[]{:S(2)}) collective-permute-start(bf16[128,256]{1,0:T(8,128)(2,1)S(1)} %fusion.1), channel_id=1, source_target_pairs={{0,10},{1,7},{2,4},{3,9},{4,2},{5,15},{6,12},{7,1},{8,14},{9,3},{1... | collective-permute-start | bytes 196616 | tf_op jit(solution)/shard_map/ppermute | solution.py:32
  15.2 0.4 %collective-permute-done.6 = bf16[2,16,512]{2,1,0:T(8,128)(2,1)S(1)} collective-permute-done((bf16[2,16,512]{2,1,0:T(8,128)(2,1)S(1)}, bf16[2,16,512]{2,1,0:T(8,128)(2,1)S(1)}, u32[]{:S(2)}, u32[]{:S(2)}) %collective-permute-start.6) | collective-permute-done | bytes 32800 | tf_op jit(solution)/shard_map/ppermute | solution.py:13
  15.6 1.6 %collective-permute-start.8 = (bf16[4,16,512]{2,1,0:T(8,128)(2,1)S(1)}, bf16[4,16,512]{2,1,0:T(8,128)(2,1)S(1)}, u32[]{:S(2)}, u32[]{:S(2)}) collective-permute-start(bf16[4,16,512]{2,1,0:T(8,128)(2,1)S(1)} %bitcast.67), channel_id=1, source_target_pairs={{0,4},{2,6},{4,0},{6,2},{8,12},{10,14},{12,8},{14,10},{16,20},{18,... | collective-permute-start | bytes 196616 | tf_op jit(solution)/shard_map/ppermute | solution.py:13
  17.2 0.2 collective-permute-done.7
  17.3 1.5 %collective-permute-start.9 = (bf16[128,256]{1,0:T(8,128)(2,1)S(1)}, bf16[128,256]{1,0:T(8,128)(2,1)S(1)}, u32[]{:S(2)}, u32[]{:S(2)}) collective-permute-start(bf16[128,256]{1,0:T(8,128)(2,1)S(1)} %add_convert_fusion.2), channel_id=1, source_target_pairs={{0,6},{1,19},{2,16},{3,5},{4,22},{5,3},{6,0},{7,21},{8,26},{9,15},... | collective-permute-start | bytes 196616 | tf_op jit(solution)/shard_map/ppermute | solution.py:32
  18.8 1.1 %collective-permute-done.8 = bf16[4,16,512]{2,1,0:T(8,128)(2,1)S(1)} collective-permute-done((bf16[4,16,512]{2,1,0:T(8,128)(2,1)S(1)}, bf16[4,16,512]{2,1,0:T(8,128)(2,1)S(1)}, u32[]{:S(2)}, u32[]{:S(2)}) %collective-permute-start.8) | collective-permute-done | bytes 65568 | tf_op jit(solution)/shard_map/ppermute | solution.py:13
  20.0 0.4 %collective-permute-start.11 = (bf16[128,512]{1,0:T(8,128)(2,1)S(1)}, bf16[128,512]{1,0:T(8,128)(2,1)S(1)}, u32[]{:S(2)}, u32[]{:S(2)}) collective-permute-start(bf16[128,512]{1,0:T(8,128)(2,1)S(1)} %bitcast.58), channel_id=1, source_target_pairs={{0,2},{2,0},{4,6},{6,4},{8,10},{10,8},{12,14},{14,12},{16,18},{18,... | collective-permute-start | bytes 393224 | tf_op jit(solution)/shard_map/ppermute | solution.py:13
  20.4 0.7 %collective-permute-done.9 = bf16[128,256]{1,0:T(8,128)(2,1)S(1)} collective-permute-done((bf16[128,256]{1,0:T(8,128)(2,1)S(1)}, bf16[128,256]{1,0:T(8,128)(2,1)S(1)}, u32[]{:S(2)}, u32[]{:S(2)}) %collective-permute-start.9) | collective-permute-done | bytes 65568 | tf_op jit(solution)/shard_map/ppermute | solution.py:32
  21.1 2.9 %collective-permute-start.10 = (bf16[128,256]{1,0:T(8,128)(2,1)S(1)}, bf16[128,256]{1,0:T(8,128)(2,1)S(1)}, u32[]{:S(2)}, u32[]{:S(2)}) collective-permute-start(bf16[128,256]{1,0:T(8,128)(2,1)S(1)} %add_convert_fusion.1), channel_id=1, source_target_pairs={{0,18},{1,11},{2,8},{3,17},{4,14},{5,23},{6,20},{7,13},{8,2},{9,27... | collective-permute-start | bytes 196616 | tf_op jit(solution)/shard_map/ppermute | solution.py:32
  24.0 0.0 collective-permute-done.11
  24.0 0.3 %fusion.8 = f32[512,512]{1,0:T(8,128)S(1)} fusion(bf16[128,512]{1,0:T(8,128)(2,1)S(1)} %bitcast.66, bf16[128,512]{1,0:T(8,128)(2,1)S(1)} %collective-permute-done.11), kind=kOutput, calls=%fused_computation.36 | convolution fusion | flops 67108864 | bytes 1310720 | tf_op jit(solution)/shard_map/dot_general | solution.py:67
  24.3 0.0 copy-done
  24.3 1.4 %convolution_convert_fusion = bf16[512,512]{1,0:T(8,128)(2,1)} fusion(bf16[512,512]{1,0:T(8,128)(2,1)S(1)} %copy-done, f32[512,512]{1,0:T(8,128)S(1)} %fusion.8, bf16[128,512]{1,0:T(8,128)(2,1)S(1)} %bitcast.65, bf16[128,512]{1,0:T(8,128)(2,1)S(1)} %bitcast.59), kind=kOutput, calls=%fused_computation.2 | convolution fusion | flops 336330752 | bytes 2359296 | tf_op jit(solution)/shard_map/dot_general | solution.py:67
  25.7 0.3 collective-permute-done.10
  26.0 0.6 %collective-permute-start.12 = (bf16[128,256]{1,0:T(8,128)(2,1)S(1)}, bf16[128,256]{1,0:T(8,128)(2,1)S(1)}, u32[]{:S(2)}, u32[]{:S(2)}) collective-permute-start(bf16[128,256]{1,0:T(8,128)(2,1)S(1)} %add_convert_fusion), channel_id=1, source_target_pairs={{0,2},{2,0},{4,6},{6,4},{8,10},{10,8},{12,14},{14,12},{16,18},{18,... | collective-permute-start | bytes 196616 | tf_op jit(solution)/shard_map/ppermute | solution.py:13
  26.6 0.2 fusion.2.mine
  26.8 0.6 %collective-permute-done.12.other = bf16[128,256]{1,0:T(8,128)(2,1)S(1)} collective-permute-done((bf16[128,256]{1,0:T(8,128)(2,1)S(1)}, bf16[128,256]{1,0:T(8,128)(2,1)S(1)}, u32[]{:S(2)}, u32[]{:S(2)}) %collective-permute-start.12) | collective-permute-done | bytes 65568 | tf_op jit(solution)/shard_map/ppermute | solution.py:13
  27.5 1.0 %shard_map.88 = f32[256,512]{1,0:T(8,128)} custom-call(f32[256,512]{1,0:T(8,128)S(1)} %fusion.2.mine, bf16[128,256]{1,0:T(8,128)(2,1)S(1)} %collective-permute-done.12.other, bf16[128,512]{1,0:T(8,128)(2,1)S(1)} %broadcast_select_fusion.rows), custom_call_target="tpu_custom_call" | custom-call | tf_op jit(solution)/shard_map/pallas_call | solution.py:194
  (23 shorter events, 0.3 us)
Async XLA Ops:
  0.6 23.7 %copy-start = (bf16[512,512]{1,0:T(8,128)(2,1)S(1)}, bf16[512,512]{1,0:T(8,128)(2,1)}, u32[]{:S(2)}) copy-start(bf16[512,512]{1,0:T(8,128)(2,1)} %param.13) | copy-start | bytes 1572868
  0.6 4.2 %copy-start.2 = (s32[128,1024]{1,0:T(8,128)S(1)}, s32[128,1024]{1,0:T(8,128)}, u32[]{:S(2)}) copy-start(s32[128,1024]{1,0:T(8,128)} %counts.1) | copy-start | bytes 1572868
  0.7 4.3 %copy-start.1 = (bf16[512,512]{1,0:T(8,128)(2,1)S(1)}, bf16[512,512]{1,0:T(8,128)(2,1)}, u32[]{:S(2)}) copy-start(bf16[512,512]{1,0:T(8,128)(2,1)} %inputs.1) | copy-start | bytes 1572868
  1.8 6.6 %collective-permute-start = (bf16[128,512]{1,0:T(8,128)(2,1)S(1)}, bf16[128,512]{1,0:T(8,128)(2,1)S(1)}, u32[]{:S(2)}, u32[]{:S(2)}) collective-permute-start(bf16[128,512]{1,0:T(8,128)(2,1)S(1)} %get-tuple-element.25), channel_id=1, source_target_pairs={{0,1},{1,0},{2,3},{3,2},{4,5},{5,4},{6,7},{7,6},{8,9},{9,8},{10,11... | collective-permute-start | bytes 393224 | tf_op jit(solution)/shard_map/ppermute | solution.py:13
  5.2 2.8 %collective-permute-start.1 = (bf16[64,512]{1,0:T(8,128)(2,1)S(1)}, bf16[64,512]{1,0:T(8,128)(2,1)S(1)}, u32[]{:S(2)}, u32[]{:S(2)}) collective-permute-start(bf16[64,512]{1,0:T(8,128)(2,1)S(1)} %bitcast.70), channel_id=1, source_target_pairs={{0,2},{2,0},{4,6},{6,4},{8,10},{10,8},{12,14},{14,12},{16,18},{18,... | collective-permute-start | bytes 196616 | tf_op jit(solution)/shard_map/ppermute | solution.py:13
  5.3 4.7 %collective-permute-start.3 = (bf16[1,16,512]{2,1,0:T(8,128)(2,1)S(1)}, bf16[1,16,512]{2,1,0:T(8,128)(2,1)S(1)}, u32[]{:S(2)}, u32[]{:S(2)}) collective-permute-start(bf16[1,16,512]{2,1,0:T(8,128)(2,1)S(1)} %bitcast.54), channel_id=1, source_target_pairs={{0,16},{2,18},{4,20},{6,22},{8,24},{10,26},{12,28},{14,30},{16,0},... | collective-permute-start | bytes 49160 | tf_op jit(solution)/shard_map/ppermute | solution.py:13
  8.1 3.6 %collective-permute-start.4 = (bf16[64,256]{1,0:T(8,128)(2,1)S(1)}, bf16[64,256]{1,0:T(8,128)(2,1)S(1)}, u32[]{:S(2)}, u32[]{:S(2)}) collective-permute-start(bf16[64,256]{1,0:T(8,128)(2,1)S(1)} %select_convert_fusion.3), channel_id=1, source_target_pairs={{0,3},{1,2},{2,1},{3,0},{4,7},{5,6},{6,5},{7,4},{8,11},{9,10},{10,... | collective-permute-start | bytes 98312 | tf_op jit(solution)/shard_map/ppermute | solution.py:32
  8.7 1.3 %collective-permute-start.2 = (bf16[64,512]{1,0:T(8,128)(2,1)S(1)}, bf16[64,512]{1,0:T(8,128)(2,1)S(1)}, u32[]{:S(2)}, u32[]{:S(2)}) collective-permute-start(bf16[64,512]{1,0:T(8,128)(2,1)S(1)} %bitcast.71), channel_id=1, source_target_pairs={{0,2},{2,0},{4,6},{6,4},{8,10},{10,8},{12,14},{14,12},{16,18},{18,... | collective-permute-start | bytes 196616 | tf_op jit(solution)/shard_map/ppermute | solution.py:13
  10.1 3.4 %collective-permute-start.5 = (bf16[64,256]{1,0:T(8,128)(2,1)S(1)}, bf16[64,256]{1,0:T(8,128)(2,1)S(1)}, u32[]{:S(2)}, u32[]{:S(2)}) collective-permute-start(bf16[64,256]{1,0:T(8,128)(2,1)S(1)} %select_convert_fusion.2), channel_id=1, source_target_pairs={{0,3},{1,2},{2,1},{3,0},{4,7},{5,6},{6,5},{7,4},{8,11},{9,10},{10,... | collective-permute-start | bytes 98312 | tf_op jit(solution)/shard_map/ppermute | solution.py:32
  11.7 3.9 %collective-permute-start.6 = (bf16[2,16,512]{2,1,0:T(8,128)(2,1)S(1)}, bf16[2,16,512]{2,1,0:T(8,128)(2,1)S(1)}, u32[]{:S(2)}, u32[]{:S(2)}) collective-permute-start(bf16[2,16,512]{2,1,0:T(8,128)(2,1)S(1)} %maximum_select_fusion.4), channel_id=1, source_target_pairs={{0,8},{2,10},{4,12},{6,14},{8,0},{10,2},{12,4},{14,6},{16,24},{18,... | collective-permute-start | bytes 98312 | tf_op jit(solution)/shard_map/ppermute | solution.py:13
  13.6 3.8 %collective-permute-start.7 = (bf16[128,256]{1,0:T(8,128)(2,1)S(1)}, bf16[128,256]{1,0:T(8,128)(2,1)S(1)}, u32[]{:S(2)}, u32[]{:S(2)}) collective-permute-start(bf16[128,256]{1,0:T(8,128)(2,1)S(1)} %fusion.1), channel_id=1, source_target_pairs={{0,10},{1,7},{2,4},{3,9},{4,2},{5,15},{6,12},{7,1},{8,14},{9,3},{1... | collective-permute-start | bytes 196616 | tf_op jit(solution)/shard_map/ppermute | solution.py:32
  15.6 4.3 %collective-permute-start.8 = (bf16[4,16,512]{2,1,0:T(8,128)(2,1)S(1)}, bf16[4,16,512]{2,1,0:T(8,128)(2,1)S(1)}, u32[]{:S(2)}, u32[]{:S(2)}) collective-permute-start(bf16[4,16,512]{2,1,0:T(8,128)(2,1)S(1)} %bitcast.67), channel_id=1, source_target_pairs={{0,4},{2,6},{4,0},{6,2},{8,12},{10,14},{12,8},{14,10},{16,20},{18,... | collective-permute-start | bytes 196616 | tf_op jit(solution)/shard_map/ppermute | solution.py:13
  17.3 3.8 %collective-permute-start.9 = (bf16[128,256]{1,0:T(8,128)(2,1)S(1)}, bf16[128,256]{1,0:T(8,128)(2,1)S(1)}, u32[]{:S(2)}, u32[]{:S(2)}) collective-permute-start(bf16[128,256]{1,0:T(8,128)(2,1)S(1)} %add_convert_fusion.2), channel_id=1, source_target_pairs={{0,6},{1,19},{2,16},{3,5},{4,22},{5,3},{6,0},{7,21},{8,26},{9,15},... | collective-permute-start | bytes 196616 | tf_op jit(solution)/shard_map/ppermute | solution.py:32
  20.0 4.0 %collective-permute-start.11 = (bf16[128,512]{1,0:T(8,128)(2,1)S(1)}, bf16[128,512]{1,0:T(8,128)(2,1)S(1)}, u32[]{:S(2)}, u32[]{:S(2)}) collective-permute-start(bf16[128,512]{1,0:T(8,128)(2,1)S(1)} %bitcast.58), channel_id=1, source_target_pairs={{0,2},{2,0},{4,6},{6,4},{8,10},{10,8},{12,14},{14,12},{16,18},{18,... | collective-permute-start | bytes 393224 | tf_op jit(solution)/shard_map/ppermute | solution.py:13
  21.1 4.9 %collective-permute-start.10 = (bf16[128,256]{1,0:T(8,128)(2,1)S(1)}, bf16[128,256]{1,0:T(8,128)(2,1)S(1)}, u32[]{:S(2)}, u32[]{:S(2)}) collective-permute-start(bf16[128,256]{1,0:T(8,128)(2,1)S(1)} %add_convert_fusion.1), channel_id=1, source_target_pairs={{0,18},{1,11},{2,8},{3,17},{4,14},{5,23},{6,20},{7,13},{8,2},{9,27... | collective-permute-start | bytes 196616 | tf_op jit(solution)/shard_map/ppermute | solution.py:32
  26.0 1.5 %collective-permute-start.12 = (bf16[128,256]{1,0:T(8,128)(2,1)S(1)}, bf16[128,256]{1,0:T(8,128)(2,1)S(1)}, u32[]{:S(2)}, u32[]{:S(2)}) collective-permute-start(bf16[128,256]{1,0:T(8,128)(2,1)S(1)} %add_convert_fusion), channel_id=1, source_target_pairs={{0,2},{2,0},{4,6},{6,4},{8,10},{10,8},{12,14},{14,12},{16,18},{18,... | collective-permute-start | bytes 196616 | tf_op jit(solution)/shard_map/ppermute | solution.py:13
